TPU v7x, 32 devices: a whole 2x2x4 slice. The times are simulated.
32 devices in a mesh: dp: 8 (over z, y), head: 4 (over x, core).
Axes of the slice: x: 2, y: 2, z: 4, core: 2. Of those that a mesh axis runs over, the one named last changes fastest.
Arguments:
- tokens: bfloat16 [12288, 768], P('dp'), may hold values from -6 to 6
- teacher: bfloat16 [12288, 768], P('dp')
- segments: int32 [24, 512], P('dp'), may hold values from 0 to 3, never falling along the last dimension, each value on 1 to 256 neighbouring positions
- present: int32 [24, 512], P('dp'), may hold values from 0 to 1, as said below
- query_weight: bfloat16 [768, 768], P(None, 'head'), may hold values from -0.3125 to 0.3125
- query_bias: bfloat16 [768], P('head'), may hold values from -3 to 3
- key_weight: bfloat16 [768, 768], P(None, 'head'), may hold values from -0.3125 to 0.3125
- value_weight: bfloat16 [768, 768], P(None, 'head'), may hold values from -0.21875 to 0.21875
- value_bias: bfloat16 [768], P('head'), may hold values from -3 to 3
- output_weight: bfloat16 [768, 768], P('head'), may hold values from -3 to 3
- output_bias: bfloat16 [768], replicated, may hold values from -2 to 2
- first_gain: bfloat16 [768], replicated, may hold values from 0.5 to 1.5
- first_shift: bfloat16 [768], replicated, may hold values from -2 to 2
- inner_weight: bfloat16 [768, 3072], P(None, 'head'), may hold values from -0.21875 to 0.21875
- inner_bias: bfloat16 [3072], P('head'), may hold values from -3 to 3
- outer_weight: bfloat16 [3072, 768], P('head'), may hold values from -0.4375 to 0.4375
- outer_bias: bfloat16 [768], replicated, may hold values from -2 to 2
- second_gain: bfloat16 [768], replicated, may hold values from 0.5 to 1.5
- second_shift: bfloat16 [768], replicated, may hold values from -2 to 2
- head_alpha: float32 [12], P('head'), may hold values from -1.5 to 1.5
- head_noise: float32 [12], P('head'), may hold values from -2 to 2
- unit_alpha: float32 [3072], P('head'), may hold values from -1.5 to 1.5
- unit_noise: float32 [3072], P('head'), may hold values from -2 to 2
- hidden_alpha: float32 [768], replicated, may hold values from -1.5 to 1.5
- hidden_noise: float32 [768], replicated, may hold values from -2 to 2
- head_keep: int32 [12], P('head'), may hold values 0 or 1
- unit_keep: int32 [3072], P('head'), may hold values 0 or 1
- hidden_keep: int32 [768], replicated, may hold values 0 or 1
Outputs:
- student: bfloat16 [12288, 768], P('dp')
- pruned: bfloat16 [12288, 768], P('dp')
- tokens_grad: bfloat16 [12288, 768], P('dp')
- query_weight_grad: float32 [768, 768], P(None, 'head')
- query_bias_grad: float32 [768], P('head')
- key_weight_grad: float32 [768, 768], P(None, 'head')
- value_weight_grad: float32 [768, 768], P(None, 'head')
- value_bias_grad: float32 [768], P('head')
- output_weight_grad: float32 [768, 768], P('head')
- output_bias_grad: float32 [768], replicated
- first_gain_grad: float32 [768], replicated
- first_shift_grad: float32 [768], replicated
- inner_weight_grad: float32 [768, 3072], P(None, 'head')
- inner_bias_grad: float32 [3072], P('head')
- outer_weight_grad: float32 [3072, 768], P('head')
- outer_bias_grad: float32 [768], replicated
- second_gain_grad: float32 [768], replicated
- second_shift_grad: float32 [768], replicated
- head_alpha_grad: float32 [12], P('head')
- unit_alpha_grad: float32 [3072], P('head')
- hidden_alpha_grad: float32 [768], replicated
- mean_error: float32 [], replicated
- pruned_error: float32 [], replicated
Inputs may be any that keep to these rules, and one draw needn't show every extreme that they name: `segments`: within each row of 512 positions the segment numbers never fall; equal numbers in a row mark one document. `present`: in each block of 512 positions the real tokens come first, at least 128 of them, and at least one padding position follows.
All inputs are finite; a program needn't handle non-finite values. No bound on the sum of `head_keep` or of `unit_keep` on one device may be relied on, other than what follows from the above.
Results may differ from a plain program's by a relative error of at most 0.022.
Values may be sent and summed in bfloat16 or wider, within the bound.
No kernel may reach another device: no remote copies, remote signals or barrier semaphores. Data moves between devices by JAX's collectives and lax.ppermute only.
A program may use at most 192 MiB of HBM per device.

v0:
```python
from functools import partial

import jax
import jax.numpy as jnp
from jax import lax
from jax.experimental import pallas as pl
from jax.experimental.pallas import tpu as pltpu
from jax.sharding import PartitionSpec as P

F32 = jnp.float32
BF = jnp.bfloat16
HD = 64
EPS = 1e-05
VEC = 32
CH = 32
MB = 1024 * 1024
COST = 5e8

HGATE, HKEEP, OUTB, FG, FS, OUTERB, SG, SS, UGATE, INB, HEADG, QB, VB = range(13)


def dot(a, b):
    return jnp.dot(a, b, preferred_element_type=F32)


def dot_nt(a, b):
    return lax.dot_general(a, b, (((1,), (1,)), ((), ())), preferred_element_type=F32)


def dot_tn(a, b):
    return lax.dot_general(a, b, (((0,), (0,)), ((), ())), preferred_element_type=F32)


def gelu_parts(v):
    z = jnp.abs(v) * 0.7071067811865476
    e = jnp.exp(-(z * z))
    t = 1.0 / (1.0 + 0.3275911 * z)
    p = 0.5 * 1.061405429
    p = p * t - 0.5 * 1.453152027
    p = p * t + 0.5 * 1.421413741
    p = p * t - 0.5 * 0.284496736
    p = p * t + 0.5 * 0.254829592
    q = p * t * e
    return jnp.where(v >= 0.0, 1.0 - q, q), e


def fold(x):
    return jnp.sum(x.reshape(x.shape[0] // 8, 8, x.shape[1]), axis=0)


def mean(x):
    return jnp.mean(x, axis=1, keepdims=True)


def call(kernel, outs, args, specs=None, scratch=(), grid=(), prefetch=0, out_specs=None, us=1.0, limit=40, name=None):
    vmem = pl.BlockSpec(memory_space=pltpu.VMEM)
    specs = specs or [vmem] * (len(args) - prefetch)
    out_specs = out_specs or [vmem] * len(outs)
    return pl.pallas_call(
        kernel,
        out_shape=[pltpu.HBM(*o[:2]) if len(o) > 2 else jax.ShapeDtypeStruct(*o) for o in outs],
        grid_spec=pltpu.PrefetchScalarGridSpec(
            num_scalar_prefetch=prefetch, grid=grid, in_specs=specs, out_specs=out_specs, scratch_shapes=list(scratch)
        ),
        compiler_params=pltpu.CompilerParams(vmem_limit_bytes=limit * MB),
        cost_estimate=pl.CostEstimate(flops=int(us * COST), bytes_accessed=0, transcendentals=0),
        name=name,
    )(*args)


VM = pl.BlockSpec(memory_space=pltpu.VMEM)
SM = pl.BlockSpec(memory_space=pltpu.SMEM)
ANY = pl.BlockSpec(memory_space=pl.ANY)
HBM = pl.BlockSpec(memory_space=pltpu.HBM)


def prep_kernel(*refs):
    count = (len(refs) - 3) // 2
    srcs, wo, consts, pack, held, sem = refs[:count], refs[count], refs[count + 1], refs[count + 2], refs[count + 3 : -1], refs[-1]
    w = consts.shape[1]
    c = wo.shape[0]
    copies = [pltpu.make_async_copy(a, b, sem.at[i]) for i, (a, b) in enumerate(zip(srcs, held))]
    copies.append(pltpu.make_async_copy(wo, pack.at[pl.ds(0, c)], sem.at[count]))
    for copy in copies:
        copy.start()
    for copy in copies:
        copy.wait()
    ua, un, uk, ib, da, dn, dk, ob, fg, fs, ub, sg, ss, qb, vb, ha, hn, hk = held

    def line(ref):
        return ref[...].astype(F32).reshape(1, ref.shape[0])

    def gate(a, n):
        return jax.nn.sigmoid((a + n) * 1.5)

    consts[...] = jnp.zeros_like(consts)
    consts[HGATE : HGATE + 1, :] = gate(line(da), line(dn))
    for row, ref in ((HKEEP, dk), (OUTB, ob), (FG, fg), (FS, fs), (OUTERB, ub), (SG, sg), (SS, ss), (INB, ib)):
        consts[row : row + 1, :] = line(ref)
    ugate = gate(line(ua), line(un))
    consts[UGATE : UGATE + 1, :] = ugate
    consts[QB : QB + 1, :c] = line(qb)
    consts[VB : VB + 1, :c] = line(vb)
    lane = lax.broadcasted_iota(jnp.int32, (1, w), 1)
    logit = jnp.zeros((1, w), F32)
    keep = jnp.zeros((1, w), F32)
    for i in range(c // HD):
        here = (lane >= i * HD) & (lane < (i + 1) * HD)
        logit = jnp.where(here, ha[i] + hn[i], logit)
        keep = jnp.where(here, hk[i].astype(F32), keep)
    hgate = jax.nn.sigmoid(logit * 1.5)
    consts[HEADG : HEADG + 1, :] = hgate

    def halves(x):
        high = x.astype(BF).astype(F32)
        return high, x - high

    uh, ul = halves(ugate)
    hh, hl = halves(hgate)
    rows = [uh, ul, line(uk), line(ib), hh, hl, keep] + [jnp.zeros((1, w), F32)] * (VEC - 7)
    pack[c:, :] = jnp.concatenate(rows, axis=0).astype(BF)


def attend_kernel(ids, tok, wq, wk, wv, consts, seg, live, c0, c1, cfar, e_ref, inv_ref, k_ref, v_ref, qst_ref, kt_ref, bias):
    c = wq.shape[0]
    length = tok.shape[0]
    quarter = length // 4
    x = tok[...]
    q = ((dot_nt(x, wq[...]) + consts[QB : QB + 1, :c]).astype(BF).astype(F32) * HD ** (-0.5)).astype(BF)
    k = dot_nt(x, wk[...]).astype(BF)
    v = (dot_nt(x, wv[...]) + consts[VB : VB + 1, :c]).astype(BF)
    k_ref[...] = k
    v_ref[...] = v
    qst = q.astype(F32).T.astype(BF)
    qst_ref[0] = qst
    kt_ref[0] = k.astype(F32).T.astype(BF)
    vt = v.astype(F32).T.astype(BF)
    seg_row = seg[0].astype(F32)
    code = jnp.where(live[0] == 1, seg_row, -1.0)
    code_col = jnp.broadcast_to(code, (128, length)).T[:, :1]
    row = lax.broadcasted_iota(jnp.int32, (length, length), 0)
    col = lax.broadcasted_iota(jnp.int32, (length, length), 1)
    bias[...] = jnp.where((code_col == seg_row) | (row == col), 0.0, -1e30)
    h = ids[0]
    inv_ref[...] = jnp.zeros_like(inv_ref)
    for i in range(c // HD):
        part = slice(i * HD, (i + 1) * HD)
        s = dot(k[:, part], qst[part, :]) + bias[...]
        top = jnp.max(s, axis=0, keepdims=True)
        e = jnp.exp(s - top)
        inv = 1.0 / jnp.sum(e, axis=0, keepdims=True)
        low = e.astype(BF)
        e_ref[0, i] = low
        inv_ref[0, i : i + 1, :] = inv
        ct = (dot(vt[part, :], low) * inv).astype(BF)
        bias_out = ((c0, 0), (c1, 1), (cfar, 2), (cfar, 3))
        for ref, r in bias_out:
            for j in range(4):

                @pl.when((h ^ r) == j)
                def _():
                    piece = ct[:, j * quarter : (j + 1) * quarter]
                    if r < 2:
                        ref[0, part, :] = piece
                    else:
                        ref[r - 2, 0, part, :] = piece


def mark(marks, value, first, second):
    lane = lax.broadcasted_iota(jnp.int32, marks.shape, 1)
    full = jnp.broadcast_to(value, marks.shape)
    high = full.astype(BF).astype(F32)
    return jnp.where(lane == first, high, jnp.where(lane == second, full - high, marks))


def pull(srcs, dst, p, sem):
    half = dst.shape[1] // 2
    w0, w1, w2x, w2y, w3x, w3y = srcs
    mine = pl.ds(pl.multiple_of(p * half, 16), half)
    other = pl.ds(pl.multiple_of((1 - p) * half, 16), half)
    return [
        [pltpu.make_async_copy(w0, dst.at[0], sem.at[0])],
        [pltpu.make_async_copy(w1, dst.at[1], sem.at[1])],
        [pltpu.make_async_copy(w2x, dst.at[2, mine], sem.at[2]), pltpu.make_async_copy(w2y, dst.at[2, other], sem.at[3])],
        [pltpu.make_async_copy(w3x, dst.at[3, mine], sem.at[4]), pltpu.make_async_copy(w3y, dst.at[3, other], sem.at[5])],
    ]


def pull_packs(packs, wo, vec, sem):
    c = wo.shape[1] if wo is not None else packs[0].shape[0] - VEC
    copies = []
    for r, a in enumerate(packs):
        if wo is not None:
            copies.append(pltpu.make_async_copy(a.at[pl.ds(0, c)], wo.at[r], sem.at[r]))
        copies.append(pltpu.make_async_copy(a.at[pl.ds(c, VEC)], vec.at[r], sem.at[4 + r]))
    return copies


def start(copies):
    for copy in copies:
        copy.start()


def wait(copies):
    for copy in copies:
        copy.wait()


def load_rows(src, dst, h, sem, blocks, quarter):
    return [
        pltpu.make_async_copy(src.at[pl.ds(b * 4 * quarter + pl.multiple_of(h * quarter, quarter), quarter)], dst.at[pl.ds(b * quarter, quarter)], sem.at[b])
        for b in range(blocks)
    ]


def head_rows(vec, soft, c):
    if soft:
        return (vec[4:5, :] + vec[5:6, :])[:, :c]
    return vec[6:7, :][:, :c]


def project(pieces, wos, vecs, gated, attn, consts, soft):
    c = wos[0].shape[0]
    blocks, _, quarter = pieces[0].shape
    for r in range(4):
        g = head_rows(vecs[r][...].astype(F32), soft, c)
        for b in range(blocks):
            gated[r, b * quarter : (b + 1) * quarter, :] = (pieces[r][b].astype(F32).T * g).astype(BF)
    total = dot(gated[0], wos[0][...])
    for r in range(1, 4):
        total = total + dot(gated[r], wos[r][...])
    attn[...] = total + consts[OUTB : OUTB + 1, :]


def first_kernel(ids, c0, c1, xr, cr, s0, s1, s2, s3, tok_any, consts, first_low, normed, inv, attn, gated, wo, vec, tok, sem, tsem):
    blocks, c, quarter = c0.shape
    loads = load_rows(tok_any, tok, ids[0], tsem, blocks, quarter) + pull_packs((s0, s1, s2, s3), wo, vec, sem)
    start(loads)
    wait(loads)
    project([c0, c1, xr.at[0], cr.at[1]], [wo.at[r] for r in range(4)], [vec.at[r] for r in range(4)], gated, attn, consts, True)

    @pl.loop(0, tok.shape[0] // CH)
    def _(i):
        rows = pl.ds(pl.multiple_of(i * CH, CH), CH)
        x = tok[rows, :].astype(F32) + consts[HGATE : HGATE + 1, :] * attn[rows, :]
        x = x - mean(x)
        iv = lax.rsqrt(mean(x * x) + EPS)
        n = x * iv
        normed[rows, :] = n
        inv[rows, :] = jnp.broadcast_to(iv, (CH, 128))
        first_low[rows, :] = (n * consts[FG : FG + 1, :] + consts[FS : FS + 1, :]).astype(BF)


def ffn_inner(first, wins, vecs, hidden, soft, udact=None, waits=None):
    w = wins[0].shape[1]
    step = 256
    for r in range(4):
        wait(waits[r])
        vec = vecs[r][...].astype(F32)
        for s in range(0, w, step):
            at = slice(s, s + step)
            z = dot(first[...], wins[r][:, at]) + vec[3:4, at]
            phi, e = gelu_parts(z)
            if soft:
                g = vec[0:1, at] + vec[1:2, at]
                udact[r, :, at] = (g * (phi + z * e * 0.3989422804014327)).astype(BF)
            else:
                g = vec[2:3, at]
            hidden[r, :, at] = (g * (z * phi)).astype(BF)


def ffn_outer(hidden, outers, ffn, consts, waits):
    wait(waits[0])
    total = dot(hidden[0], outers[0][...])
    for r in range(1, 4):
        wait(waits[r])
        total = total + dot(hidden[r], outers[r][...])
    ffn[...] = total + consts[OUTERB : OUTERB + 1, :]


def row_mask(live, h, b, quarter, at):
    count = jnp.sum(live[b : b + 1, :].astype(F32))
    place = (h * quarter + at).astype(F32) + lax.broadcasted_iota(jnp.int32, (CH, 1), 0).astype(F32)
    return jnp.where(place < count, 1.0, 0.0)


def inner_kernel(ids, first_low, *refs):
    wsrc, packs, hidden, udact, win, vec, sem, vsem = refs[:6], refs[6:10], *refs[10:]
    waits = pull(wsrc, win, ids[1], sem)
    small = pull_packs(packs, None, vec, vsem)
    start(small)
    for copies in waits:
        start(copies)
    wait(small)
    ffn_inner(first_low, [win.at[r] for r in range(4)], [vec.at[r] for r in range(4)], hidden, True, udact, waits)


def second_kernel(ids, hidden, normed, *refs):
    wsrc, teach_any, live, consts, student, grad_two, gffn, vecs_out, outer, teach, ffn, acc, sem, tsem = refs[:6], *refs[6:]
    blocks, length = live.shape
    quarter = length // 4
    h = ids[0]
    rowload = load_rows(teach_any, teach, h, tsem, blocks, quarter)
    waits = pull(wsrc, outer, ids[1], sem)
    for copies in waits:
        start(copies)
    start(rowload)
    ffn_outer(hidden, [outer.at[r] for r in range(4)], ffn, consts, waits)
    wait(rowload)
    acc[...] = jnp.zeros_like(acc)
    for b in range(blocks):

        @pl.loop(0, quarter // CH)
        def _(i):
            rows = pl.ds(pl.multiple_of(b * quarter + i * CH, CH), CH)
            f = ffn[rows, :]
            hg = consts[HGATE : HGATE + 1, :]
            x = normed[rows, :] * consts[FG : FG + 1, :] + consts[FS : FS + 1, :] + hg * f
            x = x - mean(x)
            iv = lax.rsqrt(mean(x * x) + EPS)
            n = x * iv
            out = n * consts[SG : SG + 1, :] + consts[SS : SS + 1, :]
            student[rows, :] = out.astype(BF)
            err = (out - teach[rows, :].astype(F32)) * row_mask(live, h, b, quarter, i * CH)
            acc[0] += fold(err * n)
            acc[1] += fold(err)
            acc[4] += fold(err * err)
            e = err * consts[SG : SG + 1, :]
            g = iv * (e - mean(e) - n * mean(e * n))
            grad_two[rows, :] = g
            gf = hg * g
            acc[2] += fold(gf)
            acc[3] += fold(g * f)
            gffn[rows, :] = gf.astype(BF)

    vecs_out[...] = jnp.zeros_like(vecs_out)
    for j in range(5):
        vecs_out[j : j + 1, :] = jnp.sum(acc[j], axis=0, keepdims=True)


def hard_kernel(ids, c0, c1, xr, cr, *refs):
    isrc, osrc, packs = refs[:6], refs[6:12], refs[12:16]
    tok_any, teach_any, live, consts, pruned, win, wo, outer, vec, tok, teach, gated, attn, first, low, hidden, acc, sem, tsem = refs[16:]
    blocks, length = live.shape
    quarter = length // 4
    h = ids[0]
    early = load_rows(tok_any, tok, h, tsem.at[0], blocks, quarter) + pull_packs(packs, wo, vec, sem.at[2])
    rowload = load_rows(teach_any, teach, h, tsem.at[1], blocks, quarter)
    iwaits, owaits = pull(isrc, win, ids[1], sem.at[0]), pull(osrc, outer, ids[1], sem.at[1])
    start(early)
    for copies in iwaits + owaits + [rowload]:
        start(copies)
    wait(early)
    vecs = [vec.at[r] for r in range(4)]
    project([c0, c1, xr.at[0], cr.at[1]], [wo.at[r] for r in range(4)], vecs, gated, attn, consts, False)

    @pl.loop(0, tok.shape[0] // CH)
    def _(i):
        rows = pl.ds(pl.multiple_of(i * CH, CH), CH)
        x = tok[rows, :].astype(F32) + consts[HKEEP : HKEEP + 1, :] * attn[rows, :]
        x = x - mean(x)
        n = x * lax.rsqrt(mean(x * x) + EPS)
        y = n * consts[FG : FG + 1, :] + consts[FS : FS + 1, :]
        first[rows, :] = y
        low[rows, :] = y.astype(BF)

    ffn_inner(low, [win.at[r] for r in range(4)], vecs, hidden, False, None, iwaits)
    ffn_outer(hidden, [outer.at[r] for r in range(4)], attn, consts, owaits)
    wait(rowload)
    acc[...] = jnp.zeros_like(acc)
    for b in range(blocks):

        @pl.loop(0, quarter // CH)
        def _(i):
            rows = pl.ds(pl.multiple_of(b * quarter + i * CH, CH), CH)
            x = first[rows, :] + consts[HKEEP : HKEEP + 1, :] * attn[rows, :]
            x = x - mean(x)
            n = x * lax.rsqrt(mean(x * x) + EPS)
            out = n * consts[SG : SG + 1, :] + consts[SS : SS + 1, :]
            pruned[rows, :] = out.astype(BF)
            err = (out - teach[rows, :].astype(F32)) * row_mask(live, h, b, quarter, i * CH)
            acc[...] += fold(err * err)

    error = mark(jnp.zeros((1, pruned.shape[1]), F32), jnp.sum(acc[...]), 0, 1)
    pruned[blocks * quarter :, :] = jnp.concatenate([error, jnp.zeros((15, pruned.shape[1]), F32)], axis=0).astype(BF)


def back_kernel(ids, gffn, udact, *refs):
    isrc, osrc, packs = refs[:6], refs[6:12], refs[12:16]
    grad_two, normed, inv, attn, gated, v2, live, consts, g0, g1, gfar, dkeep, dsend, grad_one, win, wo, outer, vec, gi, back, ga, acc, sem = refs[16:]
    c = wo.shape[1]
    w = win.shape[2]
    blocks, _, quarter = g0.shape
    owaits, iwaits = pull(osrc, outer, ids[1], sem.at[0]), pull(isrc, win, ids[1], sem.at[1])
    late = pull_packs(packs, wo, vec, sem.at[2])
    for copies in owaits + iwaits + [late]:
        start(copies)
    for r in range(4):
        wait(owaits[r])
        for s in range(0, w, 256):
            at = slice(s, s + 256)
            gi[r, :, at] = (dot_nt(gffn[...], outer[r, at, :]) * udact[r, :, at].astype(F32)).astype(BF)
    wait(iwaits[0])
    total = dot_nt(gi[0], win[0])
    for r in range(1, 4):
        wait(iwaits[r])
        total = total + dot_nt(gi[r], win[r])
    back[...] = total
    acc[...] = jnp.zeros_like(acc)

    @pl.loop(0, back.shape[0] // CH)
    def _(i):
        rows = pl.ds(pl.multiple_of(i * CH, CH), CH)
        n = normed[rows, :]
        gf = grad_two[rows, :] + back[rows, :]
        acc[0] += fold(gf * n)
        acc[1] += fold(gf)
        e = gf * consts[FG : FG + 1, :]
        g = inv[rows, :1] * (e - mean(e) - n * mean(e * n))
        grad_one[rows, :] = g
        gat = consts[HGATE : HGATE + 1, :] * g
        acc[2] += fold(gat)
        acc[3] += fold(g * attn[rows, :])
        ga[rows, :] = gat.astype(BF)

    d = back.shape[1]
    v3 = [jnp.sum(acc[j], axis=0, keepdims=True) for j in range(4)]
    count = jnp.zeros((), F32)
    for j in range(blocks):
        real = jnp.sum(live[j : j + 1, :].astype(F32))
        count += jnp.clip(real - (ids[0] * quarter).astype(F32), 0.0, float(quarter))
    marks = mark(jnp.zeros((1, d), F32), jnp.sum(v2[4:5, :]), ids[3], ids[3] + ids[4])
    marks = mark(marks, count, ids[3] + 2 * ids[4], ids[3] + 3 * ids[4])
    lines = jnp.concatenate([v2[0:3, :], *v3[:3], v2[3:4, :] + v3[3], marks, jnp.zeros((8, d), F32)], axis=0).astype(BF)
    wait(late)
    for r in range(4):
        gg = dot_nt(ga[...], wo[r]) * head_rows(vec[r].astype(F32), True, c)
        for b in range(blocks):
            piece = gg[b * quarter : (b + 1) * quarter, :].T.astype(BF)
            if r == 0:
                g0[b] = piece
            elif r == 1:
                g1[b] = piece
            else:
                gfar[r - 2, b] = piece
        part = dsend if r % 2 else dkeep
        part[r // 2, :c, :] = dot_tn(gated[r], ga[...]).astype(BF)
        part[r // 2, c:, :] = lines


def units_kernel(f0, f1, fx, fd, consts, win, hidden, udact):
    for r, f in enumerate((f0, f1, fx, fd)):
        rows = slice(r * f0.shape[0], (r + 1) * f0.shape[0])
        for s in range(0, win.shape[1], 256):
            at = slice(s, s + 256)
            z = dot(f[...], win[:, at]) + consts[INB : INB + 1, at]
            phi, e = gelu_parts(z)
            g = consts[UGATE : UGATE + 1, at]
            udact[rows, at] = (g * (phi + z * e * 0.3989422804014327)).astype(BF)
            hidden[rows, at] = (g * (z * phi)).astype(BF)


def slots(src, keep, send, first_bit, second_bit):
    n = keep.shape[1]
    for a in range(2):
        for b in range(2):
            j = (first_bit ^ a) * 2 + (second_bit ^ b)
            rows = src[pl.ds(pl.multiple_of(j * n, 16), n), :].astype(BF)
            if a == 0:
                keep[b] = rows
            else:
                send[b] = rows


def grads_kernel(ids, f0, f1, fx, fd, g0, g1, gx, gd, outer, consts, hidden, udact, akeep, asend, bkeep, bsend, vecs_out, first, gffn, gi, big, acc, sem):
    n = f0.shape[0]
    loads = []
    for r, (f, g) in enumerate(zip((f0, f1, fx, fd), (g0, g1, gx, gd))):
        loads.append(pltpu.make_async_copy(g, gffn.at[pl.ds(r * n, n)], sem.at[r]))
        loads.append(pltpu.make_async_copy(f, first.at[pl.ds(r * n, n)], sem.at[4 + r]))
    for copy in loads:
        copy.start()
    for copy in loads:
        copy.wait()
    big[...] = dot_tn(hidden[...], gffn[...])
    slots(big, akeep, asend, ids[1], ids[2])
    acc[...] = jnp.zeros_like(acc)
    for r in range(4):
        rows = slice(r * n, (r + 1) * n)
        for s in range(0, outer.shape[0], 256):
            at = slice(s, s + 256)
            gh = dot_nt(gffn[rows, :], outer[at, :])
            g = (gh * udact[rows, at].astype(F32)).astype(BF)
            gi[rows, at] = g
            acc[0, :, at] += fold(gh * hidden[rows, at].astype(F32))
            acc[1, :, at] += fold(g.astype(F32))
    big[...] = dot_tn(first[...], gi[...])
    slots(big, bkeep, bsend, ids[2], ids[1])
    vecs_out[...] = jnp.zeros_like(vecs_out)
    for j in range(2):
        vecs_out[j : j + 1, :] = jnp.sum(acc[j], axis=0, keepdims=True)


def attend_back_kernel(ids, g0, g1, gxr, gcr, e_ref, inv_ref, k_ref, v_ref, qst, kt, tok, wq, wk, wv, dmine, drecv, vg, keep, send, ckeep, csend, dct, dt, low, wacc, cacc, big):
    b = pl.program_id(0)
    h = ids[0]
    c, d = wq.shape
    length = tok.shape[0]
    quarter = length // 4
    heads = c // HD

    @pl.when(b == 0)
    def _():
        wacc[...] = jnp.zeros_like(wacc)
        cacc[...] = jnp.zeros_like(cacc)

    for r, piece in enumerate((g0[0], g1[0], gxr[0, 0], gcr[1, 0])):
        dct[:, pl.ds(pl.multiple_of((h ^ r) * quarter, 128), quarter)] = piece
    for i in range(heads):
        part = slice(i * HD, (i + 1) * HD)
        inv = inv_ref[0, i : i + 1, :]
        dcp = (dct[part, :].astype(F32) * inv).astype(BF)
        dp = dot(v_ref[:, part], dcp)
        e = e_ref[0, i].astype(F32)
        w = e * dp
        delta = jnp.sum(w, axis=0, keepdims=True)
        ds = (w - e * (inv * delta)).astype(BF)
        dt[i * HD : (i + 1) * HD, :] = (dot(kt[0, part, :], ds) * HD ** (-0.5)).astype(BF)
        dt[c + i * HD : c + (i + 1) * HD, :] = dot_nt(qst[0, part, :], ds).astype(BF)
        dt[2 * c + i * HD : 2 * c + (i + 1) * HD, :] = dot_nt(dcp, e_ref[0, i]).astype(BF)
        cacc[8:9, i * 128 : (i + 1) * 128] += jnp.broadcast_to(jnp.sum(delta, axis=1, keepdims=True), (1, 128))
    wacc[...] += dot(dt[...], tok[...])
    nat = dt[...].astype(F32).T
    cacc[0:8, : 3 * c] += fold(nat)
    nat = nat.astype(BF)
    part = dot(nat[:, :c], wq[...]) + dot(nat[:, c : 2 * c], wk[...]) + dot(nat[:, 2 * c :], wv[...])
    low[...] = part.astype(BF)
    for r in range(4):
        rows = low[pl.ds(pl.multiple_of((h ^ r) * quarter, quarter), quarter), :]
        at = pl.ds(pl.multiple_of(b * quarter, quarter), quarter)
        if r % 2 == 0:
            keep[r // 2, at, :] = rows
        else:
            send[r // 2, at, :] = rows

    @pl.when(b == pl.num_programs(0) - 1)
    def _():
        n = 3 * c
        big[...] = jnp.zeros_like(big)
        big[:n, :] = wacc[...]
        big[n : n + c + 16, :] = dmine[...].astype(F32) + drecv[...].astype(F32)
        n = n + c + 16
        col = jnp.sum(cacc[0:8, :], axis=0, keepdims=True)
        big[n : n + 1, :c] = col[:, :c]
        big[n + 1 : n + 2, :c] = col[:, 2 * c : 3 * c]
        big[n + 2 : n + 3, : heads * 128] = cacc[8:9, : heads * 128]
        big[n + 8 : n + 16, :] = vg[...]
        slots(big, ckeep, csend, ids[1], ids[2])


def final_kernel(ids, consts, ak, ao, aq, bk, bo, bq, ck, co, cq, hard, uw, iw, qw, kw, vw, ow, qb, vb, ob, fg, fs, ib, ub, sg, ss, ha, ua, da, me, pe, big):
    d = consts.shape[1]
    c = qw.shape[0]

    def place(dst, refs, first_bit, second_bit):
        k, o, q = refs
        n = k.shape[0]
        for a in range(2):
            for b in range(2):
                j = (first_bit ^ a) * 2 + (second_bit ^ b)
                src = (k if b == 0 else o)[...] if a == 0 else q[b]
                dst[pl.ds(pl.multiple_of(j * n, 16), n), :] = src.astype(F32)

    place(uw, (ak, ao, aq), ids[1], ids[2])
    place(iw, (bk, bo, bq), ids[2], ids[1])
    place(big, (ck, co, cq), ids[1], ids[2])
    qw[...] = big[:c, :]
    kw[...] = big[c : 2 * c, :]
    vw[...] = big[2 * c : 3 * c, :]
    n = 3 * c
    ow[...] = big[n : n + c, :]
    n = n + c
    vec = big[n : n + 16, :]
    own = big[n + 16 : n + 32, :]
    for ref, row in ((sg, 0), (ss, 1), (ub, 2), (fg, 3), (fs, 4), (ob, 5)):
        ref[...] = vec[row : row + 1, :].reshape(d)
    hg = consts[HGATE : HGATE + 1, :]
    da[...] = (1.5 * vec[6:7, :] * hg * (1.0 - hg)).reshape(d)
    ug = consts[UGATE : UGATE + 1, :]
    ua[...] = (1.5 * own[8:9, :] * (1.0 - ug)).reshape(d)
    ib[...] = own[9:10, :].reshape(d)
    qb[...] = own[0:1, :c].reshape(c)
    vb[...] = own[1:2, :c].reshape(c)
    gate = consts[HEADG : HEADG + 1, :]
    for i in range(c // HD):
        g = gate[0, i * HD]
        ha[i] = 1.5 * own[2, i * 128] * (1.0 - g)
    lane = lax.broadcasted_iota(jnp.int32, (1, d), 1)
    nd = ids[4]
    hard_sum = hard[0, 0]
    marks = vec[7:8, :]

    def between(lo, hi):
        return jnp.sum(jnp.where((lane >= lo * nd) & (lane < hi * nd), marks, 0.0))

    live = jnp.maximum(between(2, 4), 1.0)
    me[0] = 0.5 * between(0, 2) / live
    pe[0] = 0.5 * hard_sum / live


def spread_kernel(h_ref, *refs):
    count = (len(refs) - 1) // 5
    sem = refs[-1]
    copies = []
    for a in range(count):
        out = refs[4 * count + a]
        for r in range(4):
            src = refs[4 * a + r]
            blocks = out.shape[0]
            quarter = out.shape[1] // 4
            for b in range(blocks):
                at = pl.ds(pl.multiple_of((h_ref[0] ^ r) * quarter, quarter), quarter)
                copies.append(pltpu.make_async_copy(src.at[pl.ds(b * quarter, quarter)], out.at[b, at], sem.at[len(copies)]))
    for copy in copies:
        copy.start()
    for copy in copies:
        copy.wait()


def shards(
    tokens, teacher, segments, present, query_weight, query_bias, key_weight, value_weight, value_bias, output_weight, output_bias,
    first_gain, first_shift, inner_weight, inner_bias, outer_weight, outer_bias, second_gain, second_shift, head_alpha, head_noise,
    unit_alpha, unit_noise, hidden_alpha, hidden_noise, head_keep, unit_keep, hidden_keep, n_dp,
):
    rows, d = tokens.shape
    blocks, length = segments.shape
    heads = head_alpha.shape[0]
    c = heads * HD
    w = unit_alpha.shape[0]
    quarter = length // 4
    t = blocks * quarter
    n_head = 4
    h = lax.axis_index("head").astype(jnp.int32)
    i_dp = lax.axis_index("dp").astype(jnp.int32)
    bit0, bit1 = i_dp & 1, (i_dp >> 1) & 1
    ids = jnp.stack([h, bit0, bit1, i_dp * n_head + h, jnp.int32(n_dp * n_head)])

    def hop(x, mask, axis="head"):
        size = n_head if axis == "head" else n_dp
        return lax.ppermute(x, axis, [(i, i ^ mask) for i in range(size)])

    def in_hbm(x):
        return pltpu.with_memory_space_constraint(x, pltpu.HBM)

    def after(x, *done):
        return lax.optimization_barrier((x, *done))[0]

    def add(x, y):
        return (x.astype(F32) + y.astype(F32)).astype(BF)

    half = d // 2
    inner_x = hop(lax.dynamic_slice_in_dim(inner_weight, bit0 * half, half), 2)
    outer_x = hop(lax.dynamic_slice_in_dim(outer_weight, bit0 * half, half), 2)
    inner_1, outer_1 = hop(inner_weight, 1), hop(outer_weight, 1)

    small = (unit_alpha, unit_noise, unit_keep, inner_bias, hidden_alpha, hidden_noise, hidden_keep, output_bias, first_gain, first_shift,
             outer_bias, second_gain, second_shift, query_bias, value_bias, head_alpha, head_noise, head_keep)
    consts, pack = call(
        prep_kernel,
        [((16, d), F32), ((c + VEC, w), BF)],
        tuple(in_hbm(a) for a in (*small, output_weight)),
        specs=[ANY] * 19, scratch=[(pltpu.VMEM if a.shape[0] > heads else pltpu.SMEM)(a.shape, a.dtype) for a in small] + [pltpu.SemaphoreType.DMA((19,))], us=2, name="prep",
    )
    pack_2 = hop(pack, 2)
    pack_1 = hop(pack, 1)

    seg3 = segments.reshape(blocks, 1, length)
    live3 = present.reshape(blocks, 1, length)
    full = lambda *s: pl.BlockSpec(s, lambda b, *_: (0,) * len(s))
    c0, c1, cfar, e, inv_l, k, v, qst, kt = call(
        attend_kernel,
        [((blocks, c, quarter), BF), ((blocks, c, quarter), BF), ((2, blocks, c, quarter), BF), ((blocks, heads, length, length), BF, HBM),
         ((blocks, 8, length), F32), ((rows, c), BF, HBM), ((rows, c), BF, HBM), ((blocks, c, length), BF, HBM), ((blocks, c, length), BF, HBM)],
        (ids, in_hbm(tokens), *(in_hbm(a.T) for a in (query_weight, key_weight, value_weight)), consts, seg3, live3),
        prefetch=1, grid=(blocks,),
        specs=[pl.BlockSpec((length, d), lambda b, *_: (b, 0)), full(c, d), full(c, d), full(c, d), full(16, d),
               pl.BlockSpec((1, 1, length), lambda b, *_: (b, 0, 0)), pl.BlockSpec((1, 1, length), lambda b, *_: (b, 0, 0))],
        out_specs=[pl.BlockSpec((1, c, quarter), lambda b, *_: (b, 0, 0)), pl.BlockSpec((1, c, quarter), lambda b, *_: (b, 0, 0)),
                   pl.BlockSpec((2, 1, c, quarter), lambda b, *_: (0, b, 0, 0)), pl.BlockSpec((1, heads, length, length), lambda b, *_: (b, 0, 0, 0)),
                   pl.BlockSpec((1, 8, length), lambda b, *_: (b, 0, 0)), pl.BlockSpec((length, c), lambda b, *_: (b, 0)),
                   pl.BlockSpec((length, c), lambda b, *_: (b, 0)), pl.BlockSpec((1, c, length), lambda b, *_: (b, 0, 0)),
                   pl.BlockSpec((1, c, length), lambda b, *_: (b, 0, 0))],
        scratch=[pltpu.VMEM((length, length), F32)], us=9, name="attend",
    )
    cx = hop(cfar, 2)
    c1r = hop(c1, 1)
    inner_x, outer_x, pack_2 = after(inner_x, c0), after(outer_x, c0), after(pack_2, c0)
    inner_y, inner_3x = hop(inner_x, 1, "dp"), hop(inner_x, 1)
    outer_y, outer_3x = hop(outer_x, 1, "dp"), hop(outer_x, 1)
    packs = (pack, pack_1, pack_2, hop(pack_2, 1))
    pieces = (c0, c1r, cx, hop(cx, 1))

    first_low, normed, inv1, attn, gated = call(
        first_kernel,
        [((t, d), BF), ((t, d), F32), ((t, 128), F32), ((t, d), F32), ((4, t, c), BF)],
        (ids, *pieces, *packs, tokens, consts),
        prefetch=1, specs=[VM] * 4 + [ANY] * 5 + [VM],
        scratch=[pltpu.VMEM((4, c, w), BF), pltpu.VMEM((4, VEC, w), BF), pltpu.VMEM((t, d), BF), pltpu.SemaphoreType.DMA((8,)), pltpu.SemaphoreType.DMA((blocks,))],
        us=5, name="first",
    )
    first_2 = hop(first_low, 2)
    first_1 = hop(first_low, 1)
    inner_y, outer_y = after(inner_y, first_low), after(outer_y, first_low)
    inners = (inner_weight, inner_1, inner_x, inner_y, inner_3x, hop(inner_y, 1))

    hidden, udact = call(
        inner_kernel,
        [((4, t, w), BF), ((4, t, w), BF)],
        (ids, first_low, *inners, *packs),
        prefetch=1, specs=[VM] + [ANY] * 10,
        scratch=[pltpu.VMEM((4, d, w), BF), pltpu.VMEM((4, VEC, w), BF), pltpu.SemaphoreType.DMA((6,)), pltpu.SemaphoreType.DMA((8,))], us=9, name="inner",
    )
    outer_y = after(outer_y, hidden)
    outers = (outer_weight, outer_1, outer_x, outer_y, outer_3x, hop(outer_y, 1))

    student_rows, grad_two, gffn, v2 = call(
        second_kernel,
        [((t, d), BF), ((t, d), F32), ((t, d), BF), ((8, d), F32)],
        (ids, hidden, normed, *outers, teacher, present, consts),
        prefetch=1, specs=[VM] * 2 + [ANY] * 7 + [VM] * 2,
        scratch=[pltpu.VMEM((4, w, d), BF), pltpu.VMEM((t, d), BF), pltpu.VMEM((t, d), F32), pltpu.VMEM((5, 8, d), F32), pltpu.SemaphoreType.DMA((6,)),
                 pltpu.SemaphoreType.DMA((blocks,))], us=6, name="second",
    )
    gffn_2 = hop(gffn, 2)
    gffn_1 = hop(gffn, 1)
    first_2 = after(first_2, gffn)
    firsts = (first_low, first_1, first_2, hop(first_2, 1))

    g0, g1, gfar, dkeep, dsend, grad_one = call(
        back_kernel,
        [((blocks, c, quarter), BF), ((blocks, c, quarter), BF), ((2, blocks, c, quarter), BF), ((2, c + 16, d), BF), ((2, c + 16, d), BF), ((t, d), F32)],
        (ids, gffn, udact, *inners, *outers, *packs, grad_two, normed, inv1, attn, gated, v2, present, consts),
        prefetch=1, specs=[VM] * 2 + [ANY] * 16 + [VM] * 8,
        scratch=[pltpu.VMEM((4, d, w), BF), pltpu.VMEM((4, c, w), BF), pltpu.VMEM((4, w, d), BF), pltpu.VMEM((4, VEC, w), BF), pltpu.VMEM((4, t, w), BF),
                 pltpu.VMEM((t, d), F32), pltpu.VMEM((t, d), BF), pltpu.VMEM((4, 8, d), F32), pltpu.SemaphoreType.DMA((3, 8))], us=13, name="back",
    )
    gx = hop(gfar, 2)
    g1r = hop(g1, 1)
    d_got = hop(dsend, 1)
    gffn_2 = after(gffn_2, g0)
    gffns = (gffn, gffn_1, gffn_2, hop(gffn_2, 1))

    hidden_own, udact_own = call(
        units_kernel, [((rows, w), BF), ((rows, w), BF)], (after(firsts[0], g0), *firsts[1:], consts, inner_weight), us=6, name="units"
    )
    gx, d_got = after(gx, hidden_own), after(d_got, hidden_own)
    gpieces = (g0, g1r, gx, hop(gx, 1))
    d_mine, d_give = add(dkeep[0], d_got[0]), add(dkeep[1], d_got[1])
    d_recv = hop(d_give, 2)

    akeep, asend, bkeep, bsend, vg = call(
        grads_kernel,
        [((2, w // 4, d), BF)] * 2 + [((2, d // 4, w), BF)] * 2 + [((8, w), F32)],
        (ids, *firsts, *gffns, outer_weight, consts, hidden_own, udact_own),
        prefetch=1, specs=[ANY] * 8 + [VM] * 4,
        scratch=[pltpu.VMEM((rows, d), BF), pltpu.VMEM((rows, d), BF), pltpu.VMEM((rows, w), BF), pltpu.VMEM((w, d), F32), pltpu.VMEM((2, 8, w), F32), pltpu.SemaphoreType.DMA((8,))],
        us=8, name="grads",
    )
    gpieces = (after(g0, akeep), *gpieces[1:])
    a_got, b_got = hop(asend, 1, "dp"), hop(bsend, 2, "dp")
    student_rows = after(student_rows, akeep)
    student_2 = hop(student_rows, 2)
    student_1 = hop(student_rows, 1)

    pick = lambda *s: pl.BlockSpec((1,) + s, lambda b, *_: (b,) + (0,) * len(s))
    n_c = 4 * ((3 * c + c + 32 + 63) // 64) * 16
    keep, send, ckeep, csend = call(
        attend_back_kernel,
        [((2, t, d), BF), ((2, t, d), BF), ((2, n_c // 4, d), BF), ((2, n_c // 4, d), BF)],
        (ids, *gpieces, e, inv_l, k, v, qst, kt, tokens, query_weight.T, key_weight.T, value_weight.T, d_mine, d_recv, vg),
        prefetch=1, grid=(blocks,),
        specs=[pick(c, quarter), pick(c, quarter), pl.BlockSpec((2, 1, c, quarter), lambda b, *_: (0, b, 0, 0)),
               pl.BlockSpec((2, 1, c, quarter), lambda b, *_: (0, b, 0, 0)), pick(heads, length, length), pick(8, length),
               pl.BlockSpec((length, c), lambda b, *_: (b, 0)), pl.BlockSpec((length, c), lambda b, *_: (b, 0)), pick(c, length), pick(c, length),
               pl.BlockSpec((length, d), lambda b, *_: (b, 0)), full(c, d), full(c, d), full(c, d), full(c + 16, d), full(c + 16, d), full(8, d)],
        out_specs=[full(2, t, d), full(2, t, d), full(2, n_c // 4, d), full(2, n_c // 4, d)],
        scratch=[pltpu.VMEM((c, length), BF), pltpu.VMEM((3 * c, length), BF), pltpu.VMEM((length, d), BF), pltpu.VMEM((3 * c, d), F32), pltpu.VMEM((16, d), F32),
                 pltpu.VMEM((n_c, d), F32)],
        us=15, name="attend_back",
    )
    got = hop(send, 1)
    c_got = hop(csend, 1, "dp")
    a_got, b_got, student_2 = after(a_got, keep), after(b_got, keep), after(student_2, keep)
    students = (student_rows, student_1, student_2, hop(student_2, 1))
    a_mine, a_give = add(akeep[0], a_got[0]), add(akeep[1], a_got[1])
    b_mine, b_give = add(bkeep[0], b_got[0]), add(bkeep[1], b_got[1])
    a_got, b_got = hop(a_give, 2, "dp"), hop(b_give, 1, "dp")
    give = add(keep[1], got[1])
    mine = add(keep[0], got[0])
    recv = hop(give, 2)
    both = after(jnp.stack([add(a_mine, a_got), add(b_mine, b_got)]), give)

    def across(x):
        mask = 4
        while mask < n_dp:
            x = add(x, hop(x, mask, "dp"))
            mask *= 2
        return x

    summed = across(both)
    c_got = after(c_got, both)
    c_mine, c_give = add(ckeep[0], c_got[0]), add(ckeep[1], c_got[1])
    c_got = hop(c_give, 2, "dp")
    (pruned_rows,) = call(
        hard_kernel,
        [((t + 16, d), BF)],
        (ids, after(c0, both, c_give), *pieces[1:], *inners, *outers, *packs, tokens, teacher, present, consts),
        prefetch=1, specs=[VM] * 4 + [ANY] * 18 + [VM] * 2,
        scratch=[pltpu.VMEM((4, d, w), BF), pltpu.VMEM((4, c, w), BF), pltpu.VMEM((4, w, d), BF), pltpu.VMEM((4, VEC, w), BF), pltpu.VMEM((t, d), BF),
                 pltpu.VMEM((t, d), BF), pltpu.VMEM((4, t, c), BF), pltpu.VMEM((t, d), F32), pltpu.VMEM((t, d), F32), pltpu.VMEM((t, d), BF),
                 pltpu.VMEM((4, t, w), BF), pltpu.VMEM((8, d), F32), pltpu.SemaphoreType.DMA((3, 8)), pltpu.SemaphoreType.DMA((2, blocks))],
        us=15, name="hard",
    )
    recv, c_got = after(recv, pruned_rows), after(c_got, pruned_rows)
    grad_rows = (grad_one + (mine.astype(F32) + recv.astype(F32))).astype(BF)
    grad_2 = hop(grad_rows, 2)
    grad_1 = hop(grad_rows, 1)
    pruned_2 = hop(after(pruned_rows, grad_rows), 2)
    pruned_1 = hop(pruned_rows, 1)
    c_mine = across(add(c_mine, c_got))
    summed = after(summed, grad_rows)
    a_mine, b_mine = summed[0], summed[1]
    a_other, b_other = hop(a_mine, 2, "dp"), hop(b_mine, 1, "dp")
    a_parts = (a_mine, a_other, hop(jnp.stack([a_mine, a_other]), 1, "dp"))
    b_parts = (b_mine, b_other, hop(jnp.stack([b_mine, b_other]), 2, "dp"))
    c_other = hop(c_mine, 2, "dp")
    c_parts = (c_mine, c_other, hop(jnp.stack([c_mine, c_other]), 1, "dp"))
    grads = (grad_rows, grad_1, grad_2, hop(grad_2, 1))
    pruneds = (pruned_rows, pruned_1, pruned_2, hop(pruned_2, 1))
    hard_sum = jnp.broadcast_to(sum(jnp.sum(x[t : t + 8, :128].astype(F32)) for x in pruneds), (8, 128))
    mask = 1
    while mask < n_dp:
        hard_sum = hard_sum + hop(hard_sum, mask, "dp")
        mask *= 2

    outs = call(
        spread_kernel,
        [((blocks, length, d), BF)] * 3,
        (ids, *students, *pruneds, *grads),
        prefetch=1, specs=[VM] * 12, out_specs=[ANY] * 3, scratch=[pltpu.SemaphoreType.DMA((12 * blocks,))], us=3, name="spread",
    )
    student, pruned, tokens_grad = (o.reshape(rows, d) for o in outs)

    uw, iw, qw, kw, vw, ow, qb, vb, ob, fg, fs, ib, ub, sg, ss, ha, ua, da, me, pe = call(
        final_kernel,
        [((w, d), F32), ((d, w), F32), ((c, d), F32), ((c, d), F32), ((c, d), F32), ((c, d), F32), ((c,), F32), ((c,), F32), ((d,), F32), ((d,), F32), ((d,), F32),
         ((w,), F32), ((d,), F32), ((d,), F32), ((d,), F32), ((heads,), F32), ((w,), F32), ((d,), F32), ((1,), F32), ((1,), F32)],
        (ids, consts, *a_parts, *b_parts, *c_parts, hard_sum),
        prefetch=1, specs=[VM] * 11, out_specs=[VM] * 15 + [SM] + [VM] * 2 + [SM] * 2,
        scratch=[pltpu.VMEM((n_c, d), F32)], us=4, name="final",
    )
    return (
        student, pruned, tokens_grad, qw.T, qb, kw.T, vw.T, vb, ow, ob, fg, fs, iw, ib, uw, ub, sg, ss, ha, ua, da, me.reshape(()), pe.reshape(()),
    )


def solution(mesh):
    row, col, lead, unit, none = P("dp", None), P(None, "head"), P("head", None), P("head"), P()
    return jax.shard_map(
        partial(shards, n_dp=mesh.shape["dp"]),
        mesh=mesh,
        in_specs=(row, row, row, row, col, unit, col, col, unit, lead, none, none, none, col, unit, lead, none, none, none) + (unit,) * 4 + (none,) * 2 + (unit,) * 2 + (none,),
        out_specs=(row, row, row, col, unit, col, col, unit, lead, none, none, none, col, unit, lead, none, none, none, unit, unit, none, none, none),
        check_vma=False,
    )
```

profile of v0, /device:TPU:0, one launch (start us, length us, event | category | flops | bytes accessed | tf_op | source)
XLA Modules:
  0.0 286.6 jit_solution(5888283141039745473)
XLA Ops:
  0.7 2.1 prep.1
  2.9 3.0 %collective-permute-start.4 = (bf16[224,768]{1,0:T(8,128)(2,1)}, bf16[224,768]{1,0:T(8,128)(2,1)}, u32[]{:S(2)}, u32[]{:S(2)}) collective-permute-start(bf16[224,768]{1,0:T(8,128)(2,1)} %get-tuple-element.112.s0.refs_6_.refs_12_), channel_id=1, source_target_pairs={{0,2},{1,3},{2,0},{3,1},{4,6},{5,7},{6,4},{7,5},{8,10},{9,11},{10,... | collective-permute-start | bytes 1032200 | tf_op jit(solution)/shard_map/ppermute | solution.py:650
  7.6 2.0 collective-permute-start.7
  9.7 12.6 %attend.1 = (bf16[3,192,128]{2,1,0:T(8,128)(2,1)S(1)}, bf16[3,192,128]{2,1,0:T(8,128)(2,1)S(1)}, bf16[2,3,192,128]{3,2,1,0:T(8,128)(2,1)S(1)}, bf16[3,3,512,512]...) custom-call(s32[5]{0:T(128)S(1)} %stack.49.ids.h_ref, ...), custom_call_target="tpu_custom_call" | custom-call | flops 4499999744 | tf_op jit(solution)/shard_map/attend/pallas_call | solution.py:59
  22.5 17.9 %collective-permute-done.7.refs_2_ = bf16[384,768]{1,0:T(8,128)(2,1)} collective-permute-done((bf16[384,768]{1,0:T(8,128)(2,1)}, bf16[384,768]{1,0:T(8,128)(2,1)}, u32[]{:S(2)}, u32[]{:S(2)}) %collective-permute-start.7) | collective-permute-done | bytes 589856 | tf_op jit(solution)/shard_map/ppermute | solution.py:650
  40.3 2.1 collective-permute-start.8
  43.0 2.8 collective-permute-done.1.xr
  47.8 1.8 collective-permute-start.13
  49.6 6.6 %first.1 = (bf16[384,768]{1,0:T(8,128)(2,1)}, f32[384,768]{1,0:T(8,128)S(1)}, f32[384,128]{1,0:T(8,128)S(1)}, f32[384,768]{1,0:T(8,128)S(1)}, bf16[4,384,192]{2,1,0:T(8,128)(2,1)S(1)}) custom-call(s32[5]{0:T(128)S(1)} %stack.49.ids.h_ref, bf16[3,192,128]{2,1,0:T(8,128)(2,1)S(1)} %get-tuple-element.164.c0, bf16[3,192,128]{2,1,0:T(8,128)(2,1)S(1)} %collective-permute-done.c1, ...), custom_call_target="tpu_custom_call" | custom-call | flops 2500000000 | tf_op jit(solution)/shard_map/first/pallas_call | solution.py:59
  59.7 7.2 %collective-permute-done.13.refs_3_.refs_9_ = bf16[384,768]{1,0:T(8,128)(2,1)S(1)} collective-permute-done((bf16[384,768]{1,0:T(8,128)(2,1)S(1)}, bf16[384,768]{1,0:T(8,128)(2,1)S(1)}, u32[]{:S(2)}, u32[]{:S(2)}) %collective-permute-start.13) | collective-permute-done | bytes 589856 | tf_op jit(solution)/shard_map/ppermute | solution.py:650
  66.9 9.0 %inner.1 = (bf16[4,384,768]{2,1,0:T(8,128)(2,1)S(1)}, bf16[4,384,768]{2,1,0:T(8,128)(2,1)S(1)}) custom-call(s32[5]{0:T(128)S(1)} %stack.49.ids.h_ref, bf16[384,768]{1,0:T(8,128)(2,1)} %get-tuple-element.133.first_low.f0, bf16[768,768]{1,0:T(8,128)(2,1)S(1)} %copy-done.1, bf16[768,768]{1,0:T(8,128)(2,1)S(1)} %collective-permute-done.6.refs_1_, ...), custom_call_target="tpu_custom_call" | custom-call | flops 4499999744 | tf_op jit(solution)/shard_map/inner/pallas_call | solution.py:59
  82.3 20.8 %second.1 = (bf16[384,768]{1,0:T(8,128)(2,1)}, f32[384,768]{1,0:T(8,128)S(1)}, bf16[384,768]{1,0:T(8,128)(2,1)}, f32[8,768]{1,0:T(8,128)S(1)}) custom-call(s32[5]{0:T(128)S(1)} %stack.49.ids.h_ref, bf16[4,384,768]{2,1,0:T(8,128)(2,1)S(1)} %get-tuple-element.117.hidden, f32[384,768]{1,0:T(8,128)S(1)} %copy-done.39, bf16[768,768]{1,0:T(8,128)(2,1)S(1)} %copy-done.2, ...), custom_call_target="tpu_custom_call" | custom-call | flops 3000000000 | tf_op jit(solution)/shard_map/second/pallas_call | solution.py:59
  105.4 16.0 %back.1 = (bf16[3,192,128]{2,1,0:T(8,128)(2,1)S(1)}, bf16[3,192,128]{2,1,0:T(8,128)(2,1)}, bf16[2,3,192,128]{3,2,1,0:T(8,128)(2,1)S(1)}, bf16[2,208,768]{2,1,0:T...) custom-call(s32[5]{0:T(128)S(1)} %stack.49.ids.h_ref, ...), custom_call_target="tpu_custom_call" | custom-call | flops 6499999744 | tf_op jit(solution)/shard_map/back/pallas_call | solution.py:59
  123.9 6.8 %units.1 = (bf16[1536,768]{1,0:T(8,128)(2,1)S(1)}, bf16[1536,768]{1,0:T(8,128)(2,1)S(1)}) custom-call(bf16[384,768]{1,0:T(8,128)(2,1)} %get-tuple-element.133.first_low.f0, bf16[384,768]{1,0:T(8,128)(2,1)S(1)} %collective-permute-done.16.f1, bf16[384,768]{1,0:T(8,128)(2,1)S(1)} %collective-permute-done.17.fx, ...), custom_call_target="tpu_custom_call" | custom-call | flops 3000000000 | tf_op jit(solution)/shard_map/units/pallas_call | solution.py:59
  134.1 1.7 copy-done.45
  135.8 8.1 %grads.1 = (bf16[2,192,768]{2,1,0:T(8,128)(2,1)S(1)}, bf16[2,192,768]{2,1,0:T(8,128)(2,1)S(1)}, bf16[2,192,768]{2,1,0:T(8,128)(2,1)S(1)}, bf16[2,192,768]{2,1,0:T(8,128)(2,1)S(1)}, f32[8,768]{1,0:T(8,128)S(1)}) custom-call(s32[5]{0:T(128)S(1)} %stack.49.ids.h_ref, bf16[384,768]{1,0:T(8,128)(2,1)} %get-tuple-element.133.first_low.f0, ...), custom_call_target="tpu_custom_call" | custom-call | flops 4000000000 | tf_op jit(solution)/shard_map/grads/pallas_call | solution.py:59
  151.2 14.7 %attend_back.1 = (bf16[2,384,768]{2,1,0:T(8,128)(2,1)S(1)}, bf16[2,384,768]{2,1,0:T(8,128)(2,1)S(1)}, bf16[2,208,768]{2,1,0:T(8,128)(2,1)S(1)}, bf16[2,208,768]{2,1,0:T(8,128)(2,1)S(1)}) custom-call(s32[5]{0:T(128)S(1)} %stack.49.ids.h_ref, bf16[3,192,128]{2,1,0:T(8,128)(2,1)S(1)} %copy-done.53, bf16[3,192,128]{2,1,0:T(8,128)(2,1)S(1)} %collective-permute-done.24.g1, ...), custom_call_target="tpu_custom_call" | custom-call | flops 7500000256 | tf_op jit(solution)/shard_map/attend_back/pallas_call | solution.py:59
  168.8 6.8 %collective-permute-done.31 = bf16[192,768]{1,0:T(8,128)(2,1)S(1)} collective-permute-done((bf16[192,768]{1,0:T(8,128)(2,1)S(1)}, bf16[192,768]{1,0:T(8,128)(2,1)S(1)}, u32[]{:S(2)}, u32[]{:S(2)}) %collective-permute-start.31) | collective-permute-done | bytes 294944 | tf_op jit(solution)/shard_map/ppermute | solution.py:650
  178.4 11.2 %collective-permute-done.35 = bf16[2,208,768]{2,1,0:T(8,128)(2,1)S(1)} collective-permute-done((bf16[2,208,768]{2,1,0:T(8,128)(2,1)S(1)}, bf16[2,208,768]{2,1,0:T(8,128)(2,1)S(1)}, u32[]{:S(2)}, u32[]{:S(2)}) %collective-permute-start.35) | collective-permute-done | bytes 639008 | tf_op jit(solution)/shard_map/ppermute | solution.py:650
  189.6 1.7 collective-permute-start.48
  191.3 2.6 collective-permute-start.43
  194.0 17.7 %hard.1.refs_4_ = bf16[400,768]{1,0:T(8,128)(2,1)S(1)} custom-call(s32[5]{0:T(128)S(1)} %stack.49.ids.h_ref, bf16[3,192,128]{2,1,0:T(8,128)(2,1)S(1)} %copy-done.51, bf16[3,192,128]{2,1,0:T(8,128)(2,1)S(1)} %collective-permute-done.c1, bf16[2,3,192,128]{3,2,1,0:T(8,128)(2,1)S(1)} %copy-done.35, bf16[2,3,192,128]{3,2,1,0:T(8,128)(2,1)S(1)} %copy-done.37, ...), custom_call_target="tpu_custom_call" | custom-call | flops 7500000256 | tf_op jit(solution)/shard_map/hard/pallas_call | solution.py:59
  214.1 5.1 %collective-permute-done.43 = bf16[2,192,768]{2,1,0:T(8,128)(2,1)S(1)} collective-permute-done((bf16[2,192,768]{2,1,0:T(8,128)(2,1)S(1)}, bf16[2,192,768]{2,1,0:T(8,128)(2,1)S(1)}, u32[]{:S(2)}, u32[]{:S(2)}) %collective-permute-start.43) | collective-permute-done | bytes 589856 | tf_op jit(solution)/shard_map/ppermute | solution.py:650
  219.4 7.3 %collective-permute-done.38.refs_6_ = bf16[400,768]{1,0:T(8,128)(2,1)S(1)} collective-permute-done((bf16[400,768]{1,0:T(8,128)(2,1)S(1)}, bf16[400,768]{1,0:T(8,128)(2,1)S(1)}, u32[]{:S(2)}, u32[]{:S(2)}) %collective-permute-start.38) | collective-permute-done | bytes 614432 | tf_op jit(solution)/shard_map/ppermute | solution.py:650
  230.1 4.5 %collective-permute-done.49 = bf16[208,768]{1,0:T(8,128)(2,1)} collective-permute-done((bf16[208,768]{1,0:T(8,128)(2,1)S(1)}, bf16[208,768]{1,0:T(8,128)(2,1)}, u32[]{:S(2)}, u32[]{:S(2)}) %collective-permute-start.49) | collective-permute-done | bytes 319520 | tf_op jit(solution)/shard_map/ppermute | solution.py:650
  237.9 1.9 pad_maximum_fusion.3
  243.9 4.0 %collective-permute-done.50.co = bf16[208,768]{1,0:T(8,128)(2,1)} collective-permute-done((bf16[208,768]{1,0:T(8,128)(2,1)S(1)}, bf16[208,768]{1,0:T(8,128)(2,1)}, u32[]{:S(2)}, u32[]{:S(2)}) %collective-permute-start.50) | collective-permute-done | bytes 319520 | tf_op jit(solution)/shard_map/ppermute | solution.py:650
  249.9 1.7 collective-permute-done.52
  257.7 5.5 %spread.1 = (bf16[3,512,768]{2,1,0:T(8,128)(2,1)}, bf16[3,512,768]{2,1,0:T(8,128)(2,1)}, bf16[3,512,768]{2,1,0:T(8,128)(2,1)}) custom-call(s32[5]{0:T(128)S(1)} %stack.49.ids.h_ref, bf16[384,768]{1,0:T(8,128)(2,1)} %get-tuple-element.137.refs_0_, bf16[384,768]{1,0:T(8,128)(2,1)} %collective-permute-done.22.refs_1_, ...), custom_call_target="tpu_custom_call" | custom-call | flops 1500000000 | tf_op jit(solution)/shard_map/spread/pallas_call | solution.py:59
  263.2 4.8 %collective-permute-done.54 = f32[8,128]{1,0:T(8,128)S(1)} collective-permute-done((f32[8,128]{1,0:T(8,128)S(1)}, f32[8,128]{1,0:T(8,128)S(1)}, u32[]{:S(2)}, u32[]{:S(2)}) %collective-permute-start.54) | collective-permute-done | bytes 4128 | tf_op jit(solution)/shard_map/ppermute | solution.py:650
  269.0 12.1 %collective-permute-done.45.aq = bf16[2,192,768]{2,1,0:T(8,128)(2,1)S(1)} collective-permute-done((bf16[2,192,768]{2,1,0:T(8,128)(2,1)S(1)}, bf16[2,192,768]{2,1,0:T(8,128)(2,1)S(1)}, u32[]{:S(2)}, u32[]{:S(2)}) %collective-permute-start.45) | collective-permute-done | bytes 589856 | tf_op jit(solution)/shard_map/ppermute | solution.py:650
  281.0 5.3 %final.1 = (f32[768,768]{1,0:T(8,128)}, f32[768,768]{1,0:T(8,128)}, f32[192,768]{1,0:T(8,128)}, f32[192,768]{1,0:T(8,128)}, f32[192,768]{1,0:T(8,128)}, /*index=...) custom-call(s32[5]{0:T(128)S(1)} %stack.49.ids.h_ref, ...), custom_call_target="tpu_custom_call" | custom-call | flops 2000000000 | tf_op jit(solution)/shard_map/final/pallas_call | solution.py:59
  (243 shorter events, 55.3 us)
Async XLA Ops:
  2.9 39.6 %collective-permute-start.4 = (bf16[224,768]{1,0:T(8,128)(2,1)}, bf16[224,768]{1,0:T(8,128)(2,1)}, u32[]{:S(2)}, u32[]{:S(2)}) collective-permute-start(bf16[224,768]{1,0:T(8,128)(2,1)} %get-tuple-element.112.s0.refs_6_.refs_12_), channel_id=1, source_target_pairs={{0,2},{1,3},{2,0},{3,1},{4,6},{5,7},{6,4},{7,5},{8,10},{9,11},{10,... | collective-permute-start | bytes 1032200 | tf_op jit(solution)/shard_map/ppermute | solution.py:650
  6.7 39.0 %collective-permute-start.12 = (bf16[384,768]{1,0:T(8,128)(2,1)}, bf16[384,768]{1,0:T(8,128)(2,1)S(1)}, u32[]{:S(2)}, u32[]{:S(2)}) collective-permute-start(bf16[384,768]{1,0:T(8,128)(2,1)} %constant_dynamic-slice_fusion), channel_id=1, source_target_pairs={{0,2},{1,3},{2,0},{3,1},{4,6},{5,7},{6,4},{7,5},{8,10},{9,11},{10,... | collective-permute-start | bytes 1769480 | tf_op jit(solution)/shard_map/ppermute | solution.py:650
  7.6 32.7 %collective-permute-start.7 = (bf16[384,768]{1,0:T(8,128)(2,1)}, bf16[384,768]{1,0:T(8,128)(2,1)}, u32[]{:S(2)}, u32[]{:S(2)}) collective-permute-start(bf16[384,768]{1,0:T(8,128)(2,1)} %constant_dynamic-slice_fusion.1), channel_id=1, source_target_pairs={{0,2},{1,3},{2,0},{3,1},{4,6},{5,7},{6,4},{7,5},{8,10},{9,11},{10,... | collective-permute-start | bytes 1769480 | tf_op jit(solution)/shard_map/ppermute | solution.py:650
  22.3 23.4 %collective-permute-start.1 = (bf16[2,3,192,128]{3,2,1,0:T(8,128)(2,1)S(1)}, bf16[2,3,192,128]{3,2,1,0:T(8,128)(2,1)S(1)}, u32[]{:S(2)}, u32[]{:S(2)}) collective-permute-start(bf16[2,3,192,128]{3,2,1,0:T(8,128)(2,1)S(1)} %get-tuple-element.111), channel_id=1, source_target_pairs={{0,2},{1,3},{2,0},{3,1},{4,6},{5,7},{6,4},{7,5},{8,10},{9,11},{10,... | collective-permute-start | bytes 884744 | tf_op jit(solution)/shard_map/ppermute | solution.py:650
  22.4 20.1 %collective-permute-start = (bf16[3,192,128]{2,1,0:T(8,128)(2,1)S(1)}, bf16[3,192,128]{2,1,0:T(8,128)(2,1)S(1)}, u32[]{:S(2)}, u32[]{:S(2)}) collective-permute-start(bf16[3,192,128]{2,1,0:T(8,128)(2,1)S(1)} %get-tuple-element.110), channel_id=1, source_target_pairs={{0,1},{1,0},{2,3},{3,2},{4,5},{5,4},{6,7},{7,6},{8,9},{9,8},{10,11... | collective-permute-start | bytes 442376 | tf_op jit(solution)/shard_map/ppermute | solution.py:650
  40.3 18.8 %collective-permute-start.8 = (bf16[384,768]{1,0:T(8,128)(2,1)}, bf16[384,768]{1,0:T(8,128)(2,1)S(1)}, u32[]{:S(2)}, u32[]{:S(2)}) collective-permute-start(bf16[384,768]{1,0:T(8,128)(2,1)} %collective-permute-done.7.refs_2_), channel_id=1, source_target_pairs={{0,4},{4,0},{8,12},{12,8},{16,20},{20,16},{24,28},{28,24},{1,5},{5... | collective-permute-start | bytes 1769480 | tf_op jit(solution)/shard_map/ppermute | solution.py:650
  42.4 24.5 %collective-permute-start.6 = (bf16[768,768]{1,0:T(8,128)(2,1)S(1)}, bf16[768,768]{1,0:T(8,128)(2,1)S(1)}, u32[]{:S(2)}, u32[]{:S(2)}) collective-permute-start(bf16[768,768]{1,0:T(8,128)(2,1)S(1)} %copy-done.1), channel_id=1, source_target_pairs={{0,1},{1,0},{2,3},{3,2},{4,5},{5,4},{6,7},{7,6},{8,9},{9,8},{10,11... | collective-permute-start | bytes 3538952 | tf_op jit(solution)/shard_map/ppermute | solution.py:650
  46.3 20.6 %collective-permute-start.9 = (bf16[384,768]{1,0:T(8,128)(2,1)}, bf16[384,768]{1,0:T(8,128)(2,1)S(1)}, u32[]{:S(2)}, u32[]{:S(2)}) collective-permute-start(bf16[384,768]{1,0:T(8,128)(2,1)} %collective-permute-done.7.refs_2_), channel_id=1, source_target_pairs={{0,1},{1,0},{2,3},{3,2},{4,5},{5,4},{6,7},{7,6},{8,9},{9,8},{10,11... | collective-permute-start | bytes 1769480 | tf_op jit(solution)/shard_map/ppermute | solution.py:650
  47.8 19.1 %collective-permute-start.13 = (bf16[384,768]{1,0:T(8,128)(2,1)S(1)}, bf16[384,768]{1,0:T(8,128)(2,1)S(1)}, u32[]{:S(2)}, u32[]{:S(2)}) collective-permute-start(bf16[384,768]{1,0:T(8,128)(2,1)S(1)} %collective-permute-done.12.refs_2_.refs_8_), channel_id=1, source_target_pairs={{0,4},{4,0},{8,12},{12,8},{16,20},{20,16},{24,28},{28,24},{1,5},{5... | collective-permute-start | bytes 1769480 | tf_op jit(solution)/shard_map/ppermute | solution.py:650
  59.2 20.1 %collective-permute-start.11 = (bf16[768,768]{1,0:T(8,128)(2,1)S(1)}, bf16[768,768]{1,0:T(8,128)(2,1)S(1)}, u32[]{:S(2)}, u32[]{:S(2)}) collective-permute-start(bf16[768,768]{1,0:T(8,128)(2,1)S(1)} %copy-done.2), channel_id=1, source_target_pairs={{0,1},{1,0},{2,3},{3,2},{4,5},{5,4},{6,7},{7,6},{8,9},{9,8},{10,11... | collective-permute-start | bytes 3538952 | tf_op jit(solution)/shard_map/ppermute | solution.py:650
  77.8 27.4 %collective-permute-start.17 = (bf16[384,768]{1,0:T(8,128)(2,1)}, bf16[384,768]{1,0:T(8,128)(2,1)S(1)}, u32[]{:S(2)}, u32[]{:S(2)}) collective-permute-start(bf16[384,768]{1,0:T(8,128)(2,1)} %get-tuple-element.133.first_low.f0), channel_id=1, source_target_pairs={{0,2},{1,3},{2,0},{3,1},{4,6},{5,7},{6,4},{7,5},{8,10},{9,11},{10,... | collective-permute-start | bytes 1769480 | tf_op jit(solution)/shard_map/ppermute | solution.py:650
  79.3 43.8 %collective-permute-start.16 = (bf16[384,768]{1,0:T(8,128)(2,1)}, bf16[384,768]{1,0:T(8,128)(2,1)S(1)}, u32[]{:S(2)}, u32[]{:S(2)}) collective-permute-start(bf16[384,768]{1,0:T(8,128)(2,1)} %get-tuple-element.133.first_low.f0), channel_id=1, source_target_pairs={{0,1},{1,0},{2,3},{3,2},{4,5},{5,4},{6,7},{7,6},{8,9},{9,8},{10,11... | collective-permute-start | bytes 1769480 | tf_op jit(solution)/shard_map/ppermute | solution.py:650
  104.1 18.6 %collective-permute-start.20 = (bf16[384,768]{1,0:T(8,128)(2,1)}, bf16[384,768]{1,0:T(8,128)(2,1)S(1)}, u32[]{:S(2)}, u32[]{:S(2)}) collective-permute-start(bf16[384,768]{1,0:T(8,128)(2,1)} %get-tuple-element.123.gffn.g0), channel_id=1, source_target_pairs={{0,2},{1,3},{2,0},{3,1},{4,6},{5,7},{6,4},{7,5},{8,10},{9,11},{10,... | collective-permute-start | bytes 1769480 | tf_op jit(solution)/shard_map/ppermute | solution.py:650
  105.3 18.6 %collective-permute-start.18 = (bf16[384,768]{1,0:T(8,128)(2,1)S(1)}, bf16[384,768]{1,0:T(8,128)(2,1)S(1)}, u32[]{:S(2)}, u32[]{:S(2)}) collective-permute-start(bf16[384,768]{1,0:T(8,128)(2,1)S(1)} %collective-permute-done.17.fx), channel_id=1, source_target_pairs={{0,1},{1,0},{2,3},{3,2},{4,5},{5,4},{6,7},{7,6},{8,9},{9,8},{10,11... | collective-permute-start | bytes 1769480 | tf_op jit(solution)/shard_map/ppermute | solution.py:650
  123.9 23.1 %collective-permute-start.24 = (bf16[3,192,128]{2,1,0:T(8,128)(2,1)}, bf16[3,192,128]{2,1,0:T(8,128)(2,1)S(1)}, u32[]{:S(2)}, u32[]{:S(2)}) collective-permute-start(bf16[3,192,128]{2,1,0:T(8,128)(2,1)} %get-tuple-element.139), channel_id=1, source_target_pairs={{0,1},{1,0},{2,3},{3,2},{4,5},{5,4},{6,7},{7,6},{8,9},{9,8},{10,11... | collective-permute-start | bytes 442376 | tf_op jit(solution)/shard_map/ppermute | solution.py:650
  132.2 15.6 %collective-permute-start.26 = (bf16[2,3,192,128]{3,2,1,0:T(8,128)(2,1)S(1)}, bf16[2,3,192,128]{3,2,1,0:T(8,128)(2,1)S(1)}, u32[]{:S(2)}, u32[]{:S(2)}) collective-permute-start(bf16[2,3,192,128]{3,2,1,0:T(8,128)(2,1)S(1)} %collective-permute-done.25.gxr), channel_id=1, source_target_pairs={{0,1},{1,0},{2,3},{3,2},{4,5},{5,4},{6,7},{7,6},{8,9},{9,8},{10,11... | collective-permute-start | bytes 884744 | tf_op jit(solution)/shard_map/ppermute | solution.py:650
  132.8 15.0 %collective-permute-start.28 = (bf16[208,768]{1,0:T(8,128)(2,1)S(1)}, bf16[208,768]{1,0:T(8,128)(2,1)S(1)}, u32[]{:S(2)}, u32[]{:S(2)}) collective-permute-start(bf16[208,768]{1,0:T(8,128)(2,1)S(1)} %get-tuple-element.193), channel_id=1, source_target_pairs={{0,2},{1,3},{2,0},{3,1},{4,6},{5,7},{6,4},{7,5},{8,10},{9,11},{10,... | collective-permute-start | bytes 958472 | tf_op jit(solution)/shard_map/ppermute | solution.py:650
  143.9 22.1 %collective-permute-start.30 = (bf16[2,192,768]{2,1,0:T(8,128)(2,1)S(1)}, bf16[2,192,768]{2,1,0:T(8,128)(2,1)S(1)}, u32[]{:S(2)}, u32[]{:S(2)}) collective-permute-start(bf16[2,192,768]{2,1,0:T(8,128)(2,1)S(1)} %get-tuple-element.154), channel_id=1, source_target_pairs={{0,4},{4,0},{8,12},{12,8},{16,20},{20,16},{24,28},{28,24},{1,5},{5... | collective-permute-start | bytes 1769480 | tf_op jit(solution)/shard_map/ppermute | solution.py:650
  145.5 21.2 %collective-permute-start.32 = (bf16[2,192,768]{2,1,0:T(8,128)(2,1)S(1)}, bf16[2,192,768]{2,1,0:T(8,128)(2,1)S(1)}, u32[]{:S(2)}, u32[]{:S(2)}) collective-permute-start(bf16[2,192,768]{2,1,0:T(8,128)(2,1)S(1)} %get-tuple-element.157), channel_id=1, source_target_pairs={{0,8},{4,12},{8,0},{12,4},{16,24},{20,28},{24,16},{28,20},{1,9},{5... | collective-permute-start | bytes 1769480 | tf_op jit(solution)/shard_map/ppermute | solution.py:650
  147.0 20.3 %collective-permute-start.23 = (bf16[384,768]{1,0:T(8,128)(2,1)}, bf16[384,768]{1,0:T(8,128)(2,1)}, u32[]{:S(2)}, u32[]{:S(2)}) collective-permute-start(bf16[384,768]{1,0:T(8,128)(2,1)} %get-tuple-element.137.refs_0_), channel_id=1, source_target_pairs={{0,2},{1,3},{2,0},{3,1},{4,6},{5,7},{6,4},{7,5},{8,10},{9,11},{10,... | collective-permute-start | bytes 1769480 | tf_op jit(solution)/shard_map/ppermute | solution.py:650
  167.4 84.2 %collective-permute-start.22 = (bf16[384,768]{1,0:T(8,128)(2,1)}, bf16[384,768]{1,0:T(8,128)(2,1)}, u32[]{:S(2)}, u32[]{:S(2)}) collective-permute-start(bf16[384,768]{1,0:T(8,128)(2,1)} %get-tuple-element.137.refs_0_), channel_id=1, source_target_pairs={{0,1},{1,0},{2,3},{3,2},{4,5},{5,4},{6,7},{7,6},{8,9},{9,8},{10,11... | collective-permute-start | bytes 1769480 | tf_op jit(solution)/shard_map/ppermute | solution.py:650
  167.4 22.2 %collective-permute-start.35 = (bf16[2,208,768]{2,1,0:T(8,128)(2,1)S(1)}, bf16[2,208,768]{2,1,0:T(8,128)(2,1)S(1)}, u32[]{:S(2)}, u32[]{:S(2)}) collective-permute-start(bf16[2,208,768]{2,1,0:T(8,128)(2,1)S(1)} %get-tuple-element.162), channel_id=1, source_target_pairs={{0,4},{4,0},{8,12},{12,8},{16,20},{20,16},{24,28},{28,24},{1,5},{5... | collective-permute-start | bytes 1916936 | tf_op jit(solution)/shard_map/ppermute | solution.py:650
  175.6 78.9 %collective-permute-start.29 = (bf16[384,768]{1,0:T(8,128)(2,1)}, bf16[384,768]{1,0:T(8,128)(2,1)}, u32[]{:S(2)}, u32[]{:S(2)}) collective-permute-start(bf16[384,768]{1,0:T(8,128)(2,1)} %collective-permute-done.23.refs_2_), channel_id=1, source_target_pairs={{0,1},{1,0},{2,3},{3,2},{4,5},{5,4},{6,7},{7,6},{8,9},{9,8},{10,11... | collective-permute-start | bytes 1769480 | tf_op jit(solution)/shard_map/ppermute | solution.py:650
  177.0 34.7 %collective-permute-start.37 = (bf16[384,768]{1,0:T(8,128)(2,1)S(1)}, bf16[384,768]{1,0:T(8,128)(2,1)S(1)}, u32[]{:S(2)}, u32[]{:S(2)}) collective-permute-start(bf16[384,768]{1,0:T(8,128)(2,1)S(1)} %fusion.3), channel_id=1, source_target_pairs={{0,2},{1,3},{2,0},{3,1},{4,6},{5,7},{6,4},{7,5},{8,10},{9,11},{10,... | collective-permute-start | bytes 1769480 | tf_op jit(solution)/shard_map/ppermute | solution.py:650
  189.6 24.3 %collective-permute-start.48 = (bf16[208,768]{1,0:T(8,128)(2,1)S(1)}, bf16[208,768]{1,0:T(8,128)(2,1)S(1)}, u32[]{:S(2)}, u32[]{:S(2)}) collective-permute-start(bf16[208,768]{1,0:T(8,128)(2,1)S(1)} %fusion.9), channel_id=1, source_target_pairs={{0,8},{4,12},{8,0},{12,4},{16,24},{20,28},{24,16},{28,20},{1,9},{5... | collective-permute-start | bytes 958472 | tf_op jit(solution)/shard_map/ppermute | solution.py:650
  191.3 27.9 %collective-permute-start.43 = (bf16[2,192,768]{2,1,0:T(8,128)(2,1)S(1)}, bf16[2,192,768]{2,1,0:T(8,128)(2,1)S(1)}, u32[]{:S(2)}, u32[]{:S(2)}) collective-permute-start(bf16[2,192,768]{2,1,0:T(8,128)(2,1)S(1)} %pad_maximum_fusion.1), channel_id=1, source_target_pairs={{0,16},{4,20},{8,24},{12,28},{16,0},{20,4},{24,8},{28,12},{1,17},{... | collective-permute-start | bytes 1769480 | tf_op jit(solution)/shard_map/ppermute | solution.py:650
  212.0 14.6 %collective-permute-start.38 = (bf16[400,768]{1,0:T(8,128)(2,1)S(1)}, bf16[400,768]{1,0:T(8,128)(2,1)S(1)}, u32[]{:S(2)}, u32[]{:S(2)}) collective-permute-start(bf16[400,768]{1,0:T(8,128)(2,1)S(1)} %hard.1.refs_4_), channel_id=1, source_target_pairs={{0,2},{1,3},{2,0},{3,1},{4,6},{5,7},{6,4},{7,5},{8,10},{9,11},{10,... | collective-permute-start | bytes 1843208 | tf_op jit(solution)/shard_map/ppermute | solution.py:650
  219.2 15.3 %collective-permute-start.49 = (bf16[208,768]{1,0:T(8,128)(2,1)S(1)}, bf16[208,768]{1,0:T(8,128)(2,1)}, u32[]{:S(2)}, u32[]{:S(2)}) collective-permute-start(bf16[208,768]{1,0:T(8,128)(2,1)S(1)} %fusion.2), channel_id=1, source_target_pairs={{0,16},{4,20},{8,24},{12,28},{16,0},{20,4},{24,8},{28,12},{1,17},{... | collective-permute-start | bytes 958472 | tf_op jit(solution)/shard_map/ppermute | solution.py:650
  234.5 15.4 %collective-permute-start.41 = (bf16[384,768]{1,0:T(8,128)(2,1)S(1)}, bf16[384,768]{1,0:T(8,128)(2,1)}, u32[]{:S(2)}, u32[]{:S(2)}) collective-permute-start(bf16[384,768]{1,0:T(8,128)(2,1)S(1)} %fusion.1.refs_8_), channel_id=1, source_target_pairs={{0,2},{1,3},{2,0},{3,1},{4,6},{5,7},{6,4},{7,5},{8,10},{9,11},{10,... | collective-permute-start | bytes 1769480 | tf_op jit(solution)/shard_map/ppermute | solution.py:650
  251.6 29.4 %collective-permute-start.51 = (bf16[2,208,768]{2,1,0:T(8,128)(2,1)S(1)}, bf16[2,208,768]{2,1,0:T(8,128)(2,1)S(1)}, u32[]{:S(2)}, u32[]{:S(2)}) collective-permute-start(bf16[2,208,768]{2,1,0:T(8,128)(2,1)S(1)} %pad_maximum_fusion), channel_id=1, source_target_pairs={{0,4},{4,0},{8,12},{12,8},{16,20},{20,16},{24,28},{28,24},{1,5},{5... | collective-permute-start | bytes 1916936 | tf_op jit(solution)/shard_map/ppermute | solution.py:650
  254.5 14.4 %collective-permute-start.47 = (bf16[2,192,768]{2,1,0:T(8,128)(2,1)S(1)}, bf16[2,192,768]{2,1,0:T(8,128)(2,1)S(1)}, u32[]{:S(2)}, u32[]{:S(2)}) collective-permute-start(bf16[2,192,768]{2,1,0:T(8,128)(2,1)S(1)} %copy-done.60), channel_id=1, source_target_pairs={{0,8},{4,12},{8,0},{12,4},{16,24},{20,28},{24,16},{28,20},{1,9},{5... | collective-permute-start | bytes 1769480 | tf_op jit(solution)/shard_map/ppermute | solution.py:650
  256.6 24.4 %collective-permute-start.45 = (bf16[2,192,768]{2,1,0:T(8,128)(2,1)S(1)}, bf16[2,192,768]{2,1,0:T(8,128)(2,1)S(1)}, u32[]{:S(2)}, u32[]{:S(2)}) collective-permute-start(bf16[2,192,768]{2,1,0:T(8,128)(2,1)S(1)} %pad_maximum_fusion.2), channel_id=1, source_target_pairs={{0,4},{4,0},{8,12},{12,8},{16,20},{20,16},{24,28},{28,24},{1,5},{5... | collective-permute-start | bytes 1769480 | tf_op jit(solution)/shard_map/ppermute | solution.py:650
  (85 other events, 1296.4 us)
where the time goes:
time: 290 us; the launch traced here: 287 us
  Pallas kernels  125 us (43%)
  waiting for transfers between devices  90.9 us (31%)
  starting transfers between devices  39 us (13%)
  local copies, waits for them, and re-layouts  18.2 us (6%)
  other arithmetic  8.95 us (3%)
  between operations  4.28 us (1%)
    pallas_call x12, Pallas kernels, call(): pl.pallas_call(kernel, out_shape=[pltpu.HBM(*o[:2]) if len(o) > 2 else ja...  125 us
    ppermute x55, waiting for transfers between devices, hop(): return lax.ppermute(x, axis, [(i, i ^ mask) for i in range(size)])  90.9 us
    ppermute x55, starting transfers between devices, hop(): return lax.ppermute(x, axis, [(i, i ^ mask) for i in range(size)])  39 us
    unnamed x124, local copies, waits for them, and re-layouts  15.4 us
  transfers between devices with their start and end apart: 55, of which 20 were waited for; matrix products, arithmetic and copies ran while one was open for 4% of the time, Pallas kernels for 41%

commit v1 on v0

v1 whole, which is shorter than its diff:
```python
from functools import partial

import jax
import jax.numpy as jnp
from jax import lax
from jax.experimental import pallas as pl
from jax.experimental.pallas import tpu as pltpu
from jax.sharding import PartitionSpec as P

F32 = jnp.float32
BF = jnp.bfloat16
HD = 64
EPS = 1e-05
VEC = 32
CH = 128
MB = 1024 * 1024
COST = 5e8

HGATE, HKEEP, OUTB, FG, FS, OUTERB, SG, SS, UGATE, INB, HEADG, QB, VB = range(13)


def dot(a, b):
    return jnp.dot(a, b, preferred_element_type=F32)


def dot_nt(a, b):
    return lax.dot_general(a, b, (((1,), (1,)), ((), ())), preferred_element_type=F32)


def dot_tn(a, b):
    return lax.dot_general(a, b, (((0,), (0,)), ((), ())), preferred_element_type=F32)


def gelu_parts(v):
    z = jnp.abs(v) * 0.7071067811865476
    e = jnp.exp(-(z * z))
    t = 1.0 / (1.0 + 0.3275911 * z)
    p = 0.5 * 1.061405429
    p = p * t - 0.5 * 1.453152027
    p = p * t + 0.5 * 1.421413741
    p = p * t - 0.5 * 0.284496736
    p = p * t + 0.5 * 0.254829592
    q = p * t * e
    return jnp.where(v >= 0.0, 1.0 - q, q), e


def fold(x):
    return jnp.sum(x.reshape(x.shape[0] // 8, 8, x.shape[1]), axis=0)


def mean(x):
    return jnp.mean(x, axis=1, keepdims=True)


def call(kernel, outs, args, specs=None, scratch=(), grid=(), prefetch=0, out_specs=None, us=1.0, limit=40, name=None):
    vmem = pl.BlockSpec(memory_space=pltpu.VMEM)
    specs = specs or [vmem] * (len(args) - prefetch)
    out_specs = out_specs or [vmem] * len(outs)
    return pl.pallas_call(
        kernel,
        out_shape=[pltpu.HBM(*o[:2]) if len(o) > 2 else jax.ShapeDtypeStruct(*o) for o in outs],
        grid_spec=pltpu.PrefetchScalarGridSpec(
            num_scalar_prefetch=prefetch, grid=grid, in_specs=specs, out_specs=out_specs, scratch_shapes=list(scratch)
        ),
        compiler_params=pltpu.CompilerParams(vmem_limit_bytes=limit * MB),
        cost_estimate=pl.CostEstimate(flops=int(us * COST), bytes_accessed=0, transcendentals=0),
        name=name,
    )(*args)


VM = pl.BlockSpec(memory_space=pltpu.VMEM)
SM = pl.BlockSpec(memory_space=pltpu.SMEM)
ANY = pl.BlockSpec(memory_space=pl.ANY)
HBM = pl.BlockSpec(memory_space=pltpu.HBM)


def prep_kernel(*refs):
    count = (len(refs) - 3) // 2
    srcs, wo, consts, pack, held, sem = refs[:count], refs[count], refs[count + 1], refs[count + 2], refs[count + 3 : -1], refs[-1]
    w = consts.shape[1]
    c = wo.shape[0]
    copies = [pltpu.make_async_copy(a, b, sem.at[i]) for i, (a, b) in enumerate(zip(srcs, held))]
    copies.append(pltpu.make_async_copy(wo, pack.at[pl.ds(0, c)], sem.at[count]))
    for copy in copies:
        copy.start()
    for copy in copies:
        copy.wait()
    ua, un, uk, ib, da, dn, dk, ob, fg, fs, ub, sg, ss, qb, vb, ha, hn, hk = held

    def line(ref):
        return ref[...].astype(F32).reshape(1, ref.shape[0])

    def gate(a, n):
        return jax.nn.sigmoid((a + n) * 1.5)

    consts[...] = jnp.zeros_like(consts)
    consts[HGATE : HGATE + 1, :] = gate(line(da), line(dn))
    for row, ref in ((HKEEP, dk), (OUTB, ob), (FG, fg), (FS, fs), (OUTERB, ub), (SG, sg), (SS, ss), (INB, ib)):
        consts[row : row + 1, :] = line(ref)
    ugate = gate(line(ua), line(un))
    consts[UGATE : UGATE + 1, :] = ugate
    consts[QB : QB + 1, :c] = line(qb)
    consts[VB : VB + 1, :c] = line(vb)
    lane = lax.broadcasted_iota(jnp.int32, (1, w), 1)
    logit = jnp.zeros((1, w), F32)
    keep = jnp.zeros((1, w), F32)
    for i in range(c // HD):
        here = (lane >= i * HD) & (lane < (i + 1) * HD)
        logit = jnp.where(here, ha[i] + hn[i], logit)
        keep = jnp.where(here, hk[i].astype(F32), keep)
    hgate = jax.nn.sigmoid(logit * 1.5)
    consts[HEADG : HEADG + 1, :] = hgate

    def halves(x):
        high = x.astype(BF).astype(F32)
        return high, x - high

    uh, ul = halves(ugate)
    hh, hl = halves(hgate)
    rows = [uh, ul, line(uk), line(ib), hh, hl, keep] + [jnp.zeros((1, w), F32)] * (VEC - 7)
    pack[c:, :] = jnp.concatenate(rows, axis=0).astype(BF)


def attend_kernel(ids, tok, wq, wk, wv, consts, seg, live, c0, c1, cfar, e_ref, inv_ref, k_ref, v_ref, q_ref, qst_ref, kt_ref, bias, ct):
    c = wq.shape[0]
    length = tok.shape[0]
    quarter = length // 4
    x = tok[...]
    q = ((dot_nt(x, wq[...]) + consts[QB : QB + 1, :c]).astype(BF).astype(F32) * HD ** (-0.5)).astype(BF)
    k = dot_nt(x, wk[...]).astype(BF)
    v = (dot_nt(x, wv[...]) + consts[VB : VB + 1, :c]).astype(BF)
    k_ref[...] = k
    v_ref[...] = v
    q_ref[...] = q
    qst = q.astype(F32).T.astype(BF)
    qst_ref[0] = qst
    kt_ref[0] = k.astype(F32).T.astype(BF)
    vt = v.astype(F32).T.astype(BF)
    seg_row = seg[0].astype(F32)
    code = jnp.where(live[0] == 1, seg_row, -1.0)
    code_col = jnp.broadcast_to(code, (128, length)).T[:, :1]
    row = lax.broadcasted_iota(jnp.int32, (length, length), 0)
    col = lax.broadcasted_iota(jnp.int32, (length, length), 1)
    bias[...] = jnp.where((code_col == seg_row) | (row == col), 0.0, -1e30)
    h = ids[0]
    inv_ref[...] = jnp.zeros_like(inv_ref)
    for i in range(c // HD):
        part = slice(i * HD, (i + 1) * HD)
        s = dot(k[:, part], qst[part, :]) + bias[...]
        top = jnp.max(s, axis=0, keepdims=True)
        e = jnp.exp(s - top)
        inv = 1.0 / jnp.sum(e, axis=0, keepdims=True)
        low = e.astype(BF)
        e_ref[0, i] = low
        inv_ref[0, i : i + 1, :] = inv
        ct[part, :] = (dot(vt[part, :], low) * inv).astype(BF)
    for r in range(4):
        piece = ct[:, pl.ds(pl.multiple_of((h ^ r) * quarter, 128), quarter)]
        if r < 2:
            (c0, c1)[r][0] = piece
        else:
            cfar[r - 2, 0] = piece


def mark(marks, value, first, second):
    lane = lax.broadcasted_iota(jnp.int32, marks.shape, 1)
    full = jnp.broadcast_to(value, marks.shape)
    high = full.astype(BF).astype(F32)
    return jnp.where(lane == first, high, jnp.where(lane == second, full - high, marks))


def unit_chunks(weights, p):
    half = weights[2].shape[1]
    chunks = []
    for r in range(2):
        chunks += [(r, weights[r], s, 256, s) for s in range(0, weights[r].shape[1], 256)]
    for r, (mine, other) in ((2, weights[2:4]), (3, weights[4:6])):
        for ref, base in ((mine, p * half), (other, (1 - p) * half)):
            for s in range(0, half, 256):
                chunks.append((r, ref, s, min(256, half - s), pl.multiple_of(base + s, 128)))
    return chunks


def start(copies):
    for copy in copies:
        copy.start()


def wait(copies):
    for copy in copies:
        copy.wait()


def load_rows(src, dst, h, sem, blocks, quarter):
    return [
        pltpu.make_async_copy(src.at[pl.ds(b * 4 * quarter + pl.multiple_of(h * quarter, quarter), quarter)], dst.at[pl.ds(b * quarter, quarter)], sem.at[b])
        for b in range(blocks)
    ]


def head_rows(vec, soft, c):
    if soft:
        return (vec[4:5, :] + vec[5:6, :])[:, :c]
    return vec[6:7, :][:, :c]


def project(pieces, packs, gated, attn, consts, soft):
    blocks, c, quarter = pieces[0].shape
    for r in range(4):
        g = head_rows(packs[r][c:, :].astype(F32), soft, c)
        for b in range(blocks):
            gated[r, b * quarter : (b + 1) * quarter, :] = (pieces[r][b].astype(F32).T * g).astype(BF)
    total = dot(gated[0], packs[0][:c, :])
    for r in range(1, 4):
        total = total + dot(gated[r], packs[r][:c, :])
    attn[...] = total + consts[OUTB : OUTB + 1, :]


def first_kernel(soft, ids, c0, c1, xr, cr, s0, s1, s2, s3, tok_any, consts, first_low, normed, *refs):
    if soft:
        inv, attn, gated, tok, tsem = refs
    else:
        tok, tsem, attn, gated = refs
    blocks, c, quarter = c0.shape
    loads = load_rows(tok_any, tok, ids[0], tsem, blocks, quarter)
    start(loads)
    project([c0, c1, xr.at[0], cr.at[1]], [s0, s1, s2, s3], gated, attn, consts, soft)
    wait(loads)
    gate = HGATE if soft else HKEEP

    @pl.loop(0, tok.shape[0] // CH)
    def _(i):
        rows = pl.ds(pl.multiple_of(i * CH, CH), CH)
        x = tok[rows, :].astype(F32) + consts[gate : gate + 1, :] * attn[rows, :]
        x = x - mean(x)
        iv = lax.rsqrt(mean(x * x) + EPS)
        n = x * iv
        normed[rows, :] = n
        if soft:
            inv[rows, :] = jnp.broadcast_to(iv, (CH, 128))
        first_low[rows, :] = (n * consts[FG : FG + 1, :] + consts[FS : FS + 1, :]).astype(BF)


def ffn_inner(first, wins, packs, p, hidden, soft, udact=None):
    c = packs[0].shape[0] - VEC
    for r, ref, s, n, unit in unit_chunks(wins, p):
        at = pl.ds(unit, n)
        vec = packs[r][c : c + 16, at].astype(F32)
        z = dot(first[...], ref[:, s : s + n]) + vec[3:4, :]
        phi, e = gelu_parts(z)
        if soft:
            g = vec[0:1, :] + vec[1:2, :]
            udact[r, :, at] = (g * (phi + z * e * 0.3989422804014327)).astype(BF)
        else:
            g = vec[2:3, :]
        hidden[r, :, at] = (g * (z * phi)).astype(BF)


def ffn_outer(hidden, outers, ffn, consts):
    half = outers[2].shape[0]
    total = dot(hidden[0], outers[0][...]) + dot(hidden[1], outers[1][...])
    for r, (a, b) in ((2, outers[2:4]), (3, outers[4:6])):
        total = total + dot(hidden[r, :, :half], a[...]) + dot(hidden[r, :, half:], b[...])
    ffn[...] = total + consts[OUTERB : OUTERB + 1, :]


def row_mask(live, h, b, quarter, at):
    count = jnp.sum(live[b : b + 1, :].astype(F32))
    place = (h * quarter + at).astype(F32) + lax.broadcasted_iota(jnp.int32, (CH, 1), 0).astype(F32)
    return jnp.where(place < count, 1.0, 0.0)


def inner_kernel(soft, ids, first_low, *refs):
    ffn_inner(first_low, refs[:6], refs[6:10], ids[1], refs[10], soft, refs[11] if soft else None)


def second_kernel(ids, hidden, normed, *refs):
    wsrc, teach_any, live, consts, student, grad_two, gffn, vecs_out, teach, ffn, acc, tsem = refs[:6], *refs[6:]
    blocks, length = live.shape
    quarter = length // 4
    h = ids[0]
    rowload = load_rows(teach_any, teach, h, tsem, blocks, quarter)
    start(rowload)
    ffn_outer(hidden, wsrc, ffn, consts)
    wait(rowload)
    acc[...] = jnp.zeros_like(acc)
    for b in range(blocks):

        @pl.loop(0, quarter // CH)
        def _(i):
            rows = pl.ds(pl.multiple_of(b * quarter + i * CH, CH), CH)
            f = ffn[rows, :]
            hg = consts[HGATE : HGATE + 1, :]
            x = normed[rows, :] * consts[FG : FG + 1, :] + consts[FS : FS + 1, :] + hg * f
            x = x - mean(x)
            iv = lax.rsqrt(mean(x * x) + EPS)
            n = x * iv
            out = n * consts[SG : SG + 1, :] + consts[SS : SS + 1, :]
            student[rows, :] = out.astype(BF)
            err = (out - teach[rows, :].astype(F32)) * row_mask(live, h, b, quarter, i * CH)
            acc[0] += fold(err * n)
            acc[1] += fold(err)
            acc[4] += fold(err * err)
            e = err * consts[SG : SG + 1, :]
            g = iv * (e - mean(e) - n * mean(e * n))
            grad_two[rows, :] = g
            gf = hg * g
            acc[2] += fold(gf)
            acc[3] += fold(g * f)
            gffn[rows, :] = gf.astype(BF)

    vecs_out[...] = jnp.zeros_like(vecs_out)
    for j in range(5):
        vecs_out[j : j + 1, :] = jnp.sum(acc[j], axis=0, keepdims=True)


def hard_kernel(ids, hidden, normed, *refs):
    wsrc, teach_any, live, consts, pruned, error, teach, ffn, acc, tsem = refs[:6], *refs[6:]
    blocks, length = live.shape
    quarter = length // 4
    h = ids[0]
    rowload = load_rows(teach_any, teach, h, tsem, blocks, quarter)
    start(rowload)
    ffn_outer(hidden, wsrc, ffn, consts)
    wait(rowload)
    acc[...] = jnp.zeros_like(acc)
    for b in range(blocks):

        @pl.loop(0, quarter // CH)
        def _(i):
            rows = pl.ds(pl.multiple_of(b * quarter + i * CH, CH), CH)
            x = normed[rows, :] * consts[FG : FG + 1, :] + consts[FS : FS + 1, :] + consts[HKEEP : HKEEP + 1, :] * ffn[rows, :]
            x = x - mean(x)
            n = x * lax.rsqrt(mean(x * x) + EPS)
            out = n * consts[SG : SG + 1, :] + consts[SS : SS + 1, :]
            pruned[rows, :] = out.astype(BF)
            err = (out - teach[rows, :].astype(F32)) * row_mask(live, h, b, quarter, i * CH)
            acc[...] += fold(err * err)

    error[...] = jnp.broadcast_to(jnp.sum(acc[...]), error.shape)


def back_kernel(ids, gffn, udact, *refs):
    isrc, osrc, packs = refs[:6], refs[6:12], refs[12:16]
    grad_two, normed, inv, attn, gated, v2, live, consts, g0, g1, gfar, dkeep, dsend, grad_one, gi, back, ga, acc = refs[16:]
    c = packs[0].shape[0] - VEC
    w = gi.shape[2]
    half = w // 2
    blocks, _, quarter = g0.shape
    for r, (a, b) in ((0, osrc[:1] * 2), (1, osrc[1:2] * 2), (2, osrc[2:4]), (3, osrc[4:6])):
        for s in (0, 256, 512) if r < 2 else (0, 256, half, half + 256):
            n = 256 if r < 2 or s % half == 0 else half - 256
            ref, row = (a, s) if r < 2 or s < half else (b, s - half)
            at = slice(s, s + n)
            gi[r, :, at] = (dot_nt(gffn[...], ref[row : row + n, :]) * udact[r, :, at].astype(F32)).astype(BF)
    total = dot_nt(gi[0], isrc[0][...]) + dot_nt(gi[1], isrc[1][...])
    for r, (x, y) in ((2, isrc[2:4]), (3, isrc[4:6])):
        for ref, q in ((x, ids[1]), (y, 1 - ids[1])):
            total = total + dot_nt(gi[r, :, pl.ds(pl.multiple_of(q * half, 128), half)], ref[...])
    back[...] = total
    acc[...] = jnp.zeros_like(acc)

    @pl.loop(0, back.shape[0] // CH)
    def _(i):
        rows = pl.ds(pl.multiple_of(i * CH, CH), CH)
        n = normed[rows, :]
        gf = grad_two[rows, :] + back[rows, :]
        acc[0] += fold(gf * n)
        acc[1] += fold(gf)
        e = gf * consts[FG : FG + 1, :]
        g = inv[rows, :1] * (e - mean(e) - n * mean(e * n))
        grad_one[rows, :] = g
        gat = consts[HGATE : HGATE + 1, :] * g
        acc[2] += fold(gat)
        acc[3] += fold(g * attn[rows, :])
        ga[rows, :] = gat.astype(BF)

    d = back.shape[1]
    v3 = [jnp.sum(acc[j], axis=0, keepdims=True) for j in range(4)]
    count = jnp.zeros((), F32)
    for j in range(blocks):
        real = jnp.sum(live[j : j + 1, :].astype(F32))
        count += jnp.clip(real - (ids[0] * quarter).astype(F32), 0.0, float(quarter))
    marks = mark(jnp.zeros((1, d), F32), jnp.sum(v2[4:5, :]), ids[3], ids[3] + ids[4])
    marks = mark(marks, count, ids[3] + 2 * ids[4], ids[3] + 3 * ids[4])
    lines = jnp.concatenate([v2[0:3, :], *v3[:3], v2[3:4, :] + v3[3], marks, jnp.zeros((8, d), F32)], axis=0).astype(BF)
    for r in range(4):
        gg = dot_nt(ga[...], packs[r][:c, :]) * head_rows(packs[r][c:, :].astype(F32), True, c)
        for b in range(blocks):
            piece = gg[b * quarter : (b + 1) * quarter, :].T.astype(BF)
            if r == 0:
                g0[b] = piece
            elif r == 1:
                g1[b] = piece
            else:
                gfar[r - 2, b] = piece
        part = dsend if r % 2 else dkeep
        part[r // 2, :c, :] = dot_tn(gated[r], ga[...]).astype(BF)
        part[r // 2, c:, :] = lines


def units_kernel(f0, f1, fx, fd, consts, win, hidden, udact):
    for r, f in enumerate((f0, f1, fx, fd)):
        rows = slice(r * f0.shape[0], (r + 1) * f0.shape[0])
        for s in range(0, win.shape[1], 256):
            at = slice(s, s + 256)
            z = dot(f[...], win[:, at]) + consts[INB : INB + 1, at]
            phi, e = gelu_parts(z)
            g = consts[UGATE : UGATE + 1, at]
            udact[rows, at] = (g * (phi + z * e * 0.3989422804014327)).astype(BF)
            hidden[rows, at] = (g * (z * phi)).astype(BF)


def slots(src, keep, send, first_bit, second_bit):
    n = keep.shape[1]
    for a in range(2):
        for b in range(2):
            j = (first_bit ^ a) * 2 + (second_bit ^ b)
            rows = src[pl.ds(pl.multiple_of(j * n, 16), n), :].astype(BF)
            if a == 0:
                keep[b] = rows
            else:
                send[b] = rows


def rows_dot(lefts, rights):
    total = dot_tn(lefts[0], rights[0])
    for left, right in zip(lefts[1:], rights[1:]):
        total = total + dot_tn(left, right)
    return total


def outer_grad_kernel(ids, g0, g1, gx, gd, hidden, akeep, asend, big):
    n = g0.shape[0]
    big[...] = rows_dot([hidden[r * n : (r + 1) * n, :] for r in range(4)], [g0[...], g1[...], gx[...], gd[...]])
    slots(big, akeep, asend, ids[1], ids[2])


def inner_grad_kernel(ids, f0, f1, fx, fd, g0, g1, gx, gd, outer, hidden, udact, bkeep, bsend, vecs_out, gi, big, acc):
    n = f0.shape[0]
    gffns = (g0, g1, gx, gd)
    acc[...] = jnp.zeros_like(acc)
    for r in range(4):
        rows = slice(r * n, (r + 1) * n)
        for s in range(0, outer.shape[0], 256):
            at = slice(s, s + 256)
            gh = dot_nt(gffns[r][...], outer[at, :])
            g = (gh * udact[rows, at].astype(F32)).astype(BF)
            gi[rows, at] = g
            acc[0, :, at] += fold(gh * hidden[rows, at].astype(F32))
            acc[1, :, at] += fold(g.astype(F32))
    big[...] = rows_dot([f0[...], f1[...], fx[...], fd[...]], [gi[r * n : (r + 1) * n, :] for r in range(4)])
    slots(big, bkeep, bsend, ids[2], ids[1])
    vecs_out[...] = jnp.zeros_like(vecs_out)
    for j in range(2):
        vecs_out[j : j + 1, :] = jnp.sum(acc[j], axis=0, keepdims=True)


def attend_back_kernel(ids, g0, g1, gxr, gcr, e_ref, inv_ref, k_ref, v_ref, q_ref, kt, tok, wq, wk, wv, keep, send, wacc, cacc, dct, nat, low):
    b = pl.program_id(0)
    h = ids[0]
    c, d = wq.shape
    length = tok.shape[0]
    quarter = length // 4
    heads = c // HD

    @pl.when(b == 0)
    def _():
        wacc[...] = jnp.zeros_like(wacc)
        cacc[...] = jnp.zeros_like(cacc)

    for r, piece in enumerate((g0[0], g1[0], gxr[0, 0], gcr[1, 0])):
        dct[:, pl.ds(pl.multiple_of((h ^ r) * quarter, 128), quarter)] = piece
    dq, dk, dv = [], [], []
    for i in range(heads):
        part = slice(i * HD, (i + 1) * HD)
        inv = inv_ref[0, i : i + 1, :]
        dcp = dct[part, :].astype(F32) * inv
        dp = dot(v_ref[:, part], dcp.astype(BF))
        e = e_ref[0, i].astype(F32)
        w = e * dp
        delta = jnp.sum(w, axis=0, keepdims=True)
        ds = (w - e * (inv * delta)).astype(BF)
        dq.append(dot(kt[0, part, :], ds) * HD ** (-0.5))
        dk.append(dot(ds, q_ref[:, part]).astype(BF))
        dv.append(dot(e_ref[0, i], dcp.T.astype(BF)).astype(BF))
        cacc[8:9, i * 128 : (i + 1) * 128] += jnp.broadcast_to(jnp.sum(delta, axis=1, keepdims=True), (1, 128))
    dq = jnp.concatenate(dq, axis=0).T.astype(BF)
    nat[...] = jnp.concatenate([dq, *dk, *dv], axis=1)
    wacc[...] += dot_tn(nat[...], tok[...])
    cacc[0:8, : 3 * c] += fold(nat[...].astype(F32))
    part = dot(nat[:, :c], wq[...]) + dot(nat[:, c : 2 * c], wk[...]) + dot(nat[:, 2 * c :], wv[...])
    low[...] = part.astype(BF)
    for r in range(4):
        rows = low[pl.ds(pl.multiple_of((h ^ r) * quarter, quarter), quarter), :]
        at = pl.ds(pl.multiple_of(b * quarter, quarter), quarter)
        if r % 2 == 0:
            keep[r // 2, at, :] = rows
        else:
            send[r // 2, at, :] = rows


def turn_kernel(ids, wacc, cacc, dmine, drecv, vg, akeep, agot, bkeep, bgot, amine, agive, bmine, bgive, ckeep, csend, big):
    n = wacc.shape[0]
    c = n // 3
    big[n + c + 32 :, :] = jnp.zeros((big.shape[0] - n - c - 32, big.shape[1]), F32)
    big[:n, :] = wacc[...]
    big[n : n + c + 16, :] = dmine[...].astype(F32) + drecv[...].astype(F32)
    n = n + c + 16
    big[n : n + 16, :] = jnp.zeros((16, big.shape[1]), F32)
    col = jnp.sum(cacc[0:8, :], axis=0, keepdims=True)
    big[n : n + 1, :c] = col[:, :c]
    big[n + 1 : n + 2, :c] = col[:, 2 * c : 3 * c]
    big[n + 2 : n + 3, : c * 2] = cacc[8:9, : c * 2]
    big[n + 8 : n + 16, :] = vg[...]
    slots(big, ckeep, csend, ids[1], ids[2])
    for keep, got, mine, give in ((akeep, agot, amine, agive), (bkeep, bgot, bmine, bgive)):
        mine[...] = (keep[0].astype(F32) + got[0].astype(F32)).astype(BF)
        give[...] = (keep[1].astype(F32) + got[1].astype(F32)).astype(BF)


def third_kernel(ids, mine, got, error, error_1, out):
    n, d = mine.shape
    out[:n, :] = (mine[...].astype(F32) + got[...].astype(F32)).astype(BF)
    total = error[0:1, :1] + error_1[0:1, :1]
    place = ids[3] // 4
    zero = jnp.zeros((1, d), F32)
    rows = [mark(zero, total, place, -1), mark(zero, total, -1, place), jnp.zeros((14, d), F32)]
    out[n:, :] = jnp.concatenate(rows, axis=0).astype(BF)


def pair_kernel(amine, aother, bmine, bother, apair, bpair):
    apair[0], apair[1] = amine[...], aother[...]
    bpair[0], bpair[1] = bmine[...], bother[...]


def last_kernel(mine, other, out):
    n = mine.shape[0] - 16
    out[:n, :] = mine[:n, :]
    out[n : 2 * n, :] = other[:n, :]
    out[2 * n :, :] = (mine[n:, :].astype(F32) + other[n:, :].astype(F32)).astype(BF)


def weights_kernel(ids, ak, ao, aq, bk, bo, bq, uw, iw):
    for dst, k, o, q, first_bit, second_bit in ((uw, ak, ao, aq, ids[1], ids[2]), (iw, bk, bo, bq, ids[2], ids[1])):
        n = k.shape[0]
        for a in range(2):
            for b in range(2):
                j = (first_bit ^ a) * 2 + (second_bit ^ b)
                src = (k if b == 0 else o)[...] if a == 0 else q[b]
                dst[pl.ds(pl.multiple_of(j * n, 16), n), :] = src.astype(F32)


def final_kernel(ids, consts, cpair, cq, qw, kw, vw, ow, qb, vb, ob, fg, fs, ib, ub, sg, ss, ha, ua, da, me, pe, big):
    d = consts.shape[1]
    c = qw.shape[0]

    n = big.shape[0] // 4
    for a, src in enumerate((cpair, cq)):
        for b in range(2):
            j = (ids[1] ^ a) * 2 + (ids[2] ^ b)
            big[pl.ds(pl.multiple_of(j * n, 16), n), :] = src[b * n : (b + 1) * n, :].astype(F32)
    qw[...] = big[:c, :]
    kw[...] = big[c : 2 * c, :]
    vw[...] = big[2 * c : 3 * c, :]
    n = 3 * c
    ow[...] = big[n : n + c, :]
    n = n + c
    vec = big[n : n + 16, :]
    own = big[n + 16 : n + 32, :]
    for ref, row in ((sg, 0), (ss, 1), (ub, 2), (fg, 3), (fs, 4), (ob, 5)):
        ref[...] = vec[row : row + 1, :].reshape(d)
    hg = consts[HGATE : HGATE + 1, :]
    da[...] = (1.5 * vec[6:7, :] * hg * (1.0 - hg)).reshape(d)
    ug = consts[UGATE : UGATE + 1, :]
    ua[...] = (1.5 * own[8:9, :] * (1.0 - ug)).reshape(d)
    ib[...] = own[9:10, :].reshape(d)
    qb[...] = own[0:1, :c].reshape(c)
    vb[...] = own[1:2, :c].reshape(c)
    gate = consts[HEADG : HEADG + 1, :]
    for i in range(c // HD):
        g = gate[0, i * HD]
        ha[i] = 1.5 * own[2, i * 128] * (1.0 - g)
    lane = lax.broadcasted_iota(jnp.int32, (1, d), 1)
    nd = ids[4]
    m = cpair.shape[0] - 16
    hard_sum = jnp.sum(cpair[m:, :].astype(F32) + cq[m:, :].astype(F32))
    marks = vec[7:8, :]

    def between(lo, hi):
        return jnp.sum(jnp.where((lane >= lo * nd) & (lane < hi * nd), marks, 0.0))

    live = jnp.maximum(between(2, 4), 1.0)
    me[0] = 0.5 * between(0, 2) / live
    pe[0] = 0.5 * hard_sum / live


def spread_kernel(h_ref, *refs):
    count = (len(refs) - 1) // 5
    sem = refs[-1]
    copies = []
    for a in range(count):
        out = refs[4 * count + a]
        for r in range(4):
            src = refs[4 * a + r]
            blocks = out.shape[0]
            quarter = out.shape[1] // 4
            for b in range(blocks):
                at = pl.ds(pl.multiple_of((h_ref[0] ^ r) * quarter, quarter), quarter)
                copies.append(pltpu.make_async_copy(src.at[pl.ds(b * quarter, quarter)], out.at[b, at], sem.at[len(copies)]))
    for copy in copies:
        copy.start()
    for copy in copies:
        copy.wait()


def shards(
    tokens, teacher, segments, present, query_weight, query_bias, key_weight, value_weight, value_bias, output_weight, output_bias,
    first_gain, first_shift, inner_weight, inner_bias, outer_weight, outer_bias, second_gain, second_shift, head_alpha, head_noise,
    unit_alpha, unit_noise, hidden_alpha, hidden_noise, head_keep, unit_keep, hidden_keep, n_dp,
):
    rows, d = tokens.shape
    blocks, length = segments.shape
    heads = head_alpha.shape[0]
    c = heads * HD
    w = unit_alpha.shape[0]
    quarter = length // 4
    t = blocks * quarter
    n_head = 4
    h = lax.axis_index("head").astype(jnp.int32)
    i_dp = lax.axis_index("dp").astype(jnp.int32)
    bit0, bit1 = i_dp & 1, (i_dp >> 1) & 1
    ids = jnp.stack([h, bit0, bit1, i_dp * n_head + h, jnp.int32(n_dp * n_head)])

    def hop(x, mask, axis="head"):
        size = n_head if axis == "head" else n_dp
        return lax.ppermute(x, axis, [(i, i ^ mask) for i in range(size)])

    def in_hbm(x):
        return pltpu.with_memory_space_constraint(x, pltpu.HBM)

    def after(x, *done):
        return lax.optimization_barrier((x, *done))[0]

    def add(x, y):
        return (x.astype(F32) + y.astype(F32)).astype(BF)

    half = d // 2
    inner_half = lax.dynamic_slice_in_dim(inner_weight, bit0 * half, half, axis=1)
    inner_x = hop(inner_half, 2)

    small = (unit_alpha, unit_noise, unit_keep, inner_bias, hidden_alpha, hidden_noise, hidden_keep, output_bias, first_gain, first_shift,
             outer_bias, second_gain, second_shift, query_bias, value_bias, head_alpha, head_noise, head_keep)
    consts, pack = call(
        prep_kernel,
        [((16, d), F32), ((c + VEC, w), BF)],
        tuple(in_hbm(a) for a in (*small, after(output_weight, inner_half))),
        specs=[ANY] * 19, scratch=[(pltpu.VMEM if a.shape[0] > heads else pltpu.SMEM)(a.shape, a.dtype) for a in small] + [pltpu.SemaphoreType.DMA((19,))], us=2, limit=8, name="prep",
    )
    pack_2 = hop(pack, 2)
    pack_1 = hop(pack, 1)
    inner_1, outer_1 = hop(inner_weight, 1), hop(outer_weight, 1)

    seg3 = segments.reshape(blocks, 1, length)
    live3 = present.reshape(blocks, 1, length)
    full = lambda *s: pl.BlockSpec(s, lambda b, *_: (0,) * len(s))
    c0, c1, cfar, e, inv_l, k, v, q, qst, kt = call(
        attend_kernel,
        [((blocks, c, quarter), BF), ((blocks, c, quarter), BF), ((2, blocks, c, quarter), BF), ((blocks, heads, length, length), BF, HBM),
         ((blocks, 8, length), F32), ((rows, c), BF, HBM), ((rows, c), BF, HBM), ((rows, c), BF, HBM), ((blocks, c, length), BF, HBM), ((blocks, c, length), BF, HBM)],
        (ids, in_hbm(tokens), *(in_hbm(a.T) for a in (query_weight, key_weight, value_weight)), consts, seg3, live3),
        prefetch=1, grid=(blocks,),
        specs=[pl.BlockSpec((length, d), lambda b, *_: (b, 0)), full(c, d), full(c, d), full(c, d), full(16, d),
               pl.BlockSpec((1, 1, length), lambda b, *_: (b, 0, 0)), pl.BlockSpec((1, 1, length), lambda b, *_: (b, 0, 0))],
        out_specs=[pl.BlockSpec((1, c, quarter), lambda b, *_: (b, 0, 0)), pl.BlockSpec((1, c, quarter), lambda b, *_: (b, 0, 0)),
                   pl.BlockSpec((2, 1, c, quarter), lambda b, *_: (0, b, 0, 0)), pl.BlockSpec((1, heads, length, length), lambda b, *_: (b, 0, 0, 0)),
                   pl.BlockSpec((1, 8, length), lambda b, *_: (b, 0, 0)), pl.BlockSpec((length, c), lambda b, *_: (b, 0)),
                   pl.BlockSpec((length, c), lambda b, *_: (b, 0)), pl.BlockSpec((length, c), lambda b, *_: (b, 0)),
                   pl.BlockSpec((1, c, length), lambda b, *_: (b, 0, 0)), pl.BlockSpec((1, c, length), lambda b, *_: (b, 0, 0))],
        scratch=[pltpu.VMEM((length, length), F32), pltpu.VMEM((c, length), BF)], us=9, limit=24, name="attend",
    )
    cx = hop(cfar, 2)
    c1r = hop(c1, 1)
    outer_a = hop(after(outer_weight, c1r)[:half], 2)
    inner_x, pack_2 = after(inner_x, c0), after(pack_2, c0)
    inner_y, inner_3x = hop(inner_x, 1, "dp"), hop(inner_x, 1)
    packs = (pack, pack_1, pack_2, hop(pack_2, 1))
    pieces = (c0, c1r, cx, hop(cx, 1))

    def first(soft, pieces):
        scratch = [pltpu.VMEM((t, d), BF), pltpu.SemaphoreType.DMA((blocks,))]
        more = [((t, 128), F32), ((t, d), F32), ((4, t, c), BF)]
        return call(
            partial(first_kernel, soft),
            [((t, d), BF), ((t, d), F32)] + (more if soft else []),
            (ids, *pieces, *packs, tokens, consts),
            prefetch=1, specs=[VM] * 8 + [ANY, VM],
            scratch=scratch if soft else scratch + [pltpu.VMEM((t, d), F32), pltpu.VMEM((4, t, c), BF)], us=4, limit=12, name="first" if soft else "hard_first",
        )

    def inner(soft, low):
        return call(
            partial(inner_kernel, soft), [((4, t, w), BF)] * (2 if soft else 1), (ids, low, *inners, *packs),
            prefetch=1, us=8, limit=16, name="inner" if soft else "hard_inner",
        )

    first_low, normed, inv1, attn, gated = first(True, pieces)
    first_2 = hop(first_low, 2)
    first_1 = hop(first_low, 1)
    inner_y = after(inner_y, first_low)
    inners = (inner_weight, inner_1, inner_x, inner_y, inner_3x, hop(inner_y, 1))
    hard_low, hard_normed = first(False, (after(c0, first_low), *pieces[1:]))
    outer_a = after(outer_a, hard_low)
    outer_3a = hop(outer_a, 1)
    outer_b = hop(after(outer_weight, outer_a)[half:], 2)
    hidden, udact = inner(True, after(first_low, hard_low))
    (hard_hidden,) = inner(False, after(hard_low, hidden))
    outer_b = after(outer_b, hard_hidden)
    outers = (outer_weight, outer_1, outer_a, outer_b, outer_3a, hop(outer_b, 1))

    student_rows, grad_two, gffn, v2 = call(
        second_kernel,
        [((t, d), BF), ((t, d), F32), ((t, d), BF), ((8, d), F32)],
        (ids, hidden, normed, *outers, teacher, present, consts),
        prefetch=1, specs=[VM] * 8 + [ANY] + [VM] * 2,
        scratch=[pltpu.VMEM((t, d), BF), pltpu.VMEM((t, d), F32), pltpu.VMEM((5, 8, d), F32), pltpu.SemaphoreType.DMA((blocks,))], us=6, limit=16, name="second",
    )
    gffn_2 = hop(gffn, 2)
    gffn_1 = hop(gffn, 1)

    g0, g1, gfar, dkeep, dsend, grad_one = call(
        back_kernel,
        [((blocks, c, quarter), BF), ((blocks, c, quarter), BF), ((2, blocks, c, quarter), BF), ((2, c + 16, d), BF), ((2, c + 16, d), BF), ((t, d), F32)],
        (ids, gffn, udact, *inners, *outers, *packs, grad_two, normed, inv1, attn, gated, v2, present, consts),
        prefetch=1,
        scratch=[pltpu.VMEM((4, t, w), BF), pltpu.VMEM((t, d), F32), pltpu.VMEM((t, d), BF), pltpu.VMEM((4, 8, d), F32)], us=13, limit=24, name="back",
    )
    gx = hop(gfar, 2)
    g1r = hop(g1, 1)
    d_got = hop(dsend, 1)
    gffn_2, first_2 = after(gffn_2, g0), after(first_2, g0)
    firsts = (first_low, first_1, first_2, hop(first_2, 1))
    gffns = (gffn, gffn_1, gffn_2, hop(gffn_2, 1))

    hidden_own, udact_own = call(
        units_kernel, [((rows, w), BF), ((rows, w), BF)], (after(firsts[0], g0), *firsts[1:], consts, inner_weight), us=6, limit=16, name="units"
    )
    gx, d_got = after(gx, hidden_own), after(d_got, hidden_own)
    gpieces = (g0, g1r, gx, hop(gx, 1))
    d_mine, d_give = add(dkeep[0], d_got[0]), add(dkeep[1], d_got[1])
    d_recv = hop(d_give, 2)

    akeep, asend = call(
        outer_grad_kernel, [((2, w // 4, d), BF)] * 2, (ids, *gffns, hidden_own), prefetch=1, scratch=[pltpu.VMEM((w, d), F32)], us=3, limit=16, name="outer_grad"
    )
    a_got = hop(asend, 1, "dp")
    bkeep, bsend, vg = call(
        inner_grad_kernel,
        [((2, d // 4, w), BF)] * 2 + [((8, w), F32)],
        (ids, *firsts, after(gffns[0], akeep), *gffns[1:], outer_weight, hidden_own, udact_own),
        prefetch=1, scratch=[pltpu.VMEM((rows, w), BF), pltpu.VMEM((w, d), F32), pltpu.VMEM((2, 8, w), F32)], us=6, limit=24, name="inner_grad",
    )
    gpieces = (after(g0, bkeep, d_recv), *gpieces[1:])
    b_got = hop(bsend, 2, "dp")
    student_rows = after(student_rows, akeep)
    student_2 = hop(student_rows, 2)
    student_1 = hop(student_rows, 1)

    pick = lambda *s: pl.BlockSpec((1,) + s, lambda b, *_: (b,) + (0,) * len(s))
    n_c = 4 * ((3 * c + c + 32 + 63) // 64) * 16
    keep, send, wacc, cacc = call(
        attend_back_kernel,
        [((2, t, d), BF), ((2, t, d), BF), ((3 * c, d), F32), ((16, d), F32)],
        (ids, *gpieces, *(in_hbm(a) for a in (e, inv_l, k, v, q, kt, tokens)), *(in_hbm(a.T) for a in (query_weight, key_weight, value_weight))),
        prefetch=1, grid=(blocks,),
        specs=[pick(c, quarter), pick(c, quarter), pl.BlockSpec((2, 1, c, quarter), lambda b, *_: (0, b, 0, 0)),
               pl.BlockSpec((2, 1, c, quarter), lambda b, *_: (0, b, 0, 0)), pick(heads, length, length), pick(8, length),
               pl.BlockSpec((length, c), lambda b, *_: (b, 0)), pl.BlockSpec((length, c), lambda b, *_: (b, 0)), pl.BlockSpec((length, c), lambda b, *_: (b, 0)), pick(c, length),
               pl.BlockSpec((length, d), lambda b, *_: (b, 0)), full(c, d), full(c, d), full(c, d)],
        out_specs=[full(2, t, d), full(2, t, d), full(3 * c, d), full(16, d)],
        scratch=[pltpu.VMEM((c, length), BF), pltpu.VMEM((length, 3 * c), BF), pltpu.VMEM((length, d), BF)],
        us=15, limit=32, name="attend_back",
    )
    a_got, b_got, student_2 = after(a_got, keep), after(b_got, keep), after(student_2, keep)
    part = (w // 4, d)
    a_mine, a_give, b_mine, b_give, ckeep, csend = call(
        turn_kernel,
        [(part, BF)] * 4 + [((2, n_c // 4, d), BF)] * 2,
        (ids, wacc, cacc, d_mine, d_recv, vg, akeep, after(a_got, student_2), bkeep, b_got),
        prefetch=1, specs=[VM] * 9, scratch=[pltpu.VMEM((n_c, d), F32)], us=0.1, limit=16, name="turn",
    )
    got = hop(after(send, a_mine), 1)
    c_got = hop(csend, 1, "dp")
    a_got, b_got = hop(a_give, 2, "dp"), hop(b_give, 1, "dp")
    give = add(keep[1], got[1])
    mine = add(keep[0], got[0])
    recv = hop(give, 2)
    students = (student_rows, student_1, student_2, hop(after(student_2, give), 1))
    a_mine, b_mine = add(a_mine, after(a_got, give)), add(b_mine, after(b_got, give))

    def across(x):
        mask = 4
        while mask < n_dp:
            got = hop(x, mask, "dp")
            x = (x, got) if mask * 2 == n_dp else add(x, got)
            mask *= 2
        return x

    a_mine, b_mine = across(a_mine), across(b_mine)
    pruned_rows, error = call(
        hard_kernel,
        [((t, d), BF), ((8, 128), F32)],
        (ids, after(hard_hidden, a_mine[0], b_mine[0], give), hard_normed, *outers, teacher, present, consts),
        prefetch=1, specs=[VM] * 8 + [ANY] + [VM] * 2,
        scratch=[pltpu.VMEM((t, d), BF), pltpu.VMEM((t, d), F32), pltpu.VMEM((8, d), F32), pltpu.SemaphoreType.DMA((blocks,))], us=6, limit=16, name="hard",
    )
    error = error + hop(error, 2)
    error_1 = hop(error, 1)
    recv, c_got = after(recv, pruned_rows), after(c_got, pruned_rows)
    c_mine, c_give = add(ckeep[0], c_got[0]), add(ckeep[1], c_got[1])
    c_got = hop(c_give, 2, "dp")
    grad_rows = (grad_one + (mine.astype(F32) + recv.astype(F32))).astype(BF)
    grad_2 = hop(grad_rows, 2)
    grad_1 = hop(grad_rows, 1)
    pruned_2 = hop(after(pruned_rows, grad_rows), 2)
    pruned_1 = hop(pruned_rows, 1)
    a_mine, b_mine = (add(x, after(got, c_give, grad_rows)) for x, got in (a_mine, b_mine))
    a_other, b_other = hop(a_mine, 2, "dp"), hop(b_mine, 1, "dp")
    (c_mine,) = call(
        third_kernel, [((n_c // 4 + 16, d), BF)], (ids, c_mine, after(c_got, a_mine, b_mine), error, error_1), prefetch=1, us=0.1, limit=8, name="third"
    )
    c_mine = across(c_mine)
    a_pair, b_pair = call(pair_kernel, [((2,) + part, BF)] * 2, (a_mine, after(a_other, c_mine[0]), b_mine, b_other), us=0.1, limit=8, name="pair")
    a_parts = (a_mine, a_other, hop(a_pair, 1, "dp"))
    b_parts = (b_mine, b_other, hop(b_pair, 2, "dp"))
    grad_2 = after(grad_2, a_pair)
    grads = (grad_rows, grad_1, grad_2, hop(grad_2, 1))
    c_mine = add(c_mine[0], after(c_mine[1], a_pair))
    c_other = hop(c_mine, 2, "dp")
    pruned_2 = after(pruned_2, c_mine)
    pruneds = (pruned_rows, pruned_1, pruned_2, hop(pruned_2, 1))

    uw, iw = call(weights_kernel, [((w, d), F32), ((d, w), F32)], (ids, after(a_parts[0], grad_2, pruned_2), *a_parts[1:], *b_parts), prefetch=1, us=1, limit=16, name="weights")
    (c_pair,) = call(last_kernel, [((n_c // 2 + 16, d), BF)], (c_mine, after(c_other, uw)), us=0.1, limit=8, name="last")
    c_last = hop(c_pair, 1, "dp")
    outs = call(
        spread_kernel,
        [((blocks, length, d), BF)] * 3,
        (ids, after(students[0], c_pair), *students[1:], *pruneds, *grads),
        prefetch=1, specs=[VM] * 12, out_specs=[ANY] * 3, scratch=[pltpu.SemaphoreType.DMA((12 * blocks,))], us=1, limit=16, name="spread",
    )
    student, pruned, tokens_grad = (o.reshape(rows, d) for o in outs)
    qw, kw, vw, ow, qb, vb, ob, fg, fs, ib, ub, sg, ss, ha, ua, da, me, pe = call(
        final_kernel,
        [((c, d), F32), ((c, d), F32), ((c, d), F32), ((c, d), F32), ((c,), F32), ((c,), F32), ((d,), F32), ((d,), F32), ((d,), F32),
         ((w,), F32), ((d,), F32), ((d,), F32), ((d,), F32), ((heads,), F32), ((w,), F32), ((d,), F32), ((1,), F32), ((1,), F32)],
        (ids, consts, c_pair, after(c_last, outs[0])),
        prefetch=1, specs=[VM] * 3, out_specs=[VM] * 13 + [SM] + [VM] * 2 + [SM] * 2,
        scratch=[pltpu.VMEM((n_c, d), F32)], us=0.1, limit=16, name="final",
    )
    return (
        student, pruned, tokens_grad, qw.T, qb, kw.T, vw.T, vb, ow, ob, fg, fs, iw, ib, uw, ub, sg, ss, ha, ua, da, me.reshape(()), pe.reshape(()),
    )


def solution(mesh):
    row, col, lead, unit, none = P("dp", None), P(None, "head"), P("head", None), P("head"), P()
    return jax.shard_map(
        partial(shards, n_dp=mesh.shape["dp"]),
        mesh=mesh,
        in_specs=(row, row, row, row, col, unit, col, col, unit, lead, none, none, none, col, unit, lead, none, none, none) + (unit,) * 4 + (none,) * 2 + (unit,) * 2 + (none,),
        out_specs=(row, row, row, col, unit, col, col, unit, lead, none, none, none, col, unit, lead, none, none, none, unit, unit, none, none, none),
        check_vma=False,
    )
```

time: 290 us -> 240 us (0.83)
  Pallas kernels: 125 us -> 92.5 us
  local copies, waits for them, and re-layouts: 18.2 us -> 1.34 us
  starting transfers between devices: 39 us -> 47.6 us
  other arithmetic: 8.95 us -> 1.1 us
  between operations: 4.28 us -> 1.3 us
    pallas_call x12 -> x20, Pallas kernels: 125 us -> 92.5 us  [call(): pl.pallas_call(kernel, out_shape=[pltpu.HBM(*o[:2]) if len(o) > 2 else ja...]
    unnamed x124 -> x14, local copies, waits for them, and re-layouts: 15.4 us -> 0.03 us
    ppermute x55, starting transfers between devices: 39 us -> 47.6 us  [hop(): return lax.ppermute(x, axis, [(i, i ^ mask) for i in range(size)])]
    another operation x6 -> x0, other arithmetic: 4.31 us -> none  [the longest x1 1.92 us: shards(): b_parts = (b_mine, b_other, hop(jnp.stack([b_mine, b_other]), 2, 'dp'))]
  transfers between devices with their start and end apart: 55 -> 55, of which waited for: 20 -> 22; matrix products, arithmetic and copies ran while one was open for 4% -> 1% of each run, Pallas kernels for 41% -> 38%
where the time goes in v1:
time: 240 us; the launch traced here: 235 us
  Pallas kernels  92.5 us (39%)
  waiting for transfers between devices  91.3 us (38%)
  starting transfers between devices  47.6 us (20%)
    pallas_call x20, Pallas kernels, call(): pl.pallas_call(kernel, out_shape=[pltpu.HBM(*o[:2]) if len(o) > 2 else ja...  92.5 us
    ppermute x55, waiting for transfers between devices, hop(): return lax.ppermute(x, axis, [(i, i ^ mask) for i in range(size)])  91.3 us
    ppermute x55, starting transfers between devices, hop(): return lax.ppermute(x, axis, [(i, i ^ mask) for i in range(size)])  47.6 us
  transfers between devices with their start and end apart: 55, of which 22 were waited for; matrix products, arithmetic and copies ran while one was open for 1% of the time, Pallas kernels for 38%

profile of v1, /device:TPU:0, one launch (start us, length us, event | category | flops | bytes accessed | tf_op | source)
XLA Modules:
  0.0 235.2 jit_solution(16922765711223916089)
XLA Ops:
  1.8 3.0 %collective-permute-start.7 = (bf16[768,384]{1,0:T(8,128)(2,1)S(1)}, bf16[768,384]{1,0:T(8,128)(2,1)S(1)}, u32[]{:S(2)}, u32[]{:S(2)}) collective-permute-start(bf16[768,384]{1,0:T(8,128)(2,1)S(1)} %constant_dynamic-slice_fusion), channel_id=1, source_target_pairs={{0,2},{1,3},{2,0},{3,1},{4,6},{5,7},{6,4},{7,5},{8,10},{9,11},{10,... | collective-permute-start | bytes 1769480 | tf_op jit(solution)/shard_map/ppermute | solution.py:637
  6.4 11.5 %attend.1 = (bf16[3,192,128]{2,1,0:T(8,128)(2,1)S(1)}, bf16[3,192,128]{2,1,0:T(8,128)(2,1)S(1)}, bf16[2,3,192,128]{3,2,1,0:T(8,128)(2,1)S(1)}, bf16[3,3,512,512]...) custom-call(s32[5]{0:T(128)S(1)} %stack.19.ids.h_ref, ...), custom_call_target="tpu_custom_call" | custom-call | flops 4499999744 | tf_op jit(solution)/shard_map/attend/pallas_call | solution.py:59
  21.7 4.7 %collective-permute-done.4.s2.refs_8_.refs_14_ = bf16[224,768]{1,0:T(8,128)(2,1)S(1)} collective-permute-done((bf16[224,768]{1,0:T(8,128)(2,1)S(1)}, bf16[224,768]{1,0:T(8,128)(2,1)S(1)}, u32[]{:S(2)}, u32[]{:S(2)}) %collective-permute-start.4) | collective-permute-done | bytes 344096 | tf_op jit(solution)/shard_map/ppermute | solution.py:637
  26.9 5.0 %collective-permute-done.1.xr = bf16[2,3,192,128]{3,2,1,0:T(8,128)(2,1)S(1)} collective-permute-done((bf16[2,3,192,128]{3,2,1,0:T(8,128)(2,1)S(1)}, bf16[2,3,192,128]{3,2,1,0:T(8,128)(2,1)S(1)}, u32[]{:S(2)}, u32[]{:S(2)}) %collective-permute-start.1) | collective-permute-done | bytes 294944 | tf_op jit(solution)/shard_map/ppermute | solution.py:637
  33.9 2.9 %first.1 = (bf16[384,768]{1,0:T(8,128)(2,1)S(1)}, f32[384,768]{1,0:T(8,128)S(1)}, f32[384,128]{1,0:T(8,128)S(1)}, f32[384,768]{1,0:T(8,128)S(1)}, bf16[4,384,192]{2,1,0:T(8,128)(2,1)S(1)}) custom-call(s32[5]{0:T(128)S(1)} %stack.19.ids.h_ref, bf16[3,192,128]{2,1,0:T(8,128)(2,1)S(1)} %get-tuple-element.147.c0, ...), custom_call_target="tpu_custom_call" | custom-call | flops 2000000000 | tf_op jit(solution)/shard_map/first/pallas_call | solution.py:59
  37.5 3.1 %hard_first.1 = (bf16[384,768]{1,0:T(8,128)(2,1)S(1)}, f32[384,768]{1,0:T(8,128)S(1)}) custom-call(s32[5]{0:T(128)S(1)} %stack.19.ids.h_ref, bf16[3,192,128]{2,1,0:T(8,128)(2,1)S(1)} %get-tuple-element.147.c0, bf16[3,192,128]{2,1,0:T(8,128)(2,1)S(1)} %collective-permute-done.c1, bf16[2,3,192,128]{3,2,1,0:T(8,128)(2,1)S(1)} %collective-permute-done.1.xr, ...), custom_call_target="tpu_custom_call" | custom-call | flops 2000000000 | tf_op jit(solution)/shard_map/hard_first/pallas_call | solution.py:59
  40.7 7.1 %collective-permute-done.12.refs_2_.refs_8_ = bf16[384,768]{1,0:T(8,128)(2,1)S(1)} collective-permute-done((bf16[384,768]{1,0:T(8,128)(2,1)S(1)}, bf16[384,768]{1,0:T(8,128)(2,1)S(1)}, u32[]{:S(2)}, u32[]{:S(2)}) %collective-permute-start.12) | collective-permute-done | bytes 589856 | tf_op jit(solution)/shard_map/ppermute | solution.py:637
  49.6 6.5 %inner.1 = (bf16[4,384,768]{2,1,0:T(8,128)(2,1)S(1)}, bf16[4,384,768]{2,1,0:T(8,128)(2,1)S(1)}) custom-call(s32[5]{0:T(128)S(1)} %stack.19.ids.h_ref, bf16[384,768]{1,0:T(8,128)(2,1)S(1)} %get-tuple-element.169.first_low.f0, bf16[768,768]{1,0:T(8,128)(2,1)S(1)} %copy-done.1, bf16[768,768]{1,0:T(8,128)(2,1)S(1)} %collective-permute-done.6.refs_1_, ...), custom_call_target="tpu_custom_call" | custom-call | flops 4000000000 | tf_op jit(solution)/shard_map/inner/pallas_call | solution.py:59
  56.1 5.8 %hard_inner.1.hidden = bf16[4,384,768]{2,1,0:T(8,128)(2,1)S(1)} custom-call(s32[5]{0:T(128)S(1)} %stack.19.ids.h_ref, bf16[384,768]{1,0:T(8,128)(2,1)S(1)} %get-tuple-element.157.first_low, bf16[768,768]{1,0:T(8,128)(2,1)S(1)} %copy-done.1, bf16[768,768]{1,0:T(8,128)(2,1)S(1)} %collective-permute-done.6.refs_1_, ...), custom_call_target="tpu_custom_call" | custom-call | flops 4000000000 | tf_op jit(solution)/shard_map/hard_inner/pallas_call | solution.py:59
  65.6 5.4 %second.1 = (bf16[384,768]{1,0:T(8,128)(2,1)S(1)}, f32[384,768]{1,0:T(8,128)S(1)}, bf16[384,768]{1,0:T(8,128)(2,1)S(1)}, f32[8,768]{1,0:T(8,128)S(1)}) custom-call(s32[5]{0:T(128)S(1)} %stack.19.ids.h_ref, bf16[4,384,768]{2,1,0:T(8,128)(2,1)S(1)} %get-tuple-element.152.hidden, f32[384,768]{1,0:T(8,128)S(1)} %get-tuple-element.153.normed.refs_17_, ...), custom_call_target="tpu_custom_call" | custom-call | flops 3000000000 | tf_op jit(solution)/shard_map/second/pallas_call | solution.py:59
  72.8 9.3 %back.1 = (bf16[3,192,128]{2,1,0:T(8,128)(2,1)S(1)}, bf16[3,192,128]{2,1,0:T(8,128)(2,1)S(1)}, bf16[2,3,192,128]{3,2,1,0:T(8,128)(2,1)S(1)}, bf16[2,208,768]{2,1...) custom-call(s32[5]{0:T(128)S(1)} %stack.19.ids.h_ref, ...), custom_call_target="tpu_custom_call" | custom-call | flops 6499999744 | tf_op jit(solution)/shard_map/back/pallas_call | solution.py:59
  82.8 9.2 %collective-permute-done.17.gx = bf16[384,768]{1,0:T(8,128)(2,1)S(1)} collective-permute-done((bf16[384,768]{1,0:T(8,128)(2,1)S(1)}, bf16[384,768]{1,0:T(8,128)(2,1)S(1)}, u32[]{:S(2)}, u32[]{:S(2)}) %collective-permute-start.17) | collective-permute-done | bytes 589856 | tf_op jit(solution)/shard_map/ppermute | solution.py:637
  93.9 5.7 %units.1 = (bf16[1536,768]{1,0:T(8,128)(2,1)S(1)}, bf16[1536,768]{1,0:T(8,128)(2,1)S(1)}) custom-call(bf16[384,768]{1,0:T(8,128)(2,1)S(1)} %get-tuple-element.169.first_low.f0, bf16[384,768]{1,0:T(8,128)(2,1)S(1)} %collective-permute-done.19.f1, bf16[384,768]{1,0:T(8,128)(2,1)S(1)} %collective-permute-done.20.fx, ...), custom_call_target="tpu_custom_call" | custom-call | flops 3000000000 | tf_op jit(solution)/shard_map/units/pallas_call | solution.py:59
  103.4 3.3 %outer_grad.1 = (bf16[2,192,768]{2,1,0:T(8,128)(2,1)S(1)}, bf16[2,192,768]{2,1,0:T(8,128)(2,1)S(1)}) custom-call(s32[5]{0:T(128)S(1)} %stack.19.ids.h_ref, bf16[384,768]{1,0:T(8,128)(2,1)S(1)} %get-tuple-element.174.gffn.g0, bf16[384,768]{1,0:T(8,128)(2,1)S(1)} %collective-permute-done.16.g1, bf16[384,768]{1,0:T(8,128)(2,1)S(1)} %collective-permute-done.17.gx, ...), custom_call_target="tpu_custom_call" | custom-call | flops 1500000000 | tf_op jit(solution)/shard_map/outer_grad/pallas_call | solution.py:59
  106.7 5.6 %inner_grad.1 = (bf16[2,192,768]{2,1,0:T(8,128)(2,1)S(1)}, bf16[2,192,768]{2,1,0:T(8,128)(2,1)S(1)}, f32[8,768]{1,0:T(8,128)S(1)}) custom-call(s32[5]{0:T(128)S(1)} %stack.19.ids.h_ref, bf16[384,768]{1,0:T(8,128)(2,1)S(1)} %get-tuple-element.169.first_low.f0, bf16[384,768]{1,0:T(8,128)(2,1)S(1)} %collective-permute-done.19.f1, ...), custom_call_target="tpu_custom_call" | custom-call | flops 3000000000 | tf_op jit(solution)/shard_map/inner_grad/pallas_call | solution.py:59
  116.4 15.8 %attend_back.1 = (bf16[2,384,768]{2,1,0:T(8,128)(2,1)S(1)}, bf16[2,384,768]{2,1,0:T(8,128)(2,1)S(1)}, f32[576,768]{1,0:T(8,128)S(1)}, f32[16,768]{1,0:T(8,128)S(1)}) custom-call(s32[5]{0:T(128)S(1)} %stack.19.ids.h_ref, bf16[3,192,128]{2,1,0:T(8,128)(2,1)S(1)} %get-tuple-element.180.g0, bf16[3,192,128]{2,1,0:T(8,128)(2,1)S(1)} %collective-permute-done.24.g1, ...), custom_call_target="tpu_custom_call" | custom-call | flops 7500000256 | tf_op jit(solution)/shard_map/attend_back/pallas_call | solution.py:59
  137.9 5.3 %collective-permute-done.31 = bf16[192,768]{1,0:T(8,128)(2,1)S(1)} collective-permute-done((bf16[192,768]{1,0:T(8,128)(2,1)S(1)}, bf16[192,768]{1,0:T(8,128)(2,1)S(1)}, u32[]{:S(2)}, u32[]{:S(2)}) %collective-permute-start.31) | collective-permute-done | bytes 294944 | tf_op jit(solution)/shard_map/ppermute | solution.py:637
  144.2 2.7 %collective-permute-start.37 = (bf16[192,768]{1,0:T(8,128)(2,1)S(1)}, bf16[192,768]{1,0:T(8,128)(2,1)S(1)}, u32[]{:S(2)}, u32[]{:S(2)}) collective-permute-start(bf16[192,768]{1,0:T(8,128)(2,1)S(1)} %add_convert_fusion.9), channel_id=1, source_target_pairs={{0,16},{4,20},{8,24},{12,28},{16,0},{20,4},{24,8},{28,12},{1,17},{... | collective-permute-start | bytes 884744 | tf_op jit(solution)/shard_map/ppermute | solution.py:637
  147.2 4.9 %hard.1 = (bf16[384,768]{1,0:T(8,128)(2,1)S(1)}, f32[8,128]{1,0:T(8,128)S(1)}) custom-call(s32[5]{0:T(128)S(1)} %stack.19.ids.h_ref, bf16[4,384,768]{2,1,0:T(8,128)(2,1)S(1)} %hard_inner.1.hidden, f32[384,768]{1,0:T(8,128)S(1)} %get-tuple-element.211.normed, bf16[768,768]{1,0:T(8,128)(2,1)S(1)} %copy-done, ...), custom_call_target="tpu_custom_call" | custom-call | flops 3000000000 | tf_op jit(solution)/shard_map/hard/pallas_call | solution.py:59
  153.3 3.7 %collective-permute-done.30 = bf16[2,208,768]{2,1,0:T(8,128)(2,1)S(1)} collective-permute-done((bf16[2,208,768]{2,1,0:T(8,128)(2,1)S(1)}, bf16[2,208,768]{2,1,0:T(8,128)(2,1)S(1)}, u32[]{:S(2)}, u32[]{:S(2)}) %collective-permute-start.30) | collective-permute-done | bytes 639008 | tf_op jit(solution)/shard_map/ppermute | solution.py:637
  160.3 6.2 %collective-permute-done.37 = bf16[192,768]{1,0:T(8,128)(2,1)S(1)} collective-permute-done((bf16[192,768]{1,0:T(8,128)(2,1)S(1)}, bf16[192,768]{1,0:T(8,128)(2,1)S(1)}, u32[]{:S(2)}, u32[]{:S(2)}) %collective-permute-start.37) | collective-permute-done | bytes 294944 | tf_op jit(solution)/shard_map/ppermute | solution.py:637
  166.6 5.3 %collective-permute-done.35 = bf16[192,768]{1,0:T(8,128)(2,1)S(1)} collective-permute-done((bf16[192,768]{1,0:T(8,128)(2,1)S(1)}, bf16[192,768]{1,0:T(8,128)(2,1)S(1)}, u32[]{:S(2)}, u32[]{:S(2)}) %collective-permute-start.35) | collective-permute-done | bytes 294944 | tf_op jit(solution)/shard_map/ppermute | solution.py:637
  172.0 5.8 %collective-permute-done.34.got = bf16[208,768]{1,0:T(8,128)(2,1)S(1)} collective-permute-done((bf16[208,768]{1,0:T(8,128)(2,1)S(1)}, bf16[208,768]{1,0:T(8,128)(2,1)S(1)}, u32[]{:S(2)}, u32[]{:S(2)}) %collective-permute-start.34) | collective-permute-done | bytes 319520 | tf_op jit(solution)/shard_map/ppermute | solution.py:637
  180.9 2.5 %collective-permute-start.41 = (bf16[192,768]{1,0:T(8,128)(2,1)S(1)}, bf16[192,768]{1,0:T(8,128)(2,1)S(1)}, u32[]{:S(2)}, u32[]{:S(2)}) collective-permute-start(bf16[192,768]{1,0:T(8,128)(2,1)S(1)} %add_convert_fusion.8.amine.ak), channel_id=1, source_target_pairs={{0,8},{4,12},{8,0},{12,4},{16,24},{20,28},{24,16},{28,20},{1,9},{5... | collective-permute-start | bytes 884744 | tf_op jit(solution)/shard_map/ppermute | solution.py:637
  185.0 9.7 %collective-permute-done.41.aother.ao = bf16[192,768]{1,0:T(8,128)(2,1)S(1)} collective-permute-done((bf16[192,768]{1,0:T(8,128)(2,1)S(1)}, bf16[192,768]{1,0:T(8,128)(2,1)S(1)}, u32[]{:S(2)}, u32[]{:S(2)}) %collective-permute-start.41) | collective-permute-done | bytes 294944 | tf_op jit(solution)/shard_map/ppermute | solution.py:637
  195.4 2.5 %collective-permute-start.47 = (bf16[2,192,768]{2,1,0:T(8,128)(2,1)S(1)}, bf16[2,192,768]{2,1,0:T(8,128)(2,1)S(1)}, u32[]{:S(2)}, u32[]{:S(2)}) collective-permute-start(bf16[2,192,768]{2,1,0:T(8,128)(2,1)S(1)} %get-tuple-element.227), channel_id=1, source_target_pairs={{0,8},{4,12},{8,0},{12,4},{16,24},{20,28},{24,16},{28,20},{1,9},{5... | collective-permute-start | bytes 1769480 | tf_op jit(solution)/shard_map/ppermute | solution.py:637
  198.6 10.7 %collective-permute-done.46.aq = bf16[2,192,768]{2,1,0:T(8,128)(2,1)S(1)} collective-permute-done((bf16[2,192,768]{2,1,0:T(8,128)(2,1)S(1)}, bf16[2,192,768]{2,1,0:T(8,128)(2,1)S(1)}, u32[]{:S(2)}, u32[]{:S(2)}) %collective-permute-start.46) | collective-permute-done | bytes 589856 | tf_op jit(solution)/shard_map/ppermute | solution.py:637
  209.2 2.9 %collective-permute-done.47.bq = bf16[2,192,768]{2,1,0:T(8,128)(2,1)S(1)} collective-permute-done((bf16[2,192,768]{2,1,0:T(8,128)(2,1)S(1)}, bf16[2,192,768]{2,1,0:T(8,128)(2,1)S(1)}, u32[]{:S(2)}, u32[]{:S(2)}) %collective-permute-start.47) | collective-permute-done | bytes 589856 | tf_op jit(solution)/shard_map/ppermute | solution.py:637
  212.1 3.0 %weights.1 = (f32[768,768]{1,0:T(8,128)}, f32[768,768]{1,0:T(8,128)}) custom-call(s32[5]{0:T(128)S(1)} %stack.19.ids.h_ref, bf16[192,768]{1,0:T(8,128)(2,1)S(1)} %add_convert_fusion.8.amine.ak, bf16[192,768]{1,0:T(8,128)(2,1)S(1)} %collective-permute-done.41.aother.ao, bf16[2,192,768]{2,1,0:T(8,128)(2,1)S(1)} %collective-permute-done.46.aq, ...), custom_call_target="tpu_custom_call" | custom-call | flops 500000000 | tf_op jit(solution)/shard_map/weights/pallas_call | solution.py:59
  215.1 2.5 %collective-permute-done.43.other = bf16[224,768]{1,0:T(8,128)(2,1)S(1)} collective-permute-done((bf16[224,768]{1,0:T(8,128)(2,1)S(1)}, bf16[224,768]{1,0:T(8,128)(2,1)S(1)}, u32[]{:S(2)}, u32[]{:S(2)}) %collective-permute-start.43) | collective-permute-done | bytes 344096 | tf_op jit(solution)/shard_map/ppermute | solution.py:637
  223.7 3.7 %spread.1 = (bf16[3,512,768]{2,1,0:T(8,128)(2,1)}, bf16[3,512,768]{2,1,0:T(8,128)(2,1)}, bf16[3,512,768]{2,1,0:T(8,128)(2,1)}) custom-call(s32[5]{0:T(128)S(1)} %stack.19.ids.h_ref, bf16[384,768]{1,0:T(8,128)(2,1)S(1)} %get-tuple-element.230.refs_0_, bf16[384,768]{1,0:T(8,128)(2,1)S(1)} %collective-permute-done.48.refs_1_, ...), custom_call_target="tpu_custom_call" | custom-call | flops 500000000 | tf_op jit(solution)/shard_map/spread/pallas_call | solution.py:59
  227.5 5.3 %collective-permute-done.54.cq = bf16[432,768]{1,0:T(8,128)(2,1)S(1)} collective-permute-done((bf16[432,768]{1,0:T(8,128)(2,1)S(1)}, bf16[432,768]{1,0:T(8,128)(2,1)S(1)}, u32[]{:S(2)}, u32[]{:S(2)}) %collective-permute-start.54) | collective-permute-done | bytes 663584 | tf_op jit(solution)/shard_map/ppermute | solution.py:637
  (128 shorter events, 53.4 us)
Async XLA Ops:
  1.8 18.1 %collective-permute-start.7 = (bf16[768,384]{1,0:T(8,128)(2,1)S(1)}, bf16[768,384]{1,0:T(8,128)(2,1)S(1)}, u32[]{:S(2)}, u32[]{:S(2)}) collective-permute-start(bf16[768,384]{1,0:T(8,128)(2,1)S(1)} %constant_dynamic-slice_fusion), channel_id=1, source_target_pairs={{0,2},{1,3},{2,0},{3,1},{4,6},{5,7},{6,4},{7,5},{8,10},{9,11},{10,... | collective-permute-start | bytes 1769480 | tf_op jit(solution)/shard_map/ppermute | solution.py:637
  6.2 20.2 %collective-permute-start.4 = (bf16[224,768]{1,0:T(8,128)(2,1)S(1)}, bf16[224,768]{1,0:T(8,128)(2,1)S(1)}, u32[]{:S(2)}, u32[]{:S(2)}) collective-permute-start(bf16[224,768]{1,0:T(8,128)(2,1)S(1)} %get-tuple-element.144.s0.refs_6_.refs_12_), channel_id=1, source_target_pairs={{0,2},{1,3},{2,0},{3,1},{4,6},{5,7},{6,4},{7,5},{8,10},{9,11},{10,... | collective-permute-start | bytes 1032200 | tf_op jit(solution)/shard_map/ppermute | solution.py:637
  20.0 17.0 %collective-permute-start.8 = (bf16[768,384]{1,0:T(8,128)(2,1)S(1)}, bf16[768,384]{1,0:T(8,128)(2,1)S(1)}, u32[]{:S(2)}, u32[]{:S(2)}) collective-permute-start(bf16[768,384]{1,0:T(8,128)(2,1)S(1)} %collective-permute-done.7.refs_2_), channel_id=1, source_target_pairs={{0,4},{4,0},{8,12},{12,8},{16,20},{20,16},{24,28},{28,24},{1,5},{5... | collective-permute-start | bytes 1769480 | tf_op jit(solution)/shard_map/ppermute | solution.py:637
  21.5 28.1 %collective-permute-start.6 = (bf16[768,768]{1,0:T(8,128)(2,1)S(1)}, bf16[768,768]{1,0:T(8,128)(2,1)S(1)}, u32[]{:S(2)}, u32[]{:S(2)}) collective-permute-start(bf16[768,768]{1,0:T(8,128)(2,1)S(1)} %copy-done.1), channel_id=1, source_target_pairs={{0,1},{1,0},{2,3},{3,2},{4,5},{5,4},{6,7},{7,6},{8,9},{9,8},{10,11... | collective-permute-start | bytes 3538952 | tf_op jit(solution)/shard_map/ppermute | solution.py:637
  31.9 15.8 %collective-permute-start.12 = (bf16[384,768]{1,0:T(8,128)(2,1)S(1)}, bf16[384,768]{1,0:T(8,128)(2,1)S(1)}, u32[]{:S(2)}, u32[]{:S(2)}) collective-permute-start(bf16[384,768]{1,0:T(8,128)(2,1)S(1)} %slice.42), channel_id=1, source_target_pairs={{0,2},{1,3},{2,0},{3,1},{4,6},{5,7},{6,4},{7,5},{8,10},{9,11},{10,... | collective-permute-start | bytes 1769480 | tf_op jit(solution)/shard_map/ppermute | solution.py:637
  37.3 28.3 %collective-permute-start.11 = (bf16[768,768]{1,0:T(8,128)(2,1)S(1)}, bf16[768,768]{1,0:T(8,128)(2,1)S(1)}, u32[]{:S(2)}, u32[]{:S(2)}) collective-permute-start(bf16[768,768]{1,0:T(8,128)(2,1)S(1)} %copy-done), channel_id=1, source_target_pairs={{0,1},{1,0},{2,3},{3,2},{4,5},{5,4},{6,7},{7,6},{8,9},{9,8},{10,11... | collective-permute-start | bytes 3538952 | tf_op jit(solution)/shard_map/ppermute | solution.py:637
  47.7 17.8 %collective-permute-start.14 = (bf16[384,768]{1,0:T(8,128)(2,1)S(1)}, bf16[384,768]{1,0:T(8,128)(2,1)S(1)}, u32[]{:S(2)}, u32[]{:S(2)}) collective-permute-start(bf16[384,768]{1,0:T(8,128)(2,1)S(1)} %collective-permute-done.12.refs_2_.refs_8_), channel_id=1, source_target_pairs={{0,1},{1,0},{2,3},{3,2},{4,5},{5,4},{6,7},{7,6},{8,9},{9,8},{10,11... | collective-permute-start | bytes 1769480 | tf_op jit(solution)/shard_map/ppermute | solution.py:637
  47.8 15.8 %collective-permute-start.13 = (bf16[384,768]{1,0:T(8,128)(2,1)S(1)}, bf16[384,768]{1,0:T(8,128)(2,1)S(1)}, u32[]{:S(2)}, u32[]{:S(2)}) collective-permute-start(bf16[384,768]{1,0:T(8,128)(2,1)S(1)} %slice.43), channel_id=1, source_target_pairs={{0,2},{1,3},{2,0},{3,1},{4,6},{5,7},{6,4},{7,5},{8,10},{9,11},{10,... | collective-permute-start | bytes 1769480 | tf_op jit(solution)/shard_map/ppermute | solution.py:637
  63.6 18.6 %collective-permute-start.20 = (bf16[384,768]{1,0:T(8,128)(2,1)S(1)}, bf16[384,768]{1,0:T(8,128)(2,1)S(1)}, u32[]{:S(2)}, u32[]{:S(2)}) collective-permute-start(bf16[384,768]{1,0:T(8,128)(2,1)S(1)} %get-tuple-element.169.first_low.f0), channel_id=1, source_target_pairs={{0,2},{1,3},{2,0},{3,1},{4,6},{5,7},{6,4},{7,5},{8,10},{9,11},{10,... | collective-permute-start | bytes 1769480 | tf_op jit(solution)/shard_map/ppermute | solution.py:637
  65.3 26.6 %collective-permute-start.19 = (bf16[384,768]{1,0:T(8,128)(2,1)S(1)}, bf16[384,768]{1,0:T(8,128)(2,1)S(1)}, u32[]{:S(2)}, u32[]{:S(2)}) collective-permute-start(bf16[384,768]{1,0:T(8,128)(2,1)S(1)} %get-tuple-element.169.first_low.f0), channel_id=1, source_target_pairs={{0,1},{1,0},{2,3},{3,2},{4,5},{5,4},{6,7},{7,6},{8,9},{9,8},{10,11... | collective-permute-start | bytes 1769480 | tf_op jit(solution)/shard_map/ppermute | solution.py:637
  71.0 20.9 %collective-permute-start.17 = (bf16[384,768]{1,0:T(8,128)(2,1)S(1)}, bf16[384,768]{1,0:T(8,128)(2,1)S(1)}, u32[]{:S(2)}, u32[]{:S(2)}) collective-permute-start(bf16[384,768]{1,0:T(8,128)(2,1)S(1)} %get-tuple-element.174.gffn.g0), channel_id=1, source_target_pairs={{0,2},{1,3},{2,0},{3,1},{4,6},{5,7},{6,4},{7,5},{8,10},{9,11},{10,... | collective-permute-start | bytes 1769480 | tf_op jit(solution)/shard_map/ppermute | solution.py:637
  82.2 19.2 %collective-permute-start.22 = (bf16[2,208,768]{2,1,0:T(8,128)(2,1)S(1)}, bf16[2,208,768]{2,1,0:T(8,128)(2,1)S(1)}, u32[]{:S(2)}, u32[]{:S(2)}) collective-permute-start(bf16[2,208,768]{2,1,0:T(8,128)(2,1)S(1)} %get-tuple-element.178), channel_id=1, source_target_pairs={{0,1},{1,0},{2,3},{3,2},{4,5},{5,4},{6,7},{7,6},{8,9},{9,8},{10,11... | collective-permute-start | bytes 1916936 | tf_op jit(solution)/shard_map/ppermute | solution.py:637
  82.7 20.6 %collective-permute-start.16 = (bf16[384,768]{1,0:T(8,128)(2,1)S(1)}, bf16[384,768]{1,0:T(8,128)(2,1)S(1)}, u32[]{:S(2)}, u32[]{:S(2)}) collective-permute-start(bf16[384,768]{1,0:T(8,128)(2,1)S(1)} %get-tuple-element.174.gffn.g0), channel_id=1, source_target_pairs={{0,1},{1,0},{2,3},{3,2},{4,5},{5,4},{6,7},{7,6},{8,9},{9,8},{10,11... | collective-permute-start | bytes 1769480 | tf_op jit(solution)/shard_map/ppermute | solution.py:637
  93.7 22.7 %collective-permute-start.24 = (bf16[3,192,128]{2,1,0:T(8,128)(2,1)S(1)}, bf16[3,192,128]{2,1,0:T(8,128)(2,1)S(1)}, u32[]{:S(2)}, u32[]{:S(2)}) collective-permute-start(bf16[3,192,128]{2,1,0:T(8,128)(2,1)S(1)} %get-tuple-element.181), channel_id=1, source_target_pairs={{0,1},{1,0},{2,3},{3,2},{4,5},{5,4},{6,7},{7,6},{8,9},{9,8},{10,11... | collective-permute-start | bytes 442376 | tf_op jit(solution)/shard_map/ppermute | solution.py:637
  101.4 15.0 %collective-permute-start.26 = (bf16[2,3,192,128]{3,2,1,0:T(8,128)(2,1)S(1)}, bf16[2,3,192,128]{3,2,1,0:T(8,128)(2,1)S(1)}, u32[]{:S(2)}, u32[]{:S(2)}) collective-permute-start(bf16[2,3,192,128]{3,2,1,0:T(8,128)(2,1)S(1)} %collective-permute-done.25.gxr), channel_id=1, source_target_pairs={{0,1},{1,0},{2,3},{3,2},{4,5},{5,4},{6,7},{7,6},{8,9},{9,8},{10,11... | collective-permute-start | bytes 884744 | tf_op jit(solution)/shard_map/ppermute | solution.py:637
  112.3 19.9 %collective-permute-start.29 = (bf16[2,192,768]{2,1,0:T(8,128)(2,1)S(1)}, bf16[2,192,768]{2,1,0:T(8,128)(2,1)S(1)}, u32[]{:S(2)}, u32[]{:S(2)}) collective-permute-start(bf16[2,192,768]{2,1,0:T(8,128)(2,1)S(1)} %get-tuple-element.198), channel_id=1, source_target_pairs={{0,8},{4,12},{8,0},{12,4},{16,24},{20,28},{24,16},{28,20},{1,9},{5... | collective-permute-start | bytes 1769480 | tf_op jit(solution)/shard_map/ppermute | solution.py:637
  114.0 18.3 %collective-permute-start.28 = (bf16[384,768]{1,0:T(8,128)(2,1)S(1)}, bf16[384,768]{1,0:T(8,128)(2,1)S(1)}, u32[]{:S(2)}, u32[]{:S(2)}) collective-permute-start(bf16[384,768]{1,0:T(8,128)(2,1)S(1)} %get-tuple-element.230.refs_0_), channel_id=1, source_target_pairs={{0,2},{1,3},{2,0},{3,1},{4,6},{5,7},{6,4},{7,5},{8,10},{9,11},{10,... | collective-permute-start | bytes 1769480 | tf_op jit(solution)/shard_map/ppermute | solution.py:637
  114.9 17.4 %collective-permute-start.27 = (bf16[2,192,768]{2,1,0:T(8,128)(2,1)S(1)}, bf16[2,192,768]{2,1,0:T(8,128)(2,1)S(1)}, u32[]{:S(2)}, u32[]{:S(2)}) collective-permute-start(bf16[2,192,768]{2,1,0:T(8,128)(2,1)S(1)} %get-tuple-element.193), channel_id=1, source_target_pairs={{0,4},{4,0},{8,12},{12,8},{16,20},{20,16},{24,28},{28,24},{1,5},{5... | collective-permute-start | bytes 1769480 | tf_op jit(solution)/shard_map/ppermute | solution.py:637
  134.8 22.3 %collective-permute-start.30 = (bf16[2,208,768]{2,1,0:T(8,128)(2,1)S(1)}, bf16[2,208,768]{2,1,0:T(8,128)(2,1)S(1)}, u32[]{:S(2)}, u32[]{:S(2)}) collective-permute-start(bf16[2,208,768]{2,1,0:T(8,128)(2,1)S(1)} %get-tuple-element.201), channel_id=1, source_target_pairs={{0,4},{4,0},{8,12},{12,8},{16,20},{20,16},{24,28},{28,24},{1,5},{5... | collective-permute-start | bytes 1916936 | tf_op jit(solution)/shard_map/ppermute | solution.py:637
  136.8 22.1 %collective-permute-start.36 = (bf16[384,768]{1,0:T(8,128)(2,1)S(1)}, bf16[384,768]{1,0:T(8,128)(2,1)S(1)}, u32[]{:S(2)}, u32[]{:S(2)}) collective-permute-start(bf16[384,768]{1,0:T(8,128)(2,1)S(1)} %fusion.2), channel_id=1, source_target_pairs={{0,2},{1,3},{2,0},{3,1},{4,6},{5,7},{6,4},{7,5},{8,10},{9,11},{10,... | collective-permute-start | bytes 1769480 | tf_op jit(solution)/shard_map/ppermute | solution.py:637
  144.2 22.3 %collective-permute-start.37 = (bf16[192,768]{1,0:T(8,128)(2,1)S(1)}, bf16[192,768]{1,0:T(8,128)(2,1)S(1)}, u32[]{:S(2)}, u32[]{:S(2)}) collective-permute-start(bf16[192,768]{1,0:T(8,128)(2,1)S(1)} %add_convert_fusion.9), channel_id=1, source_target_pairs={{0,16},{4,20},{8,24},{12,28},{16,0},{20,4},{24,8},{28,12},{1,17},{... | collective-permute-start | bytes 884744 | tf_op jit(solution)/shard_map/ppermute | solution.py:637
  146.9 25.1 %collective-permute-start.35 = (bf16[192,768]{1,0:T(8,128)(2,1)S(1)}, bf16[192,768]{1,0:T(8,128)(2,1)S(1)}, u32[]{:S(2)}, u32[]{:S(2)}) collective-permute-start(bf16[192,768]{1,0:T(8,128)(2,1)S(1)} %add_convert_fusion.10), channel_id=1, source_target_pairs={{0,16},{4,20},{8,24},{12,28},{16,0},{20,4},{24,8},{28,12},{1,17},{... | collective-permute-start | bytes 884744 | tf_op jit(solution)/shard_map/ppermute | solution.py:637
  157.2 20.6 %collective-permute-start.34 = (bf16[208,768]{1,0:T(8,128)(2,1)S(1)}, bf16[208,768]{1,0:T(8,128)(2,1)S(1)}, u32[]{:S(2)}, u32[]{:S(2)}) collective-permute-start(bf16[208,768]{1,0:T(8,128)(2,1)S(1)} %get-tuple-element.255), channel_id=1, source_target_pairs={{0,8},{4,12},{8,0},{12,4},{16,24},{20,28},{24,16},{28,20},{1,9},{5... | collective-permute-start | bytes 958472 | tf_op jit(solution)/shard_map/ppermute | solution.py:637
  158.9 19.0 %collective-permute-start.39 = (f32[8,128]{1,0:T(8,128)S(1)}, f32[8,128]{1,0:T(8,128)S(1)}, u32[]{:S(2)}, u32[]{:S(2)}) collective-permute-start(f32[8,128]{1,0:T(8,128)S(1)} %add.68.error), channel_id=1, source_target_pairs={{0,1},{1,0},{2,3},{3,2},{4,5},{5,4},{6,7},{7,6},{8,9},{9,8},{10,11... | collective-permute-start | bytes 12296 | tf_op jit(solution)/shard_map/ppermute | solution.py:637
  159.2 38.7 %collective-permute-start.45 = (bf16[384,768]{1,0:T(8,128)(2,1)S(1)}, bf16[384,768]{1,0:T(8,128)(2,1)S(1)}, u32[]{:S(2)}, u32[]{:S(2)}) collective-permute-start(bf16[384,768]{1,0:T(8,128)(2,1)S(1)} %get-tuple-element.224.refs_4_), channel_id=1, source_target_pairs={{0,2},{1,3},{2,0},{3,1},{4,6},{5,7},{6,4},{7,5},{8,10},{9,11},{10,... | collective-permute-start | bytes 1769480 | tf_op jit(solution)/shard_map/ppermute | solution.py:637
  178.5 19.3 %collective-permute-start.40 = (bf16[224,768]{1,0:T(8,128)(2,1)S(1)}, bf16[224,768]{1,0:T(8,128)(2,1)S(1)}, u32[]{:S(2)}, u32[]{:S(2)}) collective-permute-start(bf16[224,768]{1,0:T(8,128)(2,1)S(1)} %third.1), channel_id=1, source_target_pairs={{0,16},{4,20},{8,24},{12,28},{16,0},{20,4},{24,8},{28,12},{1,17},{... | collective-permute-start | bytes 1032200 | tf_op jit(solution)/shard_map/ppermute | solution.py:637
  183.9 14.6 %collective-permute-start.44 = (bf16[384,768]{1,0:T(8,128)(2,1)S(1)}, bf16[384,768]{1,0:T(8,128)(2,1)S(1)}, u32[]{:S(2)}, u32[]{:S(2)}) collective-permute-start(bf16[384,768]{1,0:T(8,128)(2,1)S(1)} %fusion.1.refs_8_), channel_id=1, source_target_pairs={{0,2},{1,3},{2,0},{3,1},{4,6},{5,7},{6,4},{7,5},{8,10},{9,11},{10,... | collective-permute-start | bytes 1769480 | tf_op jit(solution)/shard_map/ppermute | solution.py:637
  195.4 16.7 %collective-permute-start.47 = (bf16[2,192,768]{2,1,0:T(8,128)(2,1)S(1)}, bf16[2,192,768]{2,1,0:T(8,128)(2,1)S(1)}, u32[]{:S(2)}, u32[]{:S(2)}) collective-permute-start(bf16[2,192,768]{2,1,0:T(8,128)(2,1)S(1)} %get-tuple-element.227), channel_id=1, source_target_pairs={{0,8},{4,12},{8,0},{12,4},{16,24},{20,28},{24,16},{28,20},{1,9},{5... | collective-permute-start | bytes 1769480 | tf_op jit(solution)/shard_map/ppermute | solution.py:637
  197.9 21.8 %collective-permute-start.48 = (bf16[384,768]{1,0:T(8,128)(2,1)S(1)}, bf16[384,768]{1,0:T(8,128)(2,1)S(1)}, u32[]{:S(2)}, u32[]{:S(2)}) collective-permute-start(bf16[384,768]{1,0:T(8,128)(2,1)S(1)} %get-tuple-element.230.refs_0_), channel_id=1, source_target_pairs={{0,1},{1,0},{2,3},{3,2},{4,5},{5,4},{6,7},{7,6},{8,9},{9,8},{10,11... | collective-permute-start | bytes 1769480 | tf_op jit(solution)/shard_map/ppermute | solution.py:637
  197.9 21.8 %collective-permute-start.49 = (bf16[384,768]{1,0:T(8,128)(2,1)S(1)}, bf16[384,768]{1,0:T(8,128)(2,1)S(1)}, u32[]{:S(2)}, u32[]{:S(2)}) collective-permute-start(bf16[384,768]{1,0:T(8,128)(2,1)S(1)} %collective-permute-done.28.refs_2_), channel_id=1, source_target_pairs={{0,1},{1,0},{2,3},{3,2},{4,5},{5,4},{6,7},{7,6},{8,9},{9,8},{10,11... | collective-permute-start | bytes 1769480 | tf_op jit(solution)/shard_map/ppermute | solution.py:637
  198.5 19.1 %collective-permute-start.43 = (bf16[224,768]{1,0:T(8,128)(2,1)S(1)}, bf16[224,768]{1,0:T(8,128)(2,1)S(1)}, u32[]{:S(2)}, u32[]{:S(2)}) collective-permute-start(bf16[224,768]{1,0:T(8,128)(2,1)S(1)} %add_convert_fusion.2.mine), channel_id=1, source_target_pairs={{0,8},{4,12},{8,0},{12,4},{16,24},{20,28},{24,16},{28,20},{1,9},{5... | collective-permute-start | bytes 1032200 | tf_op jit(solution)/shard_map/ppermute | solution.py:637
  217.6 15.1 %collective-permute-start.54 = (bf16[432,768]{1,0:T(8,128)(2,1)S(1)}, bf16[432,768]{1,0:T(8,128)(2,1)S(1)}, u32[]{:S(2)}, u32[]{:S(2)}) collective-permute-start(bf16[432,768]{1,0:T(8,128)(2,1)S(1)} %last.1.cpair), channel_id=1, source_target_pairs={{0,4},{4,0},{8,12},{12,8},{16,20},{20,16},{24,28},{28,24},{1,5},{5... | collective-permute-start | bytes 1990664 | tf_op jit(solution)/shard_map/ppermute | solution.py:637
  (30 other events, 293.3 us)

commit v2 on v1

--- a/solution.py
+++ b/solution.py
@@ -430,30 +430,42 @@
     return total
 
 
-def outer_grad_kernel(ids, g0, g1, gx, gd, hidden, akeep, asend, big):
-    n = g0.shape[0]
-    big[...] = rows_dot([hidden[r * n : (r + 1) * n, :] for r in range(4)], [g0[...], g1[...], gx[...], gd[...]])
-    slots(big, akeep, asend, ids[1], ids[2])
-
-
-def inner_grad_kernel(ids, f0, f1, fx, fd, g0, g1, gx, gd, outer, hidden, udact, bkeep, bsend, vecs_out, gi, big, acc):
-    n = f0.shape[0]
-    gffns = (g0, g1, gx, gd)
-    acc[...] = jnp.zeros_like(acc)
-    for r in range(4):
-        rows = slice(r * n, (r + 1) * n)
+def unit_grads(first, gffns, outer, hidden, udact, gi, acc):
+    n = gffns[0].shape[0]
+    for r, gffn in enumerate(gffns):
+        rows, own = slice((first + r) * n, (first + r + 1) * n), slice(r * n, (r + 1) * n)
         for s in range(0, outer.shape[0], 256):
             at = slice(s, s + 256)
-            gh = dot_nt(gffns[r][...], outer[at, :])
+            gh = dot_nt(gffn[...], outer[at, :])
             g = (gh * udact[rows, at].astype(F32)).astype(BF)
-            gi[rows, at] = g
+            gi[own, at] = g
             acc[0, :, at] += fold(gh * hidden[rows, at].astype(F32))
             acc[1, :, at] += fold(g.astype(F32))
-    big[...] = rows_dot([f0[...], f1[...], fx[...], fd[...]], [gi[r * n : (r + 1) * n, :] for r in range(4)])
-    slots(big, bkeep, bsend, ids[2], ids[1])
-    vecs_out[...] = jnp.zeros_like(vecs_out)
+
+
+def near_grad_kernel(g0, g1, outer, hidden, udact, part, gi, acc):
+    n = g0.shape[0]
+    part[...] = rows_dot([hidden[:n, :], hidden[n : 2 * n, :]], [g0[...], g1[...]])
+    acc[...] = jnp.zeros_like(acc)
+    unit_grads(0, (g0, g1), outer, hidden, udact, gi, acc)
+
+
+def outer_grad_kernel(ids, gx, gd, hidden, part, akeep, asend, big):
+    n = gx.shape[0]
+    big[...] = part[...] + rows_dot([hidden[2 * n : 3 * n, :], hidden[3 * n :, :]], [gx[...], gd[...]])
+    slots(big, akeep, asend, ids[2], ids[1])
+
+
+def inner_grad_kernel(ids, f0, f1, fx, fd, gx, gd, outer, hidden, udact, near, sums, bkeep, bsend, gi, big, acc):
+    n = f0.shape[0]
+    d = f0.shape[1]
+    acc[...] = sums[...]
+    unit_grads(2, (gx, gd), outer, hidden, udact, gi, acc)
+    big[:d, :] = rows_dot([f0[...], f1[...], fx[...], fd[...]], [near[:n, :], near[n:, :], gi[:n, :], gi[n:, :]])
+    big[d:, :] = jnp.zeros((big.shape[0] - d, big.shape[1]), F32)
     for j in range(2):
-        vecs_out[j : j + 1, :] = jnp.sum(acc[j], axis=0, keepdims=True)
+        big[d + j : d + j + 1, :] = jnp.sum(acc[j], axis=0, keepdims=True)
+    slots(big, bkeep, bsend, ids[1], ids[2])
 
 
 def attend_back_kernel(ids, g0, g1, gxr, gcr, e_ref, inv_ref, k_ref, v_ref, q_ref, kt, tok, wq, wk, wv, keep, send, wacc, cacc, dct, nat, low):
@@ -500,7 +512,7 @@
             send[r // 2, at, :] = rows
 
 
-def turn_kernel(ids, wacc, cacc, dmine, drecv, vg, akeep, agot, bkeep, bgot, amine, agive, bmine, bgive, ckeep, csend, big):
+def turn_kernel(ids, wacc, cacc, dmine, drecv, ckeep, csend, big):
     n = wacc.shape[0]
     c = n // 3
     big[n + c + 32 :, :] = jnp.zeros((big.shape[0] - n - c - 32, big.shape[1]), F32)
@@ -512,11 +524,7 @@
     big[n : n + 1, :c] = col[:, :c]
     big[n + 1 : n + 2, :c] = col[:, 2 * c : 3 * c]
     big[n + 2 : n + 3, : c * 2] = cacc[8:9, : c * 2]
-    big[n + 8 : n + 16, :] = vg[...]
     slots(big, ckeep, csend, ids[1], ids[2])
-    for keep, got, mine, give in ((akeep, agot, amine, agive), (bkeep, bgot, bmine, bgive)):
-        mine[...] = (keep[0].astype(F32) + got[0].astype(F32)).astype(BF)
-        give[...] = (keep[1].astype(F32) + got[1].astype(F32)).astype(BF)
 
 
 def third_kernel(ids, mine, got, error, error_1, out):
@@ -529,9 +537,8 @@
     out[n:, :] = jnp.concatenate(rows, axis=0).astype(BF)
 
 
-def pair_kernel(amine, aother, bmine, bother, apair, bpair):
-    apair[0], apair[1] = amine[...], aother[...]
-    bpair[0], bpair[1] = bmine[...], bother[...]
+def pair_kernel(mine, other, out):
+    out[0], out[1] = mine[...], other[...]
 
 
 def last_kernel(mine, other, out):
@@ -541,25 +548,38 @@
     out[2 * n :, :] = (mine[n:, :].astype(F32) + other[n:, :].astype(F32)).astype(BF)
 
 
-def weights_kernel(ids, ak, ao, aq, bk, bo, bq, uw, iw):
-    for dst, k, o, q, first_bit, second_bit in ((uw, ak, ao, aq, ids[1], ids[2]), (iw, bk, bo, bq, ids[2], ids[1])):
-        n = k.shape[0]
-        for a in range(2):
-            for b in range(2):
-                j = (first_bit ^ a) * 2 + (second_bit ^ b)
-                src = (k if b == 0 else o)[...] if a == 0 else q[b]
-                dst[pl.ds(pl.multiple_of(j * n, 16), n), :] = src.astype(F32)
-
-
-def final_kernel(ids, consts, cpair, cq, qw, kw, vw, ow, qb, vb, ob, fg, fs, ib, ub, sg, ss, ha, ua, da, me, pe, big):
-    d = consts.shape[1]
-    c = qw.shape[0]
-
+def place(ids, swap, k, o, q, dst):
+    n = k.shape[0]
+    one, two = (ids[2], ids[1]) if swap else (ids[1], ids[2])
+    for a in range(2):
+        for b in range(2):
+            src = (k if b == 0 else o)[...] if a == 0 else q[b]
+            dst[pl.ds(pl.multiple_of(((one ^ a) * 2 + (two ^ b)) * n, 16), n), :] = src.astype(F32)
+
+
+def outer_out_kernel(ids, k, o, q, uw):
+    place(ids, True, k, o, q, uw)
+
+
+def inner_out_kernel(ids, consts, pair, q, live, iw, ib, ua, pe, big):
     n = big.shape[0] // 4
-    for a, src in enumerate((cpair, cq)):
+    for a, src in enumerate((pair, q)):
         for b in range(2):
             j = (ids[1] ^ a) * 2 + (ids[2] ^ b)
             big[pl.ds(pl.multiple_of(j * n, 16), n), :] = src[b * n : (b + 1) * n, :].astype(F32)
+    d = iw.shape[0]
+    iw[...] = big[:d, :]
+    ua[...] = (1.5 * big[d : d + 1, :] * (1.0 - consts[UGATE : UGATE + 1, :])).reshape(d)
+    ib[...] = big[d + 1 : d + 2, :].reshape(d)
+    hard = jnp.sum(pair[2 * n :, :].astype(F32) + q[2 * n :, :].astype(F32))
+    pe[0] = 0.5 * hard / live[0]
+
+
+def final_kernel(ids, consts, ck, co, cq, qw, kw, vw, ow, qb, vb, ob, fg, fs, ub, sg, ss, ha, da, me, live_out, big):
+    d = consts.shape[1]
+    c = qw.shape[0]
+
+    place(ids, False, ck, co, cq, big)
     qw[...] = big[:c, :]
     kw[...] = big[c : 2 * c, :]
     vw[...] = big[2 * c : 3 * c, :]
@@ -572,9 +592,6 @@
         ref[...] = vec[row : row + 1, :].reshape(d)
     hg = consts[HGATE : HGATE + 1, :]
     da[...] = (1.5 * vec[6:7, :] * hg * (1.0 - hg)).reshape(d)
-    ug = consts[UGATE : UGATE + 1, :]
-    ua[...] = (1.5 * own[8:9, :] * (1.0 - ug)).reshape(d)
-    ib[...] = own[9:10, :].reshape(d)
     qb[...] = own[0:1, :c].reshape(c)
     vb[...] = own[1:2, :c].reshape(c)
     gate = consts[HEADG : HEADG + 1, :]
@@ -583,8 +600,6 @@
         ha[i] = 1.5 * own[2, i * 128] * (1.0 - g)
     lane = lax.broadcasted_iota(jnp.int32, (1, d), 1)
     nd = ids[4]
-    m = cpair.shape[0] - 16
-    hard_sum = jnp.sum(cpair[m:, :].astype(F32) + cq[m:, :].astype(F32))
     marks = vec[7:8, :]
 
     def between(lo, hi):
@@ -592,7 +607,7 @@
 
     live = jnp.maximum(between(2, 4), 1.0)
     me[0] = 0.5 * between(0, 2) / live
-    pe[0] = 0.5 * hard_sum / live
+    live_out[0] = live
 
 
 def spread_kernel(h_ref, *refs):
@@ -655,7 +670,7 @@
         prep_kernel,
         [((16, d), F32), ((c + VEC, w), BF)],
         tuple(in_hbm(a) for a in (*small, after(output_weight, inner_half))),
-        specs=[ANY] * 19, scratch=[(pltpu.VMEM if a.shape[0] > heads else pltpu.SMEM)(a.shape, a.dtype) for a in small] + [pltpu.SemaphoreType.DMA((19,))], us=2, limit=8, name="prep",
+        specs=[ANY] * 19, scratch=[(pltpu.VMEM if a.shape[0] > heads else pltpu.SMEM)(a.shape, a.dtype) for a in small] + [pltpu.SemaphoreType.DMA((19,))], us=2, limit=4, name="prep",
     )
     pack_2 = hop(pack, 2)
     pack_1 = hop(pack, 1)
@@ -677,11 +692,13 @@
                    pl.BlockSpec((1, 8, length), lambda b, *_: (b, 0, 0)), pl.BlockSpec((length, c), lambda b, *_: (b, 0)),
                    pl.BlockSpec((length, c), lambda b, *_: (b, 0)), pl.BlockSpec((length, c), lambda b, *_: (b, 0)),
                    pl.BlockSpec((1, c, length), lambda b, *_: (b, 0, 0)), pl.BlockSpec((1, c, length), lambda b, *_: (b, 0, 0))],
-        scratch=[pltpu.VMEM((length, length), F32), pltpu.VMEM((c, length), BF)], us=9, limit=24, name="attend",
+        scratch=[pltpu.VMEM((length, length), F32), pltpu.VMEM((c, length), BF)], us=9, limit=16, name="attend",
     )
     cx = hop(cfar, 2)
     c1r = hop(c1, 1)
-    outer_a = hop(after(outer_weight, c1r)[:half], 2)
+    outer_late = after(outer_weight, c1r)
+    outer_a = hop(outer_late[:half], 2)
+    outer_b = hop(outer_late[half:], 2)
     inner_x, pack_2 = after(inner_x, c0), after(pack_2, c0)
     inner_y, inner_3x = hop(inner_x, 1, "dp"), hop(inner_x, 1)
     packs = (pack, pack_1, pack_2, hop(pack_2, 1))
@@ -695,13 +712,13 @@
             [((t, d), BF), ((t, d), F32)] + (more if soft else []),
             (ids, *pieces, *packs, tokens, consts),
             prefetch=1, specs=[VM] * 8 + [ANY, VM],
-            scratch=scratch if soft else scratch + [pltpu.VMEM((t, d), F32), pltpu.VMEM((4, t, c), BF)], us=4, limit=12, name="first" if soft else "hard_first",
+            scratch=scratch if soft else scratch + [pltpu.VMEM((t, d), F32), pltpu.VMEM((4, t, c), BF)], us=4, limit=8, name="first" if soft else "hard_first",
         )
 
     def inner(soft, low):
         return call(
             partial(inner_kernel, soft), [((4, t, w), BF)] * (2 if soft else 1), (ids, low, *inners, *packs),
-            prefetch=1, us=8, limit=16, name="inner" if soft else "hard_inner",
+            prefetch=1, us=8, limit=8, name="inner" if soft else "hard_inner",
         )
 
     first_low, normed, inv1, attn, gated = first(True, pieces)
@@ -712,7 +729,6 @@
     hard_low, hard_normed = first(False, (after(c0, first_low), *pieces[1:]))
     outer_a = after(outer_a, hard_low)
     outer_3a = hop(outer_a, 1)
-    outer_b = hop(after(outer_weight, outer_a)[half:], 2)
     hidden, udact = inner(True, after(first_low, hard_low))
     (hard_hidden,) = inner(False, after(hard_low, hidden))
     outer_b = after(outer_b, hard_hidden)
@@ -723,9 +739,8 @@
         [((t, d), BF), ((t, d), F32), ((t, d), BF), ((8, d), F32)],
         (ids, hidden, normed, *outers, teacher, present, consts),
         prefetch=1, specs=[VM] * 8 + [ANY] + [VM] * 2,
-        scratch=[pltpu.VMEM((t, d), BF), pltpu.VMEM((t, d), F32), pltpu.VMEM((5, 8, d), F32), pltpu.SemaphoreType.DMA((blocks,))], us=6, limit=16, name="second",
-    )
-    gffn_2 = hop(gffn, 2)
+        scratch=[pltpu.VMEM((t, d), BF), pltpu.VMEM((t, d), F32), pltpu.VMEM((5, 8, d), F32), pltpu.SemaphoreType.DMA((blocks,))], us=6, limit=8, name="second",
+    )
     gffn_1 = hop(gffn, 1)
 
     g0, g1, gfar, dkeep, dsend, grad_one = call(
@@ -733,41 +748,22 @@
         [((blocks, c, quarter), BF), ((blocks, c, quarter), BF), ((2, blocks, c, quarter), BF), ((2, c + 16, d), BF), ((2, c + 16, d), BF), ((t, d), F32)],
         (ids, gffn, udact, *inners, *outers, *packs, grad_two, normed, inv1, attn, gated, v2, present, consts),
         prefetch=1,
-        scratch=[pltpu.VMEM((4, t, w), BF), pltpu.VMEM((t, d), F32), pltpu.VMEM((t, d), BF), pltpu.VMEM((4, 8, d), F32)], us=13, limit=24, name="back",
+        scratch=[pltpu.VMEM((4, t, w), BF), pltpu.VMEM((t, d), F32), pltpu.VMEM((t, d), BF), pltpu.VMEM((4, 8, d), F32)], us=13, limit=12, name="back",
     )
     gx = hop(gfar, 2)
     g1r = hop(g1, 1)
     d_got = hop(dsend, 1)
-    gffn_2, first_2 = after(gffn_2, g0), after(first_2, g0)
+    first_2 = after(first_2, g0)
     firsts = (first_low, first_1, first_2, hop(first_2, 1))
-    gffns = (gffn, gffn_1, gffn_2, hop(gffn_2, 1))
-
     hidden_own, udact_own = call(
-        units_kernel, [((rows, w), BF), ((rows, w), BF)], (after(firsts[0], g0), *firsts[1:], consts, inner_weight), us=6, limit=16, name="units"
+        units_kernel, [((rows, w), BF), ((rows, w), BF)], (after(firsts[0], g0), *firsts[1:], consts, inner_weight), us=6, limit=8, name="units"
     )
     gx, d_got = after(gx, hidden_own), after(d_got, hidden_own)
     gpieces = (g0, g1r, gx, hop(gx, 1))
     d_mine, d_give = add(dkeep[0], d_got[0]), add(dkeep[1], d_got[1])
     d_recv = hop(d_give, 2)
-
-    akeep, asend = call(
-        outer_grad_kernel, [((2, w // 4, d), BF)] * 2, (ids, *gffns, hidden_own), prefetch=1, scratch=[pltpu.VMEM((w, d), F32)], us=3, limit=16, name="outer_grad"
-    )
-    a_got = hop(asend, 1, "dp")
-    bkeep, bsend, vg = call(
-        inner_grad_kernel,
-        [((2, d // 4, w), BF)] * 2 + [((8, w), F32)],
-        (ids, *firsts, after(gffns[0], akeep), *gffns[1:], outer_weight, hidden_own, udact_own),
-        prefetch=1, scratch=[pltpu.VMEM((rows, w), BF), pltpu.VMEM((w, d), F32), pltpu.VMEM((2, 8, w), F32)], us=6, limit=24, name="inner_grad",
-    )
-    gpieces = (after(g0, bkeep, d_recv), *gpieces[1:])
-    b_got = hop(bsend, 2, "dp")
-    student_rows = after(student_rows, akeep)
-    student_2 = hop(student_rows, 2)
-    student_1 = hop(student_rows, 1)
-
+    gffn_2 = hop(after(gffn, d_give, gx), 2)
     pick = lambda *s: pl.BlockSpec((1,) + s, lambda b, *_: (b,) + (0,) * len(s))
-    n_c = 4 * ((3 * c + c + 32 + 63) // 64) * 16
     keep, send, wacc, cacc = call(
         attend_back_kernel,
         [((2, t, d), BF), ((2, t, d), BF), ((3 * c, d), F32), ((16, d), F32)],
@@ -779,24 +775,37 @@
                pl.BlockSpec((length, d), lambda b, *_: (b, 0)), full(c, d), full(c, d), full(c, d)],
         out_specs=[full(2, t, d), full(2, t, d), full(3 * c, d), full(16, d)],
         scratch=[pltpu.VMEM((c, length), BF), pltpu.VMEM((length, 3 * c), BF), pltpu.VMEM((length, d), BF)],
-        us=15, limit=32, name="attend_back",
-    )
-    a_got, b_got, student_2 = after(a_got, keep), after(b_got, keep), after(student_2, keep)
-    part = (w // 4, d)
-    a_mine, a_give, b_mine, b_give, ckeep, csend = call(
-        turn_kernel,
-        [(part, BF)] * 4 + [((2, n_c // 4, d), BF)] * 2,
-        (ids, wacc, cacc, d_mine, d_recv, vg, akeep, after(a_got, student_2), bkeep, b_got),
-        prefetch=1, specs=[VM] * 9, scratch=[pltpu.VMEM((n_c, d), F32)], us=0.1, limit=16, name="turn",
-    )
-    got = hop(after(send, a_mine), 1)
+        us=15, limit=20, name="attend_back",
+    )
+    gffn_2 = after(gffn_2, keep)
+    n_c = 4 * ((3 * c + c + 32 + 63) // 64) * 16
+    ckeep, csend = call(
+        turn_kernel, [((2, n_c // 4, d), BF)] * 2, (ids, wacc, cacc, d_mine, after(d_recv, keep, gffn_2)), prefetch=1, specs=[VM] * 4,
+        scratch=[pltpu.VMEM((n_c, d), F32)], us=1, limit=8, name="turn",
+    )
+    got = hop(after(send, ckeep), 1)
     c_got = hop(csend, 1, "dp")
-    a_got, b_got = hop(a_give, 2, "dp"), hop(b_give, 1, "dp")
-    give = add(keep[1], got[1])
-    mine = add(keep[0], got[0])
+    gffn_2 = after(gffn_2, ckeep)
+    gffn_3 = hop(gffn_2, 1)
+    part, near, sums = call(
+        near_grad_kernel, [((w, d), F32), ((2 * t, w), BF), ((2, 8, w), F32)], (after(gffn, gffn_2), gffn_1, outer_weight, hidden_own, udact_own),
+        us=5, limit=8, name="near_grad",
+    )
+    got = after(got, near)
+    mine, give = add(keep[0], got[0]), add(keep[1], got[1])
     recv = hop(give, 2)
-    students = (student_rows, student_1, student_2, hop(after(student_2, give), 1))
-    a_mine, b_mine = add(a_mine, after(a_got, give)), add(b_mine, after(b_got, give))
+    akeep, asend = call(
+        outer_grad_kernel, [((2, w // 4, d), BF)] * 2, (ids, after(gffn_2, give), gffn_3, hidden_own, part), prefetch=1, scratch=[pltpu.VMEM((w, d), F32)],
+        us=2, limit=8, name="outer_grad",
+    )
+    a_got = hop(asend, 2, "dp")
+    n_b = d + 64
+    bkeep, bsend = call(
+        inner_grad_kernel, [((2, n_b // 4, w), BF)] * 2,
+        (ids, *firsts, after(gffn_2, akeep), gffn_3, outer_weight, hidden_own, udact_own, near, sums), prefetch=1,
+        scratch=[pltpu.VMEM((2 * t, w), BF), pltpu.VMEM((n_b, w), F32), pltpu.VMEM((2, 8, w), F32)], us=4, limit=12, name="inner_grad",
+    )
+    b_got = hop(bsend, 1, "dp")
 
     def across(x):
         mask = 4
@@ -806,57 +815,78 @@
             mask *= 2
         return x
 
-    a_mine, b_mine = across(a_mine), across(b_mine)
+    def split(keep, got):
+        return add(keep[0], got[0]), add(keep[1], got[1])
+
+    c_mine, c_give = split(ckeep, after(c_got, bkeep))
+    c_got = hop(c_give, 2, "dp")
     pruned_rows, error = call(
         hard_kernel,
         [((t, d), BF), ((8, 128), F32)],
-        (ids, after(hard_hidden, a_mine[0], b_mine[0], give), hard_normed, *outers, teacher, present, consts),
+        (ids, after(hard_hidden, c_give), hard_normed, *outers, teacher, present, consts),
         prefetch=1, specs=[VM] * 8 + [ANY] + [VM] * 2,
-        scratch=[pltpu.VMEM((t, d), BF), pltpu.VMEM((t, d), F32), pltpu.VMEM((8, d), F32), pltpu.SemaphoreType.DMA((blocks,))], us=6, limit=16, name="hard",
-    )
-    error = error + hop(error, 2)
-    error_1 = hop(error, 1)
-    recv, c_got = after(recv, pruned_rows), after(c_got, pruned_rows)
-    c_mine, c_give = add(ckeep[0], c_got[0]), add(ckeep[1], c_got[1])
-    c_got = hop(c_give, 2, "dp")
+        scratch=[pltpu.VMEM((t, d), BF), pltpu.VMEM((t, d), F32), pltpu.VMEM((8, d), F32), pltpu.SemaphoreType.DMA((blocks,))], us=0.1, limit=8, name="hard",
+    )
+
+    recv = after(recv, pruned_rows)
     grad_rows = (grad_one + (mine.astype(F32) + recv.astype(F32))).astype(BF)
     grad_2 = hop(grad_rows, 2)
     grad_1 = hop(grad_rows, 1)
-    pruned_2 = hop(after(pruned_rows, grad_rows), 2)
+    a_mine, a_give = split(akeep, after(a_got, grad_rows))
+    a_got = hop(a_give, 1, "dp")
+    b_mine, b_give = split(bkeep, after(b_got, a_give))
+    b_got = hop(b_give, 2, "dp")
+    pruned_rows = after(pruned_rows, b_give)
+    pruned_2 = hop(pruned_rows, 2)
     pruned_1 = hop(pruned_rows, 1)
-    a_mine, b_mine = (add(x, after(got, c_give, grad_rows)) for x, got in (a_mine, b_mine))
-    a_other, b_other = hop(a_mine, 2, "dp"), hop(b_mine, 1, "dp")
-    (c_mine,) = call(
-        third_kernel, [((n_c // 4 + 16, d), BF)], (ids, c_mine, after(c_got, a_mine, b_mine), error, error_1), prefetch=1, us=0.1, limit=8, name="third"
-    )
-    c_mine = across(c_mine)
-    a_pair, b_pair = call(pair_kernel, [((2,) + part, BF)] * 2, (a_mine, after(a_other, c_mine[0]), b_mine, b_other), us=0.1, limit=8, name="pair")
-    a_parts = (a_mine, a_other, hop(a_pair, 1, "dp"))
-    b_parts = (b_mine, b_other, hop(b_pair, 2, "dp"))
-    grad_2 = after(grad_2, a_pair)
+    c_mine = across(add(c_mine, after(c_got, b_give)))
+    error = after(error, b_give)
+    error = error + hop(error, 2)
+    error_1 = hop(error, 1)
+    a_mine = across(add(a_mine, after(a_got, c_mine[0])))
+    (b_mine,) = call(
+        third_kernel, [((n_b // 4 + 16, d), BF)], (ids, b_mine, after(b_got, a_mine[0]), error, error_1), prefetch=1, us=0.1, limit=4, name="third"
+    )
+    c_mine = add(c_mine[0], after(c_mine[1], b_mine))
+    b_mine = across(b_mine)
+    c_other = hop(c_mine, 2, "dp")
+    grad_2 = after(grad_2, c_mine)
     grads = (grad_rows, grad_1, grad_2, hop(grad_2, 1))
-    c_mine = add(c_mine[0], after(c_mine[1], a_pair))
-    c_other = hop(c_mine, 2, "dp")
-    pruned_2 = after(pruned_2, c_mine)
+    student_rows = after(student_rows, grad_2)
+    student_2 = hop(student_rows, 2)
+    student_1 = hop(student_rows, 1)
+    a_mine = add(a_mine[0], after(a_mine[1], grad_2))
+    a_other = hop(a_mine, 1, "dp")
+    (c_pair,) = call(pair_kernel, [((2,) + c_mine.shape, BF)], (c_mine, after(c_other, a_mine)), us=0.1, limit=4, name="pair3")
+    c_last = hop(c_pair, 1, "dp")
+    b_mine = add(b_mine[0], after(b_mine[1], c_pair))
+    b_other = hop(b_mine, 2, "dp")
+    (a_pair,) = call(pair_kernel, [((2,) + a_mine.shape, BF)], (a_mine, after(a_other, b_mine)), us=0.1, limit=4, name="pair")
+    a_last = hop(a_pair, 2, "dp")
+    pruned_2, student_2 = after(pruned_2, a_pair), after(student_2, a_pair)
     pruneds = (pruned_rows, pruned_1, pruned_2, hop(pruned_2, 1))
-
-    uw, iw = call(weights_kernel, [((w, d), F32), ((d, w), F32)], (ids, after(a_parts[0], grad_2, pruned_2), *a_parts[1:], *b_parts), prefetch=1, us=1, limit=16, name="weights")
-    (c_pair,) = call(last_kernel, [((n_c // 2 + 16, d), BF)], (c_mine, after(c_other, uw)), us=0.1, limit=8, name="last")
-    c_last = hop(c_pair, 1, "dp")
+    students = (student_rows, student_1, student_2, hop(student_2, 1))
+    (b_pair,) = call(last_kernel, [((n_b // 2 + 16, d), BF)], (b_mine, after(b_other, student_2, pruned_2, c_last)), us=0.1, limit=4, name="last")
+    b_last = hop(b_pair, 1, "dp")
     outs = call(
         spread_kernel,
         [((blocks, length, d), BF)] * 3,
-        (ids, after(students[0], c_pair), *students[1:], *pruneds, *grads),
-        prefetch=1, specs=[VM] * 12, out_specs=[ANY] * 3, scratch=[pltpu.SemaphoreType.DMA((12 * blocks,))], us=1, limit=16, name="spread",
+        (ids, after(students[0], b_pair), *students[1:], *pruneds, *grads),
+        prefetch=1, specs=[VM] * 12, out_specs=[ANY] * 3, scratch=[pltpu.SemaphoreType.DMA((12 * blocks,))], us=0.1, limit=4, name="spread",
     )
     student, pruned, tokens_grad = (o.reshape(rows, d) for o in outs)
-    qw, kw, vw, ow, qb, vb, ob, fg, fs, ib, ub, sg, ss, ha, ua, da, me, pe = call(
+    qw, kw, vw, ow, qb, vb, ob, fg, fs, ub, sg, ss, ha, da, me, live = call(
         final_kernel,
         [((c, d), F32), ((c, d), F32), ((c, d), F32), ((c, d), F32), ((c,), F32), ((c,), F32), ((d,), F32), ((d,), F32), ((d,), F32),
-         ((w,), F32), ((d,), F32), ((d,), F32), ((d,), F32), ((heads,), F32), ((w,), F32), ((d,), F32), ((1,), F32), ((1,), F32)],
-        (ids, consts, c_pair, after(c_last, outs[0])),
-        prefetch=1, specs=[VM] * 3, out_specs=[VM] * 13 + [SM] + [VM] * 2 + [SM] * 2,
-        scratch=[pltpu.VMEM((n_c, d), F32)], us=0.1, limit=16, name="final",
+         ((d,), F32), ((d,), F32), ((d,), F32), ((heads,), F32), ((d,), F32), ((1,), F32), ((1,), F32)],
+        (ids, consts, c_mine, c_other, after(c_last, outs[0])),
+        prefetch=1, specs=[VM] * 4, out_specs=[VM] * 12 + [SM] + [VM] + [SM] * 2,
+        scratch=[pltpu.VMEM((n_c, d), F32)], us=0.1, limit=8, name="final",
+    )
+    (uw,) = call(outer_out_kernel, [((w, d), F32)], (ids, a_mine, a_other, after(a_last, qw)), prefetch=1, us=0.1, limit=8, name="outer_out")
+    iw, ib, ua, pe = call(
+        inner_out_kernel, [((d, w), F32), ((w,), F32), ((w,), F32), ((1,), F32)], (ids, consts, b_pair, after(b_last, uw), live), prefetch=1,
+        specs=[VM] * 3 + [SM], out_specs=[VM] * 3 + [SM], scratch=[pltpu.VMEM((n_b, w), F32)], us=0.1, limit=12, name="inner_out",
     )
     return (
         student, pruned, tokens_grad, qw.T, qb, kw.T, vw.T, vb, ow, ob, fg, fs, iw, ib, uw, ub, sg, ss, ha, ua, da, me.reshape(()), pe.reshape(()),

time: 240 us -> 236 us (0.983)
  waiting for transfers between devices: 91.3 us -> 84.7 us
    ppermute x55, waiting for transfers between devices: 91.3 us -> 84.7 us  [hop(): return lax.ppermute(x, axis, [(i, i ^ mask) for i in range(size)])]
    pallas_call x20 -> x23, Pallas kernels: 92.5 us -> 94.3 us  [call(): pl.pallas_call(kernel, out_shape=[pltpu.HBM(*o[:2]) if len(o) > 2 else ja...]
  transfers between devices with their start and end apart: 55 -> 55, of which waited for: 22 -> 20; matrix products, arithmetic and copies ran while one was open for 1% -> 1% of each run, Pallas kernels for 38% -> 39%
where the time goes in v2:
time: 236 us; the launch traced here: 231 us
  Pallas kernels  94.3 us (40%)
  waiting for transfers between devices  84.7 us (36%)
  starting transfers between devices  48 us (20%)
    pallas_call x23, Pallas kernels, call(): pl.pallas_call(kernel, out_shape=[pltpu.HBM(*o[:2]) if len(o) > 2 else ja...  94.3 us
    ppermute x55, waiting for transfers between devices, hop(): return lax.ppermute(x, axis, [(i, i ^ mask) for i in range(size)])  84.7 us
    ppermute x55, starting transfers between devices, hop(): return lax.ppermute(x, axis, [(i, i ^ mask) for i in range(size)])  48 us
  transfers between devices with their start and end apart: 55, of which 20 were waited for; matrix products, arithmetic and copies ran while one was open for 1% of the time, Pallas kernels for 39%

profile of v2, /device:TPU:0, one launch (start us, length us, event | category | flops | bytes accessed | tf_op | source)
XLA Modules:
  0.0 231.0 jit_solution(12897522570438005155)
XLA Ops:
  1.8 3.0 %collective-permute-start.7 = (bf16[768,384]{1,0:T(8,128)(2,1)S(1)}, bf16[768,384]{1,0:T(8,128)(2,1)S(1)}, u32[]{:S(2)}, u32[]{:S(2)}) collective-permute-start(bf16[768,384]{1,0:T(8,128)(2,1)S(1)} %constant_dynamic-slice_fusion), channel_id=1, source_target_pairs={{0,2},{1,3},{2,0},{3,1},{4,6},{5,7},{6,4},{7,5},{8,10},{9,11},{10,... | collective-permute-start | bytes 1769480 | tf_op jit(solution)/shard_map/ppermute | solution.py:652
  6.4 11.3 %attend.1 = (bf16[3,192,128]{2,1,0:T(8,128)(2,1)S(1)}, bf16[3,192,128]{2,1,0:T(8,128)(2,1)S(1)}, bf16[2,3,192,128]{3,2,1,0:T(8,128)(2,1)S(1)}, bf16[3,3,512,512]...) custom-call(s32[5]{0:T(128)S(1)} %stack.19.ids.h_ref, ...), custom_call_target="tpu_custom_call" | custom-call | flops 4499999744 | tf_op jit(solution)/shard_map/attend/pallas_call | solution.py:59
  21.6 4.8 %collective-permute-done.4.s2.refs_8_.refs_14_ = bf16[224,768]{1,0:T(8,128)(2,1)S(1)} collective-permute-done((bf16[224,768]{1,0:T(8,128)(2,1)S(1)}, bf16[224,768]{1,0:T(8,128)(2,1)S(1)}, u32[]{:S(2)}, u32[]{:S(2)}) %collective-permute-start.4) | collective-permute-done | bytes 344096 | tf_op jit(solution)/shard_map/ppermute | solution.py:652
  26.9 5.0 %collective-permute-done.1.xr = bf16[2,3,192,128]{3,2,1,0:T(8,128)(2,1)S(1)} collective-permute-done((bf16[2,3,192,128]{3,2,1,0:T(8,128)(2,1)S(1)}, bf16[2,3,192,128]{3,2,1,0:T(8,128)(2,1)S(1)}, u32[]{:S(2)}, u32[]{:S(2)}) %collective-permute-start.1) | collective-permute-done | bytes 294944 | tf_op jit(solution)/shard_map/ppermute | solution.py:652
  34.0 3.0 %first.1 = (bf16[384,768]{1,0:T(8,128)(2,1)S(1)}, f32[384,768]{1,0:T(8,128)S(1)}, f32[384,128]{1,0:T(8,128)S(1)}, f32[384,768]{1,0:T(8,128)S(1)}, bf16[4,384,192]{2,1,0:T(8,128)(2,1)S(1)}) custom-call(s32[5]{0:T(128)S(1)} %stack.19.ids.h_ref, bf16[3,192,128]{2,1,0:T(8,128)(2,1)S(1)} %get-tuple-element.148.c0, ...), custom_call_target="tpu_custom_call" | custom-call | flops 2000000000 | tf_op jit(solution)/shard_map/first/pallas_call | solution.py:59
  37.5 3.2 %hard_first.1 = (bf16[384,768]{1,0:T(8,128)(2,1)S(1)}, f32[384,768]{1,0:T(8,128)S(1)}) custom-call(s32[5]{0:T(128)S(1)} %stack.19.ids.h_ref, bf16[3,192,128]{2,1,0:T(8,128)(2,1)S(1)} %get-tuple-element.148.c0, bf16[3,192,128]{2,1,0:T(8,128)(2,1)S(1)} %collective-permute-done.c1, bf16[2,3,192,128]{3,2,1,0:T(8,128)(2,1)S(1)} %collective-permute-done.1.xr, ...), custom_call_target="tpu_custom_call" | custom-call | flops 2000000000 | tf_op jit(solution)/shard_map/hard_first/pallas_call | solution.py:59
  40.7 7.1 %collective-permute-done.12.refs_2_.refs_8_ = bf16[384,768]{1,0:T(8,128)(2,1)S(1)} collective-permute-done((bf16[384,768]{1,0:T(8,128)(2,1)S(1)}, bf16[384,768]{1,0:T(8,128)(2,1)S(1)}, u32[]{:S(2)}, u32[]{:S(2)}) %collective-permute-start.12) | collective-permute-done | bytes 589856 | tf_op jit(solution)/shard_map/ppermute | solution.py:652
  49.5 6.5 %inner.1 = (bf16[4,384,768]{2,1,0:T(8,128)(2,1)S(1)}, bf16[4,384,768]{2,1,0:T(8,128)(2,1)S(1)}) custom-call(s32[5]{0:T(128)S(1)} %stack.19.ids.h_ref, bf16[384,768]{1,0:T(8,128)(2,1)S(1)} %get-tuple-element.171.first_low.f0, bf16[768,768]{1,0:T(8,128)(2,1)S(1)} %copy-done.2, bf16[768,768]{1,0:T(8,128)(2,1)S(1)} %collective-permute-done.6.refs_1_, ...), custom_call_target="tpu_custom_call" | custom-call | flops 4000000000 | tf_op jit(solution)/shard_map/inner/pallas_call | solution.py:59
  56.1 5.8 %hard_inner.1.hidden = bf16[4,384,768]{2,1,0:T(8,128)(2,1)S(1)} custom-call(s32[5]{0:T(128)S(1)} %stack.19.ids.h_ref, bf16[384,768]{1,0:T(8,128)(2,1)S(1)} %get-tuple-element.157.first_low, bf16[768,768]{1,0:T(8,128)(2,1)S(1)} %copy-done.2, bf16[768,768]{1,0:T(8,128)(2,1)S(1)} %collective-permute-done.6.refs_1_, ...), custom_call_target="tpu_custom_call" | custom-call | flops 4000000000 | tf_op jit(solution)/shard_map/hard_inner/pallas_call | solution.py:59
  65.0 5.4 %second.1 = (bf16[384,768]{1,0:T(8,128)(2,1)S(1)}, f32[384,768]{1,0:T(8,128)S(1)}, bf16[384,768]{1,0:T(8,128)(2,1)S(1)}, f32[8,768]{1,0:T(8,128)S(1)}) custom-call(s32[5]{0:T(128)S(1)} %stack.19.ids.h_ref, bf16[4,384,768]{2,1,0:T(8,128)(2,1)S(1)} %get-tuple-element.153.hidden, f32[384,768]{1,0:T(8,128)S(1)} %get-tuple-element.154.normed.refs_17_, ...), custom_call_target="tpu_custom_call" | custom-call | flops 3000000000 | tf_op jit(solution)/shard_map/second/pallas_call | solution.py:59
  70.4 9.4 %back.1 = (bf16[3,192,128]{2,1,0:T(8,128)(2,1)S(1)}, bf16[3,192,128]{2,1,0:T(8,128)(2,1)S(1)}, bf16[2,3,192,128]{3,2,1,0:T(8,128)(2,1)S(1)}, bf16[2,208,768]{2,1...) custom-call(s32[5]{0:T(128)S(1)} %stack.19.ids.h_ref, ...), custom_call_target="tpu_custom_call" | custom-call | flops 6499999744 | tf_op jit(solution)/shard_map/back/pallas_call | solution.py:59
  81.9 5.7 %units.1 = (bf16[1536,768]{1,0:T(8,128)(2,1)S(1)}, bf16[1536,768]{1,0:T(8,128)(2,1)S(1)}) custom-call(bf16[384,768]{1,0:T(8,128)(2,1)S(1)} %get-tuple-element.171.first_low.f0, bf16[384,768]{1,0:T(8,128)(2,1)S(1)} %collective-permute-done.18.f1, bf16[384,768]{1,0:T(8,128)(2,1)S(1)} %collective-permute-done.19.fx, ...), custom_call_target="tpu_custom_call" | custom-call | flops 3000000000 | tf_op jit(solution)/shard_map/units/pallas_call | solution.py:59
  92.1 16.0 %attend_back.1 = (bf16[2,384,768]{2,1,0:T(8,128)(2,1)S(1)}, bf16[2,384,768]{2,1,0:T(8,128)(2,1)S(1)}, f32[576,768]{1,0:T(8,128)S(1)}, f32[16,768]{1,0:T(8,128)S(1)}) custom-call(s32[5]{0:T(128)S(1)} %stack.19.ids.h_ref, bf16[3,192,128]{2,1,0:T(8,128)(2,1)S(1)} %get-tuple-element.168.g0, bf16[3,192,128]{2,1,0:T(8,128)(2,1)S(1)} %collective-permute-done.16.g1, ...), custom_call_target="tpu_custom_call" | custom-call | flops 7500000256 | tf_op jit(solution)/shard_map/attend_back/pallas_call | solution.py:59
  108.1 4.0 %collective-permute-done.24.gx = bf16[384,768]{1,0:T(8,128)(2,1)S(1)} collective-permute-done((bf16[384,768]{1,0:T(8,128)(2,1)S(1)}, bf16[384,768]{1,0:T(8,128)(2,1)S(1)}, u32[]{:S(2)}, u32[]{:S(2)}) %collective-permute-start.24) | collective-permute-done | bytes 589856 | tf_op jit(solution)/shard_map/ppermute | solution.py:652
  116.8 2.5 %near_grad.1 = (f32[768,768]{1,0:T(8,128)S(1)}, bf16[768,768]{1,0:T(8,128)(2,1)S(1)}, f32[2,8,768]{2,1,0:T(8,128)S(1)}) custom-call(bf16[384,768]{1,0:T(8,128)(2,1)S(1)} %get-tuple-element.194.gffn.g0, bf16[384,768]{1,0:T(8,128)(2,1)S(1)} %collective-permute-done.26.g1, bf16[768,768]{1,0:T(8,128)(2,1)S(1)} %copy-done, ...), custom_call_target="tpu_custom_call" | custom-call | flops 2500000000 | tf_op jit(solution)/shard_map/near_grad/pallas_call | solution.py:59
  121.1 2.1 outer_grad.1
  124.9 4.4 %inner_grad.1 = (bf16[2,208,768]{2,1,0:T(8,128)(2,1)S(1)}, bf16[2,208,768]{2,1,0:T(8,128)(2,1)S(1)}) custom-call(s32[5]{0:T(128)S(1)} %stack.19.ids.h_ref, bf16[384,768]{1,0:T(8,128)(2,1)S(1)} %get-tuple-element.171.first_low.f0, bf16[384,768]{1,0:T(8,128)(2,1)S(1)} %collective-permute-done.18.f1, bf16[384,768]{1,0:T(8,128)(2,1)S(1)} %collective-permute-done.19.fx, ...), custom_call_target="tpu_custom_call" | custom-call | flops 2000000000 | tf_op jit(solution)/shard_map/inner_grad/pallas_call | solution.py:59
  133.8 4.9 %hard.1 = (bf16[384,768]{1,0:T(8,128)(2,1)S(1)}, f32[8,128]{1,0:T(8,128)S(1)}) custom-call(s32[5]{0:T(128)S(1)} %stack.19.ids.h_ref, bf16[4,384,768]{2,1,0:T(8,128)(2,1)S(1)} %hard_inner.1.hidden, f32[384,768]{1,0:T(8,128)S(1)} %get-tuple-element.207.normed, bf16[768,768]{1,0:T(8,128)(2,1)S(1)} %copy-done, ...), custom_call_target="tpu_custom_call" | custom-call | flops 50000000 | tf_op jit(solution)/shard_map/hard/pallas_call | solution.py:59
  141.2 6.6 %collective-permute-done.32 = bf16[2,208,768]{2,1,0:T(8,128)(2,1)S(1)} collective-permute-done((bf16[2,208,768]{2,1,0:T(8,128)(2,1)S(1)}, bf16[2,208,768]{2,1,0:T(8,128)(2,1)S(1)}, u32[]{:S(2)}, u32[]{:S(2)}) %collective-permute-start.32) | collective-permute-done | bytes 639008 | tf_op jit(solution)/shard_map/ppermute | solution.py:652
  149.7 2.7 %collective-permute-start.34 = (bf16[208,768]{1,0:T(8,128)(2,1)S(1)}, bf16[208,768]{1,0:T(8,128)(2,1)S(1)}, u32[]{:S(2)}, u32[]{:S(2)}) collective-permute-start(bf16[208,768]{1,0:T(8,128)(2,1)S(1)} %fusion.2), channel_id=1, source_target_pairs={{0,16},{4,20},{8,24},{12,28},{16,0},{20,4},{24,8},{28,12},{1,17},{... | collective-permute-start | bytes 958472 | tf_op jit(solution)/shard_map/ppermute | solution.py:652
  152.9 2.7 %collective-permute-start.41 = (bf16[192,768]{1,0:T(8,128)(2,1)S(1)}, bf16[192,768]{1,0:T(8,128)(2,1)S(1)}, u32[]{:S(2)}, u32[]{:S(2)}) collective-permute-start(bf16[192,768]{1,0:T(8,128)(2,1)S(1)} %fusion.5), channel_id=1, source_target_pairs={{0,16},{4,20},{8,24},{12,28},{16,0},{20,4},{24,8},{28,12},{1,17},{... | collective-permute-start | bytes 884744 | tf_op jit(solution)/shard_map/ppermute | solution.py:652
  157.0 2.1 collective-permute-done.37
  159.2 2.1 collective-permute-done.35.got
  164.1 16.8 %collective-permute-done.34 = bf16[208,768]{1,0:T(8,128)(2,1)S(1)} collective-permute-done((bf16[208,768]{1,0:T(8,128)(2,1)S(1)}, bf16[208,768]{1,0:T(8,128)(2,1)S(1)}, u32[]{:S(2)}, u32[]{:S(2)}) %collective-permute-start.34) | collective-permute-done | bytes 319520 | tf_op jit(solution)/shard_map/ppermute | solution.py:652
  182.7 4.7 %collective-permute-done.41 = bf16[192,768]{1,0:T(8,128)(2,1)S(1)} collective-permute-done((bf16[192,768]{1,0:T(8,128)(2,1)S(1)}, bf16[192,768]{1,0:T(8,128)(2,1)S(1)}, u32[]{:S(2)}, u32[]{:S(2)}) %collective-permute-start.41) | collective-permute-done | bytes 294944 | tf_op jit(solution)/shard_map/ppermute | solution.py:652
  189.0 5.9 %collective-permute-done.40.other.co = bf16[208,768]{1,0:T(8,128)(2,1)S(1)} collective-permute-done((bf16[208,768]{1,0:T(8,128)(2,1)S(1)}, bf16[208,768]{1,0:T(8,128)(2,1)S(1)}, u32[]{:S(2)}, u32[]{:S(2)}) %collective-permute-start.40) | collective-permute-done | bytes 319520 | tf_op jit(solution)/shard_map/ppermute | solution.py:652
  197.4 10.3 %collective-permute-done.42.other = bf16[224,768]{1,0:T(8,128)(2,1)S(1)} collective-permute-done((bf16[224,768]{1,0:T(8,128)(2,1)S(1)}, bf16[224,768]{1,0:T(8,128)(2,1)S(1)}, u32[]{:S(2)}, u32[]{:S(2)}) %collective-permute-start.42) | collective-permute-done | bytes 344096 | tf_op jit(solution)/shard_map/ppermute | solution.py:652
  213.1 3.7 %spread.1 = (bf16[3,512,768]{2,1,0:T(8,128)(2,1)}, bf16[3,512,768]{2,1,0:T(8,128)(2,1)}, bf16[3,512,768]{2,1,0:T(8,128)(2,1)}) custom-call(s32[5]{0:T(128)S(1)} %stack.19.ids.h_ref, bf16[384,768]{1,0:T(8,128)(2,1)S(1)} %get-tuple-element.230.refs_0_, bf16[384,768]{1,0:T(8,128)(2,1)S(1)} %collective-permute-done.47.refs_1_, ...), custom_call_target="tpu_custom_call" | custom-call | flops 50000000 | tf_op jit(solution)/shard_map/spread/pallas_call | solution.py:59
  216.8 2.2 final.1
  219.1 6.6 %collective-permute-done.54.q = bf16[2,192,768]{2,1,0:T(8,128)(2,1)S(1)} collective-permute-done((bf16[2,192,768]{2,1,0:T(8,128)(2,1)S(1)}, bf16[2,192,768]{2,1,0:T(8,128)(2,1)S(1)}, u32[]{:S(2)}, u32[]{:S(2)}) %collective-permute-start.54) | collective-permute-done | bytes 589856 | tf_op jit(solution)/shard_map/ppermute | solution.py:652
  225.7 2.1 outer_out.1
  227.8 3.0 %inner_out.1 = (f32[768,768]{1,0:T(8,128)}, f32[768]{0:T(1024)}, f32[768]{0:T(1024)}, f32[1]{0:T(128)}) custom-call(s32[5]{0:T(128)S(1)} %stack.19.ids.h_ref, f32[16,768]{1,0:T(8,128)S(1)} %get-tuple-element.141.consts.refs_8_.refs_23_, bf16[432,768]{1,0:T(8,128)(2,1)S(1)} %last.1.pair, bf16[432,768]{1,0:T(8,128)(2,1)S(1)} %collective-permute-done.53.q, ...), custom_call_target="tpu_custom_call" | custom-call | flops 50000000 | tf_op jit(solution)/shard_map/inner_out/pallas_call | solution.py:59
  (132 shorter events, 54.0 us)
Async XLA Ops:
  1.8 18.0 %collective-permute-start.7 = (bf16[768,384]{1,0:T(8,128)(2,1)S(1)}, bf16[768,384]{1,0:T(8,128)(2,1)S(1)}, u32[]{:S(2)}, u32[]{:S(2)}) collective-permute-start(bf16[768,384]{1,0:T(8,128)(2,1)S(1)} %constant_dynamic-slice_fusion), channel_id=1, source_target_pairs={{0,2},{1,3},{2,0},{3,1},{4,6},{5,7},{6,4},{7,5},{8,10},{9,11},{10,... | collective-permute-start | bytes 1769480 | tf_op jit(solution)/shard_map/ppermute | solution.py:652
  6.2 20.2 %collective-permute-start.4 = (bf16[224,768]{1,0:T(8,128)(2,1)S(1)}, bf16[224,768]{1,0:T(8,128)(2,1)S(1)}, u32[]{:S(2)}, u32[]{:S(2)}) collective-permute-start(bf16[224,768]{1,0:T(8,128)(2,1)S(1)} %get-tuple-element.145.s0.refs_6_.refs_12_), channel_id=1, source_target_pairs={{0,2},{1,3},{2,0},{3,1},{4,6},{5,7},{6,4},{7,5},{8,10},{9,11},{10,... | collective-permute-start | bytes 1032200 | tf_op jit(solution)/shard_map/ppermute | solution.py:652
  17.7 14.1 %collective-permute-start.1 = (bf16[2,3,192,128]{3,2,1,0:T(8,128)(2,1)S(1)}, bf16[2,3,192,128]{3,2,1,0:T(8,128)(2,1)S(1)}, u32[]{:S(2)}, u32[]{:S(2)}) collective-permute-start(bf16[2,3,192,128]{3,2,1,0:T(8,128)(2,1)S(1)} %get-tuple-element.144), channel_id=1, source_target_pairs={{0,2},{1,3},{2,0},{3,1},{4,6},{5,7},{6,4},{7,5},{8,10},{9,11},{10,... | collective-permute-start | bytes 884744 | tf_op jit(solution)/shard_map/ppermute | solution.py:652
  19.8 17.2 %collective-permute-start.8 = (bf16[768,384]{1,0:T(8,128)(2,1)S(1)}, bf16[768,384]{1,0:T(8,128)(2,1)S(1)}, u32[]{:S(2)}, u32[]{:S(2)}) collective-permute-start(bf16[768,384]{1,0:T(8,128)(2,1)S(1)} %collective-permute-done.7.refs_2_), channel_id=1, source_target_pairs={{0,4},{4,0},{8,12},{12,8},{16,20},{20,16},{24,28},{28,24},{1,5},{5... | collective-permute-start | bytes 1769480 | tf_op jit(solution)/shard_map/ppermute | solution.py:652
  21.4 28.1 %collective-permute-start.6 = (bf16[768,768]{1,0:T(8,128)(2,1)S(1)}, bf16[768,768]{1,0:T(8,128)(2,1)S(1)}, u32[]{:S(2)}, u32[]{:S(2)}) collective-permute-start(bf16[768,768]{1,0:T(8,128)(2,1)S(1)} %copy-done.2), channel_id=1, source_target_pairs={{0,1},{1,0},{2,3},{3,2},{4,5},{5,4},{6,7},{7,6},{8,9},{9,8},{10,11... | collective-permute-start | bytes 3538952 | tf_op jit(solution)/shard_map/ppermute | solution.py:652
  32.0 15.8 %collective-permute-start.12 = (bf16[384,768]{1,0:T(8,128)(2,1)S(1)}, bf16[384,768]{1,0:T(8,128)(2,1)S(1)}, u32[]{:S(2)}, u32[]{:S(2)}) collective-permute-start(bf16[384,768]{1,0:T(8,128)(2,1)S(1)} %get-tuple-element.262), channel_id=1, source_target_pairs={{0,2},{1,3},{2,0},{3,1},{4,6},{5,7},{6,4},{7,5},{8,10},{9,11},{10,... | collective-permute-start | bytes 1769480 | tf_op jit(solution)/shard_map/ppermute | solution.py:652
  33.8 15.7 %collective-permute-start.9 = (bf16[768,384]{1,0:T(8,128)(2,1)S(1)}, bf16[768,384]{1,0:T(8,128)(2,1)S(1)}, u32[]{:S(2)}, u32[]{:S(2)}) collective-permute-start(bf16[768,384]{1,0:T(8,128)(2,1)S(1)} %collective-permute-done.7.refs_2_), channel_id=1, source_target_pairs={{0,1},{1,0},{2,3},{3,2},{4,5},{5,4},{6,7},{7,6},{8,9},{9,8},{10,11... | collective-permute-start | bytes 1769480 | tf_op jit(solution)/shard_map/ppermute | solution.py:652
  37.3 27.7 %collective-permute-start.11 = (bf16[768,768]{1,0:T(8,128)(2,1)S(1)}, bf16[768,768]{1,0:T(8,128)(2,1)S(1)}, u32[]{:S(2)}, u32[]{:S(2)}) collective-permute-start(bf16[768,768]{1,0:T(8,128)(2,1)S(1)} %copy-done), channel_id=1, source_target_pairs={{0,1},{1,0},{2,3},{3,2},{4,5},{5,4},{6,7},{7,6},{8,9},{9,8},{10,11... | collective-permute-start | bytes 3538952 | tf_op jit(solution)/shard_map/ppermute | solution.py:652
  47.8 15.0 %collective-permute-start.13 = (bf16[384,768]{1,0:T(8,128)(2,1)S(1)}, bf16[384,768]{1,0:T(8,128)(2,1)S(1)}, u32[]{:S(2)}, u32[]{:S(2)}) collective-permute-start(bf16[384,768]{1,0:T(8,128)(2,1)S(1)} %get-tuple-element.261), channel_id=1, source_target_pairs={{0,2},{1,3},{2,0},{3,1},{4,6},{5,7},{6,4},{7,5},{8,10},{9,11},{10,... | collective-permute-start | bytes 1769480 | tf_op jit(solution)/shard_map/ppermute | solution.py:652
  49.5 15.5 %collective-permute-start.14 = (bf16[384,768]{1,0:T(8,128)(2,1)S(1)}, bf16[384,768]{1,0:T(8,128)(2,1)S(1)}, u32[]{:S(2)}, u32[]{:S(2)}) collective-permute-start(bf16[384,768]{1,0:T(8,128)(2,1)S(1)} %collective-permute-done.12.refs_2_.refs_8_), channel_id=1, source_target_pairs={{0,1},{1,0},{2,3},{3,2},{4,5},{5,4},{6,7},{7,6},{8,9},{9,8},{10,11... | collective-permute-start | bytes 1769480 | tf_op jit(solution)/shard_map/ppermute | solution.py:652
  62.7 19.1 %collective-permute-start.18 = (bf16[384,768]{1,0:T(8,128)(2,1)S(1)}, bf16[384,768]{1,0:T(8,128)(2,1)S(1)}, u32[]{:S(2)}, u32[]{:S(2)}) collective-permute-start(bf16[384,768]{1,0:T(8,128)(2,1)S(1)} %get-tuple-element.171.first_low.f0), channel_id=1, source_target_pairs={{0,1},{1,0},{2,3},{3,2},{4,5},{5,4},{6,7},{7,6},{8,9},{9,8},{10,11... | collective-permute-start | bytes 1769480 | tf_op jit(solution)/shard_map/ppermute | solution.py:652
  63.2 16.6 %collective-permute-start.19 = (bf16[384,768]{1,0:T(8,128)(2,1)S(1)}, bf16[384,768]{1,0:T(8,128)(2,1)S(1)}, u32[]{:S(2)}, u32[]{:S(2)}) collective-permute-start(bf16[384,768]{1,0:T(8,128)(2,1)S(1)} %get-tuple-element.171.first_low.f0), channel_id=1, source_target_pairs={{0,2},{1,3},{2,0},{3,1},{4,6},{5,7},{6,4},{7,5},{8,10},{9,11},{10,... | collective-permute-start | bytes 1769480 | tf_op jit(solution)/shard_map/ppermute | solution.py:652
  90.0 22.2 %collective-permute-start.23 = (bf16[208,768]{1,0:T(8,128)(2,1)S(1)}, bf16[208,768]{1,0:T(8,128)(2,1)S(1)}, u32[]{:S(2)}, u32[]{:S(2)}) collective-permute-start(bf16[208,768]{1,0:T(8,128)(2,1)S(1)} %get-tuple-element.259), channel_id=1, source_target_pairs={{0,2},{1,3},{2,0},{3,1},{4,6},{5,7},{6,4},{7,5},{8,10},{9,11},{10,... | collective-permute-start | bytes 958472 | tf_op jit(solution)/shard_map/ppermute | solution.py:652
  91.6 20.6 %collective-permute-start.24 = (bf16[384,768]{1,0:T(8,128)(2,1)S(1)}, bf16[384,768]{1,0:T(8,128)(2,1)S(1)}, u32[]{:S(2)}, u32[]{:S(2)}) collective-permute-start(bf16[384,768]{1,0:T(8,128)(2,1)S(1)} %get-tuple-element.194.gffn.g0), channel_id=1, source_target_pairs={{0,2},{1,3},{2,0},{3,1},{4,6},{5,7},{6,4},{7,5},{8,10},{9,11},{10,... | collective-permute-start | bytes 1769480 | tf_op jit(solution)/shard_map/ppermute | solution.py:652
  113.7 16.7 %collective-permute-start.28 = (bf16[2,208,768]{2,1,0:T(8,128)(2,1)S(1)}, bf16[2,208,768]{2,1,0:T(8,128)(2,1)S(1)}, u32[]{:S(2)}, u32[]{:S(2)}) collective-permute-start(bf16[2,208,768]{2,1,0:T(8,128)(2,1)S(1)} %get-tuple-element.198), channel_id=1, source_target_pairs={{0,4},{4,0},{8,12},{12,8},{16,20},{20,16},{24,28},{28,24},{1,5},{5... | collective-permute-start | bytes 1916936 | tf_op jit(solution)/shard_map/ppermute | solution.py:652
  119.5 19.1 %collective-permute-start.27 = (bf16[384,768]{1,0:T(8,128)(2,1)S(1)}, bf16[384,768]{1,0:T(8,128)(2,1)S(1)}, u32[]{:S(2)}, u32[]{:S(2)}) collective-permute-start(bf16[384,768]{1,0:T(8,128)(2,1)S(1)} %fusion.4), channel_id=1, source_target_pairs={{0,2},{1,3},{2,0},{3,1},{4,6},{5,7},{6,4},{7,5},{8,10},{9,11},{10,... | collective-permute-start | bytes 1769480 | tf_op jit(solution)/shard_map/ppermute | solution.py:652
  123.3 17.2 %collective-permute-start.33 = (bf16[2,192,768]{2,1,0:T(8,128)(2,1)S(1)}, bf16[2,192,768]{2,1,0:T(8,128)(2,1)S(1)}, u32[]{:S(2)}, u32[]{:S(2)}) collective-permute-start(bf16[2,192,768]{2,1,0:T(8,128)(2,1)S(1)} %get-tuple-element.211), channel_id=1, source_target_pairs={{0,8},{4,12},{8,0},{12,4},{16,24},{20,28},{24,16},{28,20},{1,9},{5... | collective-permute-start | bytes 1769480 | tf_op jit(solution)/shard_map/ppermute | solution.py:652
  130.5 17.3 %collective-permute-start.32 = (bf16[2,208,768]{2,1,0:T(8,128)(2,1)S(1)}, bf16[2,208,768]{2,1,0:T(8,128)(2,1)S(1)}, u32[]{:S(2)}, u32[]{:S(2)}) collective-permute-start(bf16[2,208,768]{2,1,0:T(8,128)(2,1)S(1)} %get-tuple-element.210), channel_id=1, source_target_pairs={{0,4},{4,0},{8,12},{12,8},{16,20},{20,16},{24,28},{28,24},{1,5},{5... | collective-permute-start | bytes 1916936 | tf_op jit(solution)/shard_map/ppermute | solution.py:652
  132.1 17.5 %collective-permute-start.31 = (bf16[208,768]{1,0:T(8,128)(2,1)S(1)}, bf16[208,768]{1,0:T(8,128)(2,1)S(1)}, u32[]{:S(2)}, u32[]{:S(2)}) collective-permute-start(bf16[208,768]{1,0:T(8,128)(2,1)S(1)} %fusion.8), channel_id=1, source_target_pairs={{0,8},{4,12},{8,0},{12,4},{16,24},{20,28},{24,16},{28,20},{1,9},{5... | collective-permute-start | bytes 958472 | tf_op jit(solution)/shard_map/ppermute | solution.py:652
  138.9 42.2 %collective-permute-start.30 = (bf16[384,768]{1,0:T(8,128)(2,1)S(1)}, bf16[384,768]{1,0:T(8,128)(2,1)S(1)}, u32[]{:S(2)}, u32[]{:S(2)}) collective-permute-start(bf16[384,768]{1,0:T(8,128)(2,1)S(1)} %fusion.1.refs_8_), channel_id=1, source_target_pairs={{0,2},{1,3},{2,0},{3,1},{4,6},{5,7},{6,4},{7,5},{8,10},{9,11},{10,... | collective-permute-start | bytes 1769480 | tf_op jit(solution)/shard_map/ppermute | solution.py:652
  147.9 13.4 %collective-permute-start.35 = (bf16[208,768]{1,0:T(8,128)(2,1)S(1)}, bf16[208,768]{1,0:T(8,128)(2,1)S(1)}, u32[]{:S(2)}, u32[]{:S(2)}) collective-permute-start(bf16[208,768]{1,0:T(8,128)(2,1)S(1)} %get-tuple-element.258), channel_id=1, source_target_pairs={{0,8},{4,12},{8,0},{12,4},{16,24},{20,28},{24,16},{28,20},{1,9},{5... | collective-permute-start | bytes 958472 | tf_op jit(solution)/shard_map/ppermute | solution.py:652
  149.7 31.2 %collective-permute-start.34 = (bf16[208,768]{1,0:T(8,128)(2,1)S(1)}, bf16[208,768]{1,0:T(8,128)(2,1)S(1)}, u32[]{:S(2)}, u32[]{:S(2)}) collective-permute-start(bf16[208,768]{1,0:T(8,128)(2,1)S(1)} %fusion.2), channel_id=1, source_target_pairs={{0,16},{4,20},{8,24},{12,28},{16,0},{20,4},{24,8},{28,12},{1,17},{... | collective-permute-start | bytes 958472 | tf_op jit(solution)/shard_map/ppermute | solution.py:652
  152.9 34.5 %collective-permute-start.41 = (bf16[192,768]{1,0:T(8,128)(2,1)S(1)}, bf16[192,768]{1,0:T(8,128)(2,1)S(1)}, u32[]{:S(2)}, u32[]{:S(2)}) collective-permute-start(bf16[192,768]{1,0:T(8,128)(2,1)S(1)} %fusion.5), channel_id=1, source_target_pairs={{0,16},{4,20},{8,24},{12,28},{16,0},{20,4},{24,8},{28,12},{1,17},{... | collective-permute-start | bytes 884744 | tf_op jit(solution)/shard_map/ppermute | solution.py:652
  161.3 35.3 %collective-permute-start.45 = (bf16[384,768]{1,0:T(8,128)(2,1)S(1)}, bf16[384,768]{1,0:T(8,128)(2,1)S(1)}, u32[]{:S(2)}, u32[]{:S(2)}) collective-permute-start(bf16[384,768]{1,0:T(8,128)(2,1)S(1)} %get-tuple-element.227.refs_4_), channel_id=1, source_target_pairs={{0,2},{1,3},{2,0},{3,1},{4,6},{5,7},{6,4},{7,5},{8,10},{9,11},{10,... | collective-permute-start | bytes 1769480 | tf_op jit(solution)/shard_map/ppermute | solution.py:652
  163.5 33.1 %collective-permute-start.39 = (bf16[224,768]{1,0:T(8,128)(2,1)S(1)}, bf16[224,768]{1,0:T(8,128)(2,1)S(1)}, u32[]{:S(2)}, u32[]{:S(2)}) collective-permute-start(bf16[224,768]{1,0:T(8,128)(2,1)S(1)} %third.1), channel_id=1, source_target_pairs={{0,16},{4,20},{8,24},{12,28},{16,0},{20,4},{24,8},{28,12},{1,17},{... | collective-permute-start | bytes 1032200 | tf_op jit(solution)/shard_map/ppermute | solution.py:652
  181.0 13.9 %collective-permute-start.40 = (bf16[208,768]{1,0:T(8,128)(2,1)S(1)}, bf16[208,768]{1,0:T(8,128)(2,1)S(1)}, u32[]{:S(2)}, u32[]{:S(2)}) collective-permute-start(bf16[208,768]{1,0:T(8,128)(2,1)S(1)} %add_convert_fusion.3.mine.ck), channel_id=1, source_target_pairs={{0,8},{4,12},{8,0},{12,4},{16,24},{20,28},{24,16},{28,20},{1,9},{5... | collective-permute-start | bytes 958472 | tf_op jit(solution)/shard_map/ppermute | solution.py:652
  181.1 16.2 %collective-permute-start.43 = (bf16[384,768]{1,0:T(8,128)(2,1)S(1)}, bf16[384,768]{1,0:T(8,128)(2,1)S(1)}, u32[]{:S(2)}, u32[]{:S(2)}) collective-permute-start(bf16[384,768]{1,0:T(8,128)(2,1)S(1)} %get-tuple-element.230.refs_0_), channel_id=1, source_target_pairs={{0,2},{1,3},{2,0},{3,1},{4,6},{5,7},{6,4},{7,5},{8,10},{9,11},{10,... | collective-permute-start | bytes 1769480 | tf_op jit(solution)/shard_map/ppermute | solution.py:652
  196.6 12.8 %collective-permute-start.51 = (bf16[384,768]{1,0:T(8,128)(2,1)S(1)}, bf16[384,768]{1,0:T(8,128)(2,1)S(1)}, u32[]{:S(2)}, u32[]{:S(2)}) collective-permute-start(bf16[384,768]{1,0:T(8,128)(2,1)S(1)} %fusion.1.refs_8_), channel_id=1, source_target_pairs={{0,1},{1,0},{2,3},{3,2},{4,5},{5,4},{6,7},{7,6},{8,9},{9,8},{10,11... | collective-permute-start | bytes 1769480 | tf_op jit(solution)/shard_map/ppermute | solution.py:652
  196.6 13.3 %collective-permute-start.49 = (bf16[384,768]{1,0:T(8,128)(2,1)S(1)}, bf16[384,768]{1,0:T(8,128)(2,1)S(1)}, u32[]{:S(2)}, u32[]{:S(2)}) collective-permute-start(bf16[384,768]{1,0:T(8,128)(2,1)S(1)} %get-tuple-element.227.refs_4_), channel_id=1, source_target_pairs={{0,1},{1,0},{2,3},{3,2},{4,5},{5,4},{6,7},{7,6},{8,9},{9,8},{10,11... | collective-permute-start | bytes 1769480 | tf_op jit(solution)/shard_map/ppermute | solution.py:652
  197.1 12.9 %collective-permute-start.47 = (bf16[384,768]{1,0:T(8,128)(2,1)S(1)}, bf16[384,768]{1,0:T(8,128)(2,1)S(1)}, u32[]{:S(2)}, u32[]{:S(2)}) collective-permute-start(bf16[384,768]{1,0:T(8,128)(2,1)S(1)} %get-tuple-element.230.refs_0_), channel_id=1, source_target_pairs={{0,1},{1,0},{2,3},{3,2},{4,5},{5,4},{6,7},{7,6},{8,9},{9,8},{10,11... | collective-permute-start | bytes 1769480 | tf_op jit(solution)/shard_map/ppermute | solution.py:652
  207.8 19.9 %collective-permute-start.53 = (bf16[432,768]{1,0:T(8,128)(2,1)S(1)}, bf16[432,768]{1,0:T(8,128)(2,1)S(1)}, u32[]{:S(2)}, u32[]{:S(2)}) collective-permute-start(bf16[432,768]{1,0:T(8,128)(2,1)S(1)} %last.1.pair), channel_id=1, source_target_pairs={{0,4},{4,0},{8,12},{12,8},{16,20},{20,16},{24,28},{28,24},{1,5},{5... | collective-permute-start | bytes 1990664 | tf_op jit(solution)/shard_map/ppermute | solution.py:652
  210.0 15.7 %collective-permute-start.54 = (bf16[2,192,768]{2,1,0:T(8,128)(2,1)S(1)}, bf16[2,192,768]{2,1,0:T(8,128)(2,1)S(1)}, u32[]{:S(2)}, u32[]{:S(2)}) collective-permute-start(bf16[2,192,768]{2,1,0:T(8,128)(2,1)S(1)} %pair.1), channel_id=1, source_target_pairs={{0,8},{4,12},{8,0},{12,4},{16,24},{20,28},{24,16},{28,20},{1,9},{5... | collective-permute-start | bytes 1769480 | tf_op jit(solution)/shard_map/ppermute | solution.py:652
  (30 other events, 227.6 us)

commit v3 on v2

--- a/solution.py
+++ b/solution.py
@@ -557,20 +557,27 @@
             dst[pl.ds(pl.multiple_of(((one ^ a) * 2 + (two ^ b)) * n, 16), n), :] = src.astype(F32)
 
 
-def outer_out_kernel(ids, k, o, q, uw):
-    place(ids, True, k, o, q, uw)
-
-
-def inner_out_kernel(ids, consts, pair, q, live, iw, ib, ua, pe, big):
-    n = big.shape[0] // 4
+def weights_out_kernel(ids, consts, ak, ao, aq, pair, q, live, uw, iw, ib, ua, pe, sums):
+    place(ids, True, ak, ao, aq, uw)
+    d = iw.shape[0]
+    n = pair.shape[0] // 2 - 8
+    head = d - 3 * n
     for a, src in enumerate((pair, q)):
         for b in range(2):
             j = (ids[1] ^ a) * 2 + (ids[2] ^ b)
-            big[pl.ds(pl.multiple_of(j * n, 16), n), :] = src[b * n : (b + 1) * n, :].astype(F32)
-    d = iw.shape[0]
-    iw[...] = big[:d, :]
-    ua[...] = (1.5 * big[d : d + 1, :] * (1.0 - consts[UGATE : UGATE + 1, :])).reshape(d)
-    ib[...] = big[d + 1 : d + 2, :].reshape(d)
+            iw[pl.ds(pl.multiple_of(j * n, 16), head), :] = src[b * n : b * n + head, :].astype(F32)
+            rest = src[b * n + head : (b + 1) * n, :].astype(F32)
+
+            @pl.when(j < 3)
+            def _():
+                iw[pl.ds(pl.multiple_of(j * n + head, 16), n - head), :] = rest
+
+            @pl.when(j == 3)
+            def _():
+                sums[...] = rest
+
+    ua[...] = (1.5 * sums[0:1, :] * (1.0 - consts[UGATE : UGATE + 1, :])).reshape(d)
+    ib[...] = sums[1:2, :].reshape(d)
     hard = jnp.sum(pair[2 * n :, :].astype(F32) + q[2 * n :, :].astype(F32))
     pe[0] = 0.5 * hard / live[0]
 
@@ -681,7 +688,7 @@
     full = lambda *s: pl.BlockSpec(s, lambda b, *_: (0,) * len(s))
     c0, c1, cfar, e, inv_l, k, v, q, qst, kt = call(
         attend_kernel,
-        [((blocks, c, quarter), BF), ((blocks, c, quarter), BF), ((2, blocks, c, quarter), BF), ((blocks, heads, length, length), BF, HBM),
+        [((blocks, c, quarter), BF), ((blocks, c, quarter), BF), ((2, blocks, c, quarter), BF), ((blocks, heads, length, length), BF),
          ((blocks, 8, length), F32), ((rows, c), BF, HBM), ((rows, c), BF, HBM), ((rows, c), BF, HBM), ((blocks, c, length), BF, HBM), ((blocks, c, length), BF, HBM)],
         (ids, in_hbm(tokens), *(in_hbm(a.T) for a in (query_weight, key_weight, value_weight)), consts, seg3, live3),
         prefetch=1, grid=(blocks,),
@@ -767,7 +774,7 @@
     keep, send, wacc, cacc = call(
         attend_back_kernel,
         [((2, t, d), BF), ((2, t, d), BF), ((3 * c, d), F32), ((16, d), F32)],
-        (ids, *gpieces, *(in_hbm(a) for a in (e, inv_l, k, v, q, kt, tokens)), *(in_hbm(a.T) for a in (query_weight, key_weight, value_weight))),
+        (ids, *gpieces, e, *(in_hbm(a) for a in (inv_l, k, v, q, kt, tokens)), *(in_hbm(a.T) for a in (query_weight, key_weight, value_weight))),
         prefetch=1, grid=(blocks,),
         specs=[pick(c, quarter), pick(c, quarter), pl.BlockSpec((2, 1, c, quarter), lambda b, *_: (0, b, 0, 0)),
                pl.BlockSpec((2, 1, c, quarter), lambda b, *_: (0, b, 0, 0)), pick(heads, length, length), pick(8, length),
@@ -883,10 +890,11 @@
         prefetch=1, specs=[VM] * 4, out_specs=[VM] * 12 + [SM] + [VM] + [SM] * 2,
         scratch=[pltpu.VMEM((n_c, d), F32)], us=0.1, limit=8, name="final",
     )
-    (uw,) = call(outer_out_kernel, [((w, d), F32)], (ids, a_mine, a_other, after(a_last, qw)), prefetch=1, us=0.1, limit=8, name="outer_out")
-    iw, ib, ua, pe = call(
-        inner_out_kernel, [((d, w), F32), ((w,), F32), ((w,), F32), ((1,), F32)], (ids, consts, b_pair, after(b_last, uw), live), prefetch=1,
-        specs=[VM] * 3 + [SM], out_specs=[VM] * 3 + [SM], scratch=[pltpu.VMEM((n_b, w), F32)], us=0.1, limit=12, name="inner_out",
+    uw, iw, ib, ua, pe = call(
+        weights_out_kernel,
+        [((w, d), F32), ((d, w), F32), ((w,), F32), ((w,), F32), ((1,), F32)],
+        (ids, consts, a_mine, a_other, after(a_last, qw), b_pair, b_last, live), prefetch=1,
+        specs=[VM] * 6 + [SM], out_specs=[VM] * 4 + [SM], scratch=[pltpu.VMEM((n_b - d, w), F32)], us=0.1, limit=8, name="weights_out",
     )
     return (
         student, pruned, tokens_grad, qw.T, qb, kw.T, vw.T, vb, ow, ob, fg, fs, iw, ib, uw, ub, sg, ss, ha, ua, da, me.reshape(()), pe.reshape(()),

time: 236 us -> 234 us (level)
    pallas_call x23 -> x22, Pallas kernels: 94.3 us -> 92 us  [call(): pl.pallas_call(kernel, out_shape=[pltpu.HBM(*o[:2]) if len(o) > 2 else ja...]
  transfers between devices with their start and end apart: 55 -> 55, of which waited for: 20 -> 20; matrix products, arithmetic and copies ran while one was open for 1% -> 1% of each run, Pallas kernels for 39% -> 38%
where the time goes in v3:
time: 234 us; the launch traced here: 230 us
  Pallas kernels  92 us (39%)
  waiting for transfers between devices  85.6 us (37%)
  starting transfers between devices  48 us (21%)
    pallas_call x22, Pallas kernels, call(): pl.pallas_call(kernel, out_shape=[pltpu.HBM(*o[:2]) if len(o) > 2 else ja...  92 us
    ppermute x55, waiting for transfers between devices, hop(): return lax.ppermute(x, axis, [(i, i ^ mask) for i in range(size)])  85.6 us
    ppermute x55, starting transfers between devices, hop(): return lax.ppermute(x, axis, [(i, i ^ mask) for i in range(size)])  48 us
  transfers between devices with their start and end apart: 55, of which 20 were waited for; matrix products, arithmetic and copies ran while one was open for 1% of the time, Pallas kernels for 38%

profile of v3, /device:TPU:0, one launch (start us, length us, event | category | flops | bytes accessed | tf_op | source)
XLA Modules:
  0.0 229.7 jit_solution(11073976619905665952)
XLA Ops:
  1.8 3.0 %collective-permute-start.7 = (bf16[768,384]{1,0:T(8,128)(2,1)S(1)}, bf16[768,384]{1,0:T(8,128)(2,1)S(1)}, u32[]{:S(2)}, u32[]{:S(2)}) collective-permute-start(bf16[768,384]{1,0:T(8,128)(2,1)S(1)} %constant_dynamic-slice_fusion), channel_id=1, source_target_pairs={{0,2},{1,3},{2,0},{3,1},{4,6},{5,7},{6,4},{7,5},{8,10},{9,11},{10,... | collective-permute-start | bytes 1769480 | tf_op jit(solution)/shard_map/ppermute | solution.py:659
  6.4 10.8 %attend.1 = (bf16[3,192,128]{2,1,0:T(8,128)(2,1)S(1)}, bf16[3,192,128]{2,1,0:T(8,128)(2,1)S(1)}, bf16[2,3,192,128]{3,2,1,0:T(8,128)(2,1)S(1)}, bf16[3,3,512,512]...) custom-call(s32[5]{0:T(128)S(1)} %stack.19.ids.h_ref, ...), custom_call_target="tpu_custom_call" | custom-call | flops 4499999744 | tf_op jit(solution)/shard_map/attend/pallas_call | solution.py:59
  17.2 2.0 collective-permute-start.1
  21.1 5.3 %collective-permute-done.4.s2.refs_8_.refs_14_ = bf16[224,768]{1,0:T(8,128)(2,1)S(1)} collective-permute-done((bf16[224,768]{1,0:T(8,128)(2,1)S(1)}, bf16[224,768]{1,0:T(8,128)(2,1)S(1)}, u32[]{:S(2)}, u32[]{:S(2)}) %collective-permute-start.4) | collective-permute-done | bytes 344096 | tf_op jit(solution)/shard_map/ppermute | solution.py:659
  26.9 5.0 %collective-permute-done.1.xr = bf16[2,3,192,128]{3,2,1,0:T(8,128)(2,1)S(1)} collective-permute-done((bf16[2,3,192,128]{3,2,1,0:T(8,128)(2,1)S(1)}, bf16[2,3,192,128]{3,2,1,0:T(8,128)(2,1)S(1)}, u32[]{:S(2)}, u32[]{:S(2)}) %collective-permute-start.1) | collective-permute-done | bytes 294944 | tf_op jit(solution)/shard_map/ppermute | solution.py:659
  34.0 3.0 %first.1 = (bf16[384,768]{1,0:T(8,128)(2,1)S(1)}, f32[384,768]{1,0:T(8,128)S(1)}, f32[384,128]{1,0:T(8,128)S(1)}, f32[384,768]{1,0:T(8,128)S(1)}, bf16[4,384,192]{2,1,0:T(8,128)(2,1)S(1)}) custom-call(s32[5]{0:T(128)S(1)} %stack.19.ids.h_ref, bf16[3,192,128]{2,1,0:T(8,128)(2,1)S(1)} %get-tuple-element.148.c0, ...), custom_call_target="tpu_custom_call" | custom-call | flops 2000000000 | tf_op jit(solution)/shard_map/first/pallas_call | solution.py:59
  37.5 3.1 %hard_first.1 = (bf16[384,768]{1,0:T(8,128)(2,1)S(1)}, f32[384,768]{1,0:T(8,128)S(1)}) custom-call(s32[5]{0:T(128)S(1)} %stack.19.ids.h_ref, bf16[3,192,128]{2,1,0:T(8,128)(2,1)S(1)} %get-tuple-element.148.c0, bf16[3,192,128]{2,1,0:T(8,128)(2,1)S(1)} %collective-permute-done.c1, bf16[2,3,192,128]{3,2,1,0:T(8,128)(2,1)S(1)} %collective-permute-done.1.xr, ...), custom_call_target="tpu_custom_call" | custom-call | flops 2000000000 | tf_op jit(solution)/shard_map/hard_first/pallas_call | solution.py:59
  40.7 7.1 %collective-permute-done.12.refs_2_.refs_8_ = bf16[384,768]{1,0:T(8,128)(2,1)S(1)} collective-permute-done((bf16[384,768]{1,0:T(8,128)(2,1)S(1)}, bf16[384,768]{1,0:T(8,128)(2,1)S(1)}, u32[]{:S(2)}, u32[]{:S(2)}) %collective-permute-start.12) | collective-permute-done | bytes 589856 | tf_op jit(solution)/shard_map/ppermute | solution.py:659
  49.5 6.5 %inner.1 = (bf16[4,384,768]{2,1,0:T(8,128)(2,1)S(1)}, bf16[4,384,768]{2,1,0:T(8,128)(2,1)S(1)}) custom-call(s32[5]{0:T(128)S(1)} %stack.19.ids.h_ref, bf16[384,768]{1,0:T(8,128)(2,1)S(1)} %get-tuple-element.171.first_low.f0, bf16[768,768]{1,0:T(8,128)(2,1)S(1)} %copy-done.2, bf16[768,768]{1,0:T(8,128)(2,1)S(1)} %collective-permute-done.6.refs_1_, ...), custom_call_target="tpu_custom_call" | custom-call | flops 4000000000 | tf_op jit(solution)/shard_map/inner/pallas_call | solution.py:59
  56.1 5.7 %hard_inner.1.hidden = bf16[4,384,768]{2,1,0:T(8,128)(2,1)S(1)} custom-call(s32[5]{0:T(128)S(1)} %stack.19.ids.h_ref, bf16[384,768]{1,0:T(8,128)(2,1)S(1)} %get-tuple-element.157.first_low, bf16[768,768]{1,0:T(8,128)(2,1)S(1)} %copy-done.2, bf16[768,768]{1,0:T(8,128)(2,1)S(1)} %collective-permute-done.6.refs_1_, ...), custom_call_target="tpu_custom_call" | custom-call | flops 4000000000 | tf_op jit(solution)/shard_map/hard_inner/pallas_call | solution.py:59
  65.0 5.5 %second.1 = (bf16[384,768]{1,0:T(8,128)(2,1)S(1)}, f32[384,768]{1,0:T(8,128)S(1)}, bf16[384,768]{1,0:T(8,128)(2,1)S(1)}, f32[8,768]{1,0:T(8,128)S(1)}) custom-call(s32[5]{0:T(128)S(1)} %stack.19.ids.h_ref, bf16[4,384,768]{2,1,0:T(8,128)(2,1)S(1)} %get-tuple-element.153.hidden, f32[384,768]{1,0:T(8,128)S(1)} %get-tuple-element.154.normed.refs_17_, ...), custom_call_target="tpu_custom_call" | custom-call | flops 3000000000 | tf_op jit(solution)/shard_map/second/pallas_call | solution.py:59
  70.4 9.4 %back.1 = (bf16[3,192,128]{2,1,0:T(8,128)(2,1)S(1)}, bf16[3,192,128]{2,1,0:T(8,128)(2,1)S(1)}, bf16[2,3,192,128]{3,2,1,0:T(8,128)(2,1)S(1)}, bf16[2,208,768]{2,1...) custom-call(s32[5]{0:T(128)S(1)} %stack.19.ids.h_ref, ...), custom_call_target="tpu_custom_call" | custom-call | flops 6499999744 | tf_op jit(solution)/shard_map/back/pallas_call | solution.py:59
  81.9 5.7 %units.1 = (bf16[1536,768]{1,0:T(8,128)(2,1)S(1)}, bf16[1536,768]{1,0:T(8,128)(2,1)S(1)}) custom-call(bf16[384,768]{1,0:T(8,128)(2,1)S(1)} %get-tuple-element.171.first_low.f0, bf16[384,768]{1,0:T(8,128)(2,1)S(1)} %collective-permute-done.18.f1, bf16[384,768]{1,0:T(8,128)(2,1)S(1)} %collective-permute-done.19.fx, ...), custom_call_target="tpu_custom_call" | custom-call | flops 3000000000 | tf_op jit(solution)/shard_map/units/pallas_call | solution.py:59
  92.2 15.5 %attend_back.1 = (bf16[2,384,768]{2,1,0:T(8,128)(2,1)S(1)}, bf16[2,384,768]{2,1,0:T(8,128)(2,1)S(1)}, f32[576,768]{1,0:T(8,128)S(1)}, f32[16,768]{1,0:T(8,128)S(1)}) custom-call(s32[5]{0:T(128)S(1)} %stack.19.ids.h_ref, bf16[3,192,128]{2,1,0:T(8,128)(2,1)S(1)} %get-tuple-element.168.g0, bf16[3,192,128]{2,1,0:T(8,128)(2,1)S(1)} %collective-permute-done.16.g1, ...), custom_call_target="tpu_custom_call" | custom-call | flops 7500000256 | tf_op jit(solution)/shard_map/attend_back/pallas_call | solution.py:59
  107.7 4.5 %collective-permute-done.24.gx = bf16[384,768]{1,0:T(8,128)(2,1)S(1)} collective-permute-done((bf16[384,768]{1,0:T(8,128)(2,1)S(1)}, bf16[384,768]{1,0:T(8,128)(2,1)S(1)}, u32[]{:S(2)}, u32[]{:S(2)}) %collective-permute-start.24) | collective-permute-done | bytes 589856 | tf_op jit(solution)/shard_map/ppermute | solution.py:659
  116.9 2.6 %near_grad.1 = (f32[768,768]{1,0:T(8,128)S(1)}, bf16[768,768]{1,0:T(8,128)(2,1)S(1)}, f32[2,8,768]{2,1,0:T(8,128)S(1)}) custom-call(bf16[384,768]{1,0:T(8,128)(2,1)S(1)} %get-tuple-element.194.gffn.g0, bf16[384,768]{1,0:T(8,128)(2,1)S(1)} %collective-permute-done.26.g1, bf16[768,768]{1,0:T(8,128)(2,1)S(1)} %copy-done, ...), custom_call_target="tpu_custom_call" | custom-call | flops 2500000000 | tf_op jit(solution)/shard_map/near_grad/pallas_call | solution.py:59
  121.2 2.1 outer_grad.1
  124.9 4.4 %inner_grad.1 = (bf16[2,208,768]{2,1,0:T(8,128)(2,1)S(1)}, bf16[2,208,768]{2,1,0:T(8,128)(2,1)S(1)}) custom-call(s32[5]{0:T(128)S(1)} %stack.19.ids.h_ref, bf16[384,768]{1,0:T(8,128)(2,1)S(1)} %get-tuple-element.171.first_low.f0, bf16[384,768]{1,0:T(8,128)(2,1)S(1)} %collective-permute-done.18.f1, bf16[384,768]{1,0:T(8,128)(2,1)S(1)} %collective-permute-done.19.fx, ...), custom_call_target="tpu_custom_call" | custom-call | flops 2000000000 | tf_op jit(solution)/shard_map/inner_grad/pallas_call | solution.py:59
  133.8 4.9 %hard.1 = (bf16[384,768]{1,0:T(8,128)(2,1)S(1)}, f32[8,128]{1,0:T(8,128)S(1)}) custom-call(s32[5]{0:T(128)S(1)} %stack.19.ids.h_ref, bf16[4,384,768]{2,1,0:T(8,128)(2,1)S(1)} %hard_inner.1.hidden, f32[384,768]{1,0:T(8,128)S(1)} %get-tuple-element.207.normed, bf16[768,768]{1,0:T(8,128)(2,1)S(1)} %copy-done, ...), custom_call_target="tpu_custom_call" | custom-call | flops 50000000 | tf_op jit(solution)/shard_map/hard/pallas_call | solution.py:59
  141.2 6.5 %collective-permute-done.32 = bf16[2,208,768]{2,1,0:T(8,128)(2,1)S(1)} collective-permute-done((bf16[2,208,768]{2,1,0:T(8,128)(2,1)S(1)}, bf16[2,208,768]{2,1,0:T(8,128)(2,1)S(1)}, u32[]{:S(2)}, u32[]{:S(2)}) %collective-permute-start.32) | collective-permute-done | bytes 639008 | tf_op jit(solution)/shard_map/ppermute | solution.py:659
  149.8 2.7 %collective-permute-start.34 = (bf16[208,768]{1,0:T(8,128)(2,1)S(1)}, bf16[208,768]{1,0:T(8,128)(2,1)S(1)}, u32[]{:S(2)}, u32[]{:S(2)}) collective-permute-start(bf16[208,768]{1,0:T(8,128)(2,1)S(1)} %fusion.2), channel_id=1, source_target_pairs={{0,16},{4,20},{8,24},{12,28},{16,0},{20,4},{24,8},{28,12},{1,17},{... | collective-permute-start | bytes 958472 | tf_op jit(solution)/shard_map/ppermute | solution.py:659
  152.9 2.7 %collective-permute-start.41 = (bf16[192,768]{1,0:T(8,128)(2,1)S(1)}, bf16[192,768]{1,0:T(8,128)(2,1)S(1)}, u32[]{:S(2)}, u32[]{:S(2)}) collective-permute-start(bf16[192,768]{1,0:T(8,128)(2,1)S(1)} %fusion.5), channel_id=1, source_target_pairs={{0,16},{4,20},{8,24},{12,28},{16,0},{20,4},{24,8},{28,12},{1,17},{... | collective-permute-start | bytes 884744 | tf_op jit(solution)/shard_map/ppermute | solution.py:659
  157.1 2.1 collective-permute-done.37
  159.2 2.1 collective-permute-done.35.got
  164.2 16.8 %collective-permute-done.34 = bf16[208,768]{1,0:T(8,128)(2,1)S(1)} collective-permute-done((bf16[208,768]{1,0:T(8,128)(2,1)S(1)}, bf16[208,768]{1,0:T(8,128)(2,1)S(1)}, u32[]{:S(2)}, u32[]{:S(2)}) %collective-permute-start.34) | collective-permute-done | bytes 319520 | tf_op jit(solution)/shard_map/ppermute | solution.py:659
  182.7 4.7 %collective-permute-done.41 = bf16[192,768]{1,0:T(8,128)(2,1)S(1)} collective-permute-done((bf16[192,768]{1,0:T(8,128)(2,1)S(1)}, bf16[192,768]{1,0:T(8,128)(2,1)S(1)}, u32[]{:S(2)}, u32[]{:S(2)}) %collective-permute-start.41) | collective-permute-done | bytes 294944 | tf_op jit(solution)/shard_map/ppermute | solution.py:659
  189.1 5.9 %collective-permute-done.40.other.co = bf16[208,768]{1,0:T(8,128)(2,1)S(1)} collective-permute-done((bf16[208,768]{1,0:T(8,128)(2,1)S(1)}, bf16[208,768]{1,0:T(8,128)(2,1)S(1)}, u32[]{:S(2)}, u32[]{:S(2)}) %collective-permute-start.40) | collective-permute-done | bytes 319520 | tf_op jit(solution)/shard_map/ppermute | solution.py:659
  197.5 10.3 %collective-permute-done.42.other = bf16[224,768]{1,0:T(8,128)(2,1)S(1)} collective-permute-done((bf16[224,768]{1,0:T(8,128)(2,1)S(1)}, bf16[224,768]{1,0:T(8,128)(2,1)S(1)}, u32[]{:S(2)}, u32[]{:S(2)}) %collective-permute-start.42) | collective-permute-done | bytes 344096 | tf_op jit(solution)/shard_map/ppermute | solution.py:659
  213.1 3.7 %spread.1 = (bf16[3,512,768]{2,1,0:T(8,128)(2,1)}, bf16[3,512,768]{2,1,0:T(8,128)(2,1)}, bf16[3,512,768]{2,1,0:T(8,128)(2,1)}) custom-call(s32[5]{0:T(128)S(1)} %stack.19.ids.h_ref, bf16[384,768]{1,0:T(8,128)(2,1)S(1)} %get-tuple-element.230.refs_0_, bf16[384,768]{1,0:T(8,128)(2,1)S(1)} %collective-permute-done.47.refs_1_, ...), custom_call_target="tpu_custom_call" | custom-call | flops 50000000 | tf_op jit(solution)/shard_map/spread/pallas_call | solution.py:59
  216.9 2.2 final.1
  219.1 6.6 %collective-permute-done.53.aq = bf16[2,192,768]{2,1,0:T(8,128)(2,1)S(1)} collective-permute-done((bf16[2,192,768]{2,1,0:T(8,128)(2,1)S(1)}, bf16[2,192,768]{2,1,0:T(8,128)(2,1)S(1)}, u32[]{:S(2)}, u32[]{:S(2)}) %collective-permute-start.53) | collective-permute-done | bytes 589856 | tf_op jit(solution)/shard_map/ppermute | solution.py:659
  225.7 3.8 %weights_out.1 = (f32[768,768]{1,0:T(8,128)}, f32[768,768]{1,0:T(8,128)}, f32[768]{0:T(1024)}, f32[768]{0:T(1024)}, f32[1]{0:T(128)}) custom-call(s32[5]{0:T(128)S(1)} %stack.19.ids.h_ref, f32[16,768]{1,0:T(8,128)S(1)} %get-tuple-element.141.consts.refs_8_.refs_23_, bf16[192,768]{1,0:T(8,128)(2,1)S(1)} %add_convert_fusion.10.mine.ak, ...), custom_call_target="tpu_custom_call" | custom-call | flops 50000000 | tf_op jit(solution)/shard_map/weights_out/pallas_call | solution.py:59
  (131 shorter events, 52.0 us)
Async XLA Ops:
  1.8 17.4 %collective-permute-start.7 = (bf16[768,384]{1,0:T(8,128)(2,1)S(1)}, bf16[768,384]{1,0:T(8,128)(2,1)S(1)}, u32[]{:S(2)}, u32[]{:S(2)}) collective-permute-start(bf16[768,384]{1,0:T(8,128)(2,1)S(1)} %constant_dynamic-slice_fusion), channel_id=1, source_target_pairs={{0,2},{1,3},{2,0},{3,1},{4,6},{5,7},{6,4},{7,5},{8,10},{9,11},{10,... | collective-permute-start | bytes 1769480 | tf_op jit(solution)/shard_map/ppermute | solution.py:659
  6.2 20.2 %collective-permute-start.4 = (bf16[224,768]{1,0:T(8,128)(2,1)S(1)}, bf16[224,768]{1,0:T(8,128)(2,1)S(1)}, u32[]{:S(2)}, u32[]{:S(2)}) collective-permute-start(bf16[224,768]{1,0:T(8,128)(2,1)S(1)} %get-tuple-element.145.s0.refs_6_.refs_12_), channel_id=1, source_target_pairs={{0,2},{1,3},{2,0},{3,1},{4,6},{5,7},{6,4},{7,5},{8,10},{9,11},{10,... | collective-permute-start | bytes 1032200 | tf_op jit(solution)/shard_map/ppermute | solution.py:659
  17.2 14.6 %collective-permute-start.1 = (bf16[2,3,192,128]{3,2,1,0:T(8,128)(2,1)S(1)}, bf16[2,3,192,128]{3,2,1,0:T(8,128)(2,1)S(1)}, u32[]{:S(2)}, u32[]{:S(2)}) collective-permute-start(bf16[2,3,192,128]{3,2,1,0:T(8,128)(2,1)S(1)} %get-tuple-element.144), channel_id=1, source_target_pairs={{0,2},{1,3},{2,0},{3,1},{4,6},{5,7},{6,4},{7,5},{8,10},{9,11},{10,... | collective-permute-start | bytes 884744 | tf_op jit(solution)/shard_map/ppermute | solution.py:659
  19.3 17.7 %collective-permute-start.8 = (bf16[768,384]{1,0:T(8,128)(2,1)S(1)}, bf16[768,384]{1,0:T(8,128)(2,1)S(1)}, u32[]{:S(2)}, u32[]{:S(2)}) collective-permute-start(bf16[768,384]{1,0:T(8,128)(2,1)S(1)} %collective-permute-done.7.refs_2_), channel_id=1, source_target_pairs={{0,4},{4,0},{8,12},{12,8},{16,20},{20,16},{24,28},{28,24},{1,5},{5... | collective-permute-start | bytes 1769480 | tf_op jit(solution)/shard_map/ppermute | solution.py:659
  21.1 28.4 %collective-permute-start.6 = (bf16[768,768]{1,0:T(8,128)(2,1)S(1)}, bf16[768,768]{1,0:T(8,128)(2,1)S(1)}, u32[]{:S(2)}, u32[]{:S(2)}) collective-permute-start(bf16[768,768]{1,0:T(8,128)(2,1)S(1)} %copy-done.2), channel_id=1, source_target_pairs={{0,1},{1,0},{2,3},{3,2},{4,5},{5,4},{6,7},{7,6},{8,9},{9,8},{10,11... | collective-permute-start | bytes 3538952 | tf_op jit(solution)/shard_map/ppermute | solution.py:659
  32.0 15.8 %collective-permute-start.12 = (bf16[384,768]{1,0:T(8,128)(2,1)S(1)}, bf16[384,768]{1,0:T(8,128)(2,1)S(1)}, u32[]{:S(2)}, u32[]{:S(2)}) collective-permute-start(bf16[384,768]{1,0:T(8,128)(2,1)S(1)} %get-tuple-element.262), channel_id=1, source_target_pairs={{0,2},{1,3},{2,0},{3,1},{4,6},{5,7},{6,4},{7,5},{8,10},{9,11},{10,... | collective-permute-start | bytes 1769480 | tf_op jit(solution)/shard_map/ppermute | solution.py:659
  33.8 15.7 %collective-permute-start.9 = (bf16[768,384]{1,0:T(8,128)(2,1)S(1)}, bf16[768,384]{1,0:T(8,128)(2,1)S(1)}, u32[]{:S(2)}, u32[]{:S(2)}) collective-permute-start(bf16[768,384]{1,0:T(8,128)(2,1)S(1)} %collective-permute-done.7.refs_2_), channel_id=1, source_target_pairs={{0,1},{1,0},{2,3},{3,2},{4,5},{5,4},{6,7},{7,6},{8,9},{9,8},{10,11... | collective-permute-start | bytes 1769480 | tf_op jit(solution)/shard_map/ppermute | solution.py:659
  37.3 27.7 %collective-permute-start.11 = (bf16[768,768]{1,0:T(8,128)(2,1)S(1)}, bf16[768,768]{1,0:T(8,128)(2,1)S(1)}, u32[]{:S(2)}, u32[]{:S(2)}) collective-permute-start(bf16[768,768]{1,0:T(8,128)(2,1)S(1)} %copy-done), channel_id=1, source_target_pairs={{0,1},{1,0},{2,3},{3,2},{4,5},{5,4},{6,7},{7,6},{8,9},{9,8},{10,11... | collective-permute-start | bytes 3538952 | tf_op jit(solution)/shard_map/ppermute | solution.py:659
  47.8 15.0 %collective-permute-start.13 = (bf16[384,768]{1,0:T(8,128)(2,1)S(1)}, bf16[384,768]{1,0:T(8,128)(2,1)S(1)}, u32[]{:S(2)}, u32[]{:S(2)}) collective-permute-start(bf16[384,768]{1,0:T(8,128)(2,1)S(1)} %get-tuple-element.261), channel_id=1, source_target_pairs={{0,2},{1,3},{2,0},{3,1},{4,6},{5,7},{6,4},{7,5},{8,10},{9,11},{10,... | collective-permute-start | bytes 1769480 | tf_op jit(solution)/shard_map/ppermute | solution.py:659
  49.5 15.5 %collective-permute-start.14 = (bf16[384,768]{1,0:T(8,128)(2,1)S(1)}, bf16[384,768]{1,0:T(8,128)(2,1)S(1)}, u32[]{:S(2)}, u32[]{:S(2)}) collective-permute-start(bf16[384,768]{1,0:T(8,128)(2,1)S(1)} %collective-permute-done.12.refs_2_.refs_8_), channel_id=1, source_target_pairs={{0,1},{1,0},{2,3},{3,2},{4,5},{5,4},{6,7},{7,6},{8,9},{9,8},{10,11... | collective-permute-start | bytes 1769480 | tf_op jit(solution)/shard_map/ppermute | solution.py:659
  62.7 19.2 %collective-permute-start.18 = (bf16[384,768]{1,0:T(8,128)(2,1)S(1)}, bf16[384,768]{1,0:T(8,128)(2,1)S(1)}, u32[]{:S(2)}, u32[]{:S(2)}) collective-permute-start(bf16[384,768]{1,0:T(8,128)(2,1)S(1)} %get-tuple-element.171.first_low.f0), channel_id=1, source_target_pairs={{0,1},{1,0},{2,3},{3,2},{4,5},{5,4},{6,7},{7,6},{8,9},{9,8},{10,11... | collective-permute-start | bytes 1769480 | tf_op jit(solution)/shard_map/ppermute | solution.py:659
  63.2 16.6 %collective-permute-start.19 = (bf16[384,768]{1,0:T(8,128)(2,1)S(1)}, bf16[384,768]{1,0:T(8,128)(2,1)S(1)}, u32[]{:S(2)}, u32[]{:S(2)}) collective-permute-start(bf16[384,768]{1,0:T(8,128)(2,1)S(1)} %get-tuple-element.171.first_low.f0), channel_id=1, source_target_pairs={{0,2},{1,3},{2,0},{3,1},{4,6},{5,7},{6,4},{7,5},{8,10},{9,11},{10,... | collective-permute-start | bytes 1769480 | tf_op jit(solution)/shard_map/ppermute | solution.py:659
  90.1 22.2 %collective-permute-start.23 = (bf16[208,768]{1,0:T(8,128)(2,1)S(1)}, bf16[208,768]{1,0:T(8,128)(2,1)S(1)}, u32[]{:S(2)}, u32[]{:S(2)}) collective-permute-start(bf16[208,768]{1,0:T(8,128)(2,1)S(1)} %get-tuple-element.259), channel_id=1, source_target_pairs={{0,2},{1,3},{2,0},{3,1},{4,6},{5,7},{6,4},{7,5},{8,10},{9,11},{10,... | collective-permute-start | bytes 958472 | tf_op jit(solution)/shard_map/ppermute | solution.py:659
  91.6 20.6 %collective-permute-start.24 = (bf16[384,768]{1,0:T(8,128)(2,1)S(1)}, bf16[384,768]{1,0:T(8,128)(2,1)S(1)}, u32[]{:S(2)}, u32[]{:S(2)}) collective-permute-start(bf16[384,768]{1,0:T(8,128)(2,1)S(1)} %get-tuple-element.194.gffn.g0), channel_id=1, source_target_pairs={{0,2},{1,3},{2,0},{3,1},{4,6},{5,7},{6,4},{7,5},{8,10},{9,11},{10,... | collective-permute-start | bytes 1769480 | tf_op jit(solution)/shard_map/ppermute | solution.py:659
  113.8 16.7 %collective-permute-start.28 = (bf16[2,208,768]{2,1,0:T(8,128)(2,1)S(1)}, bf16[2,208,768]{2,1,0:T(8,128)(2,1)S(1)}, u32[]{:S(2)}, u32[]{:S(2)}) collective-permute-start(bf16[2,208,768]{2,1,0:T(8,128)(2,1)S(1)} %get-tuple-element.198), channel_id=1, source_target_pairs={{0,4},{4,0},{8,12},{12,8},{16,20},{20,16},{24,28},{28,24},{1,5},{5... | collective-permute-start | bytes 1916936 | tf_op jit(solution)/shard_map/ppermute | solution.py:659
  119.6 19.1 %collective-permute-start.27 = (bf16[384,768]{1,0:T(8,128)(2,1)S(1)}, bf16[384,768]{1,0:T(8,128)(2,1)S(1)}, u32[]{:S(2)}, u32[]{:S(2)}) collective-permute-start(bf16[384,768]{1,0:T(8,128)(2,1)S(1)} %fusion.4), channel_id=1, source_target_pairs={{0,2},{1,3},{2,0},{3,1},{4,6},{5,7},{6,4},{7,5},{8,10},{9,11},{10,... | collective-permute-start | bytes 1769480 | tf_op jit(solution)/shard_map/ppermute | solution.py:659
  123.3 17.3 %collective-permute-start.33 = (bf16[2,192,768]{2,1,0:T(8,128)(2,1)S(1)}, bf16[2,192,768]{2,1,0:T(8,128)(2,1)S(1)}, u32[]{:S(2)}, u32[]{:S(2)}) collective-permute-start(bf16[2,192,768]{2,1,0:T(8,128)(2,1)S(1)} %get-tuple-element.211), channel_id=1, source_target_pairs={{0,8},{4,12},{8,0},{12,4},{16,24},{20,28},{24,16},{28,20},{1,9},{5... | collective-permute-start | bytes 1769480 | tf_op jit(solution)/shard_map/ppermute | solution.py:659
  130.5 17.3 %collective-permute-start.32 = (bf16[2,208,768]{2,1,0:T(8,128)(2,1)S(1)}, bf16[2,208,768]{2,1,0:T(8,128)(2,1)S(1)}, u32[]{:S(2)}, u32[]{:S(2)}) collective-permute-start(bf16[2,208,768]{2,1,0:T(8,128)(2,1)S(1)} %get-tuple-element.210), channel_id=1, source_target_pairs={{0,4},{4,0},{8,12},{12,8},{16,20},{20,16},{24,28},{28,24},{1,5},{5... | collective-permute-start | bytes 1916936 | tf_op jit(solution)/shard_map/ppermute | solution.py:659
  132.1 17.5 %collective-permute-start.31 = (bf16[208,768]{1,0:T(8,128)(2,1)S(1)}, bf16[208,768]{1,0:T(8,128)(2,1)S(1)}, u32[]{:S(2)}, u32[]{:S(2)}) collective-permute-start(bf16[208,768]{1,0:T(8,128)(2,1)S(1)} %fusion.8), channel_id=1, source_target_pairs={{0,8},{4,12},{8,0},{12,4},{16,24},{20,28},{24,16},{28,20},{1,9},{5... | collective-permute-start | bytes 958472 | tf_op jit(solution)/shard_map/ppermute | solution.py:659
  139.0 42.1 %collective-permute-start.30 = (bf16[384,768]{1,0:T(8,128)(2,1)S(1)}, bf16[384,768]{1,0:T(8,128)(2,1)S(1)}, u32[]{:S(2)}, u32[]{:S(2)}) collective-permute-start(bf16[384,768]{1,0:T(8,128)(2,1)S(1)} %fusion.1.refs_8_), channel_id=1, source_target_pairs={{0,2},{1,3},{2,0},{3,1},{4,6},{5,7},{6,4},{7,5},{8,10},{9,11},{10,... | collective-permute-start | bytes 1769480 | tf_op jit(solution)/shard_map/ppermute | solution.py:659
  148.0 13.4 %collective-permute-start.35 = (bf16[208,768]{1,0:T(8,128)(2,1)S(1)}, bf16[208,768]{1,0:T(8,128)(2,1)S(1)}, u32[]{:S(2)}, u32[]{:S(2)}) collective-permute-start(bf16[208,768]{1,0:T(8,128)(2,1)S(1)} %get-tuple-element.258), channel_id=1, source_target_pairs={{0,8},{4,12},{8,0},{12,4},{16,24},{20,28},{24,16},{28,20},{1,9},{5... | collective-permute-start | bytes 958472 | tf_op jit(solution)/shard_map/ppermute | solution.py:659
  149.8 31.2 %collective-permute-start.34 = (bf16[208,768]{1,0:T(8,128)(2,1)S(1)}, bf16[208,768]{1,0:T(8,128)(2,1)S(1)}, u32[]{:S(2)}, u32[]{:S(2)}) collective-permute-start(bf16[208,768]{1,0:T(8,128)(2,1)S(1)} %fusion.2), channel_id=1, source_target_pairs={{0,16},{4,20},{8,24},{12,28},{16,0},{20,4},{24,8},{28,12},{1,17},{... | collective-permute-start | bytes 958472 | tf_op jit(solution)/shard_map/ppermute | solution.py:659
  152.9 34.5 %collective-permute-start.41 = (bf16[192,768]{1,0:T(8,128)(2,1)S(1)}, bf16[192,768]{1,0:T(8,128)(2,1)S(1)}, u32[]{:S(2)}, u32[]{:S(2)}) collective-permute-start(bf16[192,768]{1,0:T(8,128)(2,1)S(1)} %fusion.5), channel_id=1, source_target_pairs={{0,16},{4,20},{8,24},{12,28},{16,0},{20,4},{24,8},{28,12},{1,17},{... | collective-permute-start | bytes 884744 | tf_op jit(solution)/shard_map/ppermute | solution.py:659
  161.3 35.3 %collective-permute-start.45 = (bf16[384,768]{1,0:T(8,128)(2,1)S(1)}, bf16[384,768]{1,0:T(8,128)(2,1)S(1)}, u32[]{:S(2)}, u32[]{:S(2)}) collective-permute-start(bf16[384,768]{1,0:T(8,128)(2,1)S(1)} %get-tuple-element.227.refs_4_), channel_id=1, source_target_pairs={{0,2},{1,3},{2,0},{3,1},{4,6},{5,7},{6,4},{7,5},{8,10},{9,11},{10,... | collective-permute-start | bytes 1769480 | tf_op jit(solution)/shard_map/ppermute | solution.py:659
  163.5 33.1 %collective-permute-start.39 = (bf16[224,768]{1,0:T(8,128)(2,1)S(1)}, bf16[224,768]{1,0:T(8,128)(2,1)S(1)}, u32[]{:S(2)}, u32[]{:S(2)}) collective-permute-start(bf16[224,768]{1,0:T(8,128)(2,1)S(1)} %third.1), channel_id=1, source_target_pairs={{0,16},{4,20},{8,24},{12,28},{16,0},{20,4},{24,8},{28,12},{1,17},{... | collective-permute-start | bytes 1032200 | tf_op jit(solution)/shard_map/ppermute | solution.py:659
  181.1 13.9 %collective-permute-start.40 = (bf16[208,768]{1,0:T(8,128)(2,1)S(1)}, bf16[208,768]{1,0:T(8,128)(2,1)S(1)}, u32[]{:S(2)}, u32[]{:S(2)}) collective-permute-start(bf16[208,768]{1,0:T(8,128)(2,1)S(1)} %add_convert_fusion.3.mine.ck), channel_id=1, source_target_pairs={{0,8},{4,12},{8,0},{12,4},{16,24},{20,28},{24,16},{28,20},{1,9},{5... | collective-permute-start | bytes 958472 | tf_op jit(solution)/shard_map/ppermute | solution.py:659
  181.2 16.2 %collective-permute-start.43 = (bf16[384,768]{1,0:T(8,128)(2,1)S(1)}, bf16[384,768]{1,0:T(8,128)(2,1)S(1)}, u32[]{:S(2)}, u32[]{:S(2)}) collective-permute-start(bf16[384,768]{1,0:T(8,128)(2,1)S(1)} %get-tuple-element.230.refs_0_), channel_id=1, source_target_pairs={{0,2},{1,3},{2,0},{3,1},{4,6},{5,7},{6,4},{7,5},{8,10},{9,11},{10,... | collective-permute-start | bytes 1769480 | tf_op jit(solution)/shard_map/ppermute | solution.py:659
  196.6 12.8 %collective-permute-start.51 = (bf16[384,768]{1,0:T(8,128)(2,1)S(1)}, bf16[384,768]{1,0:T(8,128)(2,1)S(1)}, u32[]{:S(2)}, u32[]{:S(2)}) collective-permute-start(bf16[384,768]{1,0:T(8,128)(2,1)S(1)} %fusion.1.refs_8_), channel_id=1, source_target_pairs={{0,1},{1,0},{2,3},{3,2},{4,5},{5,4},{6,7},{7,6},{8,9},{9,8},{10,11... | collective-permute-start | bytes 1769480 | tf_op jit(solution)/shard_map/ppermute | solution.py:659
  196.7 13.3 %collective-permute-start.49 = (bf16[384,768]{1,0:T(8,128)(2,1)S(1)}, bf16[384,768]{1,0:T(8,128)(2,1)S(1)}, u32[]{:S(2)}, u32[]{:S(2)}) collective-permute-start(bf16[384,768]{1,0:T(8,128)(2,1)S(1)} %get-tuple-element.227.refs_4_), channel_id=1, source_target_pairs={{0,1},{1,0},{2,3},{3,2},{4,5},{5,4},{6,7},{7,6},{8,9},{9,8},{10,11... | collective-permute-start | bytes 1769480 | tf_op jit(solution)/shard_map/ppermute | solution.py:659
  197.2 12.9 %collective-permute-start.47 = (bf16[384,768]{1,0:T(8,128)(2,1)S(1)}, bf16[384,768]{1,0:T(8,128)(2,1)S(1)}, u32[]{:S(2)}, u32[]{:S(2)}) collective-permute-start(bf16[384,768]{1,0:T(8,128)(2,1)S(1)} %get-tuple-element.230.refs_0_), channel_id=1, source_target_pairs={{0,1},{1,0},{2,3},{3,2},{4,5},{5,4},{6,7},{7,6},{8,9},{9,8},{10,11... | collective-permute-start | bytes 1769480 | tf_op jit(solution)/shard_map/ppermute | solution.py:659
  207.9 17.8 %collective-permute-start.54 = (bf16[432,768]{1,0:T(8,128)(2,1)S(1)}, bf16[432,768]{1,0:T(8,128)(2,1)S(1)}, u32[]{:S(2)}, u32[]{:S(2)}) collective-permute-start(bf16[432,768]{1,0:T(8,128)(2,1)S(1)} %last.1.pair), channel_id=1, source_target_pairs={{0,4},{4,0},{8,12},{12,8},{16,20},{20,16},{24,28},{28,24},{1,5},{5... | collective-permute-start | bytes 1990664 | tf_op jit(solution)/shard_map/ppermute | solution.py:659
  210.0 15.7 %collective-permute-start.53 = (bf16[2,192,768]{2,1,0:T(8,128)(2,1)S(1)}, bf16[2,192,768]{2,1,0:T(8,128)(2,1)S(1)}, u32[]{:S(2)}, u32[]{:S(2)}) collective-permute-start(bf16[2,192,768]{2,1,0:T(8,128)(2,1)S(1)} %pair.1), channel_id=1, source_target_pairs={{0,8},{4,12},{8,0},{12,4},{16,24},{20,28},{24,16},{28,20},{1,9},{5... | collective-permute-start | bytes 1769480 | tf_op jit(solution)/shard_map/ppermute | solution.py:659
  (30 other events, 228.9 us)

commit v4 on v3

--- a/solution.py
+++ b/solution.py
@@ -769,7 +769,7 @@
     gpieces = (g0, g1r, gx, hop(gx, 1))
     d_mine, d_give = add(dkeep[0], d_got[0]), add(dkeep[1], d_got[1])
     d_recv = hop(d_give, 2)
-    gffn_2 = hop(after(gffn, d_give, gx), 2)
+    gffn_2 = hop(after(gffn, gx), 2)
     pick = lambda *s: pl.BlockSpec((1,) + s, lambda b, *_: (b,) + (0,) * len(s))
     keep, send, wacc, cacc = call(
         attend_back_kernel,

time: 234 us -> 234 us (level)
  no operation moved by 1% of the time
where the time goes in v4:
time: 234 us; the launch traced here: 230 us
  Pallas kernels  92.1 us (39%)
  waiting for transfers between devices  85.3 us (36%)
  starting transfers between devices  48 us (21%)
    pallas_call x22, Pallas kernels, call(): pl.pallas_call(kernel, out_shape=[pltpu.HBM(*o[:2]) if len(o) > 2 else ja...  92.1 us
    ppermute x55, waiting for transfers between devices, hop(): return lax.ppermute(x, axis, [(i, i ^ mask) for i in range(size)])  85.3 us
    ppermute x55, starting transfers between devices, hop(): return lax.ppermute(x, axis, [(i, i ^ mask) for i in range(size)])  48 us
  transfers between devices with their start and end apart: 55, of which 20 were waited for; matrix products, arithmetic and copies ran while one was open for 1% of the time, Pallas kernels for 38%

profile of v4, /device:TPU:0, one launch (start us, length us, event | category | flops | bytes accessed | tf_op | source)
XLA Modules:
  0.0 229.5 jit_solution(14088902029414130528)
XLA Ops:
  1.8 3.0 %collective-permute-start.7 = (bf16[768,384]{1,0:T(8,128)(2,1)S(1)}, bf16[768,384]{1,0:T(8,128)(2,1)S(1)}, u32[]{:S(2)}, u32[]{:S(2)}) collective-permute-start(bf16[768,384]{1,0:T(8,128)(2,1)S(1)} %constant_dynamic-slice_fusion), channel_id=1, source_target_pairs={{0,2},{1,3},{2,0},{3,1},{4,6},{5,7},{6,4},{7,5},{8,10},{9,11},{10,... | collective-permute-start | bytes 1769480 | tf_op jit(solution)/shard_map/ppermute | solution.py:659
  6.4 10.8 %attend.1 = (bf16[3,192,128]{2,1,0:T(8,128)(2,1)S(1)}, bf16[3,192,128]{2,1,0:T(8,128)(2,1)S(1)}, bf16[2,3,192,128]{3,2,1,0:T(8,128)(2,1)S(1)}, bf16[3,3,512,512]...) custom-call(s32[5]{0:T(128)S(1)} %stack.19.ids.h_ref, ...), custom_call_target="tpu_custom_call" | custom-call | flops 4499999744 | tf_op jit(solution)/shard_map/attend/pallas_call | solution.py:59
  17.2 2.0 collective-permute-start.1
  21.1 5.3 %collective-permute-done.4.s2.refs_8_.refs_14_ = bf16[224,768]{1,0:T(8,128)(2,1)S(1)} collective-permute-done((bf16[224,768]{1,0:T(8,128)(2,1)S(1)}, bf16[224,768]{1,0:T(8,128)(2,1)S(1)}, u32[]{:S(2)}, u32[]{:S(2)}) %collective-permute-start.4) | collective-permute-done | bytes 344096 | tf_op jit(solution)/shard_map/ppermute | solution.py:659
  26.9 5.0 %collective-permute-done.1.xr = bf16[2,3,192,128]{3,2,1,0:T(8,128)(2,1)S(1)} collective-permute-done((bf16[2,3,192,128]{3,2,1,0:T(8,128)(2,1)S(1)}, bf16[2,3,192,128]{3,2,1,0:T(8,128)(2,1)S(1)}, u32[]{:S(2)}, u32[]{:S(2)}) %collective-permute-start.1) | collective-permute-done | bytes 294944 | tf_op jit(solution)/shard_map/ppermute | solution.py:659
  34.0 3.0 %first.1 = (bf16[384,768]{1,0:T(8,128)(2,1)S(1)}, f32[384,768]{1,0:T(8,128)S(1)}, f32[384,128]{1,0:T(8,128)S(1)}, f32[384,768]{1,0:T(8,128)S(1)}, bf16[4,384,192]{2,1,0:T(8,128)(2,1)S(1)}) custom-call(s32[5]{0:T(128)S(1)} %stack.19.ids.h_ref, bf16[3,192,128]{2,1,0:T(8,128)(2,1)S(1)} %get-tuple-element.148.c0, ...), custom_call_target="tpu_custom_call" | custom-call | flops 2000000000 | tf_op jit(solution)/shard_map/first/pallas_call | solution.py:59
  37.5 3.2 %hard_first.1 = (bf16[384,768]{1,0:T(8,128)(2,1)S(1)}, f32[384,768]{1,0:T(8,128)S(1)}) custom-call(s32[5]{0:T(128)S(1)} %stack.19.ids.h_ref, bf16[3,192,128]{2,1,0:T(8,128)(2,1)S(1)} %get-tuple-element.148.c0, bf16[3,192,128]{2,1,0:T(8,128)(2,1)S(1)} %collective-permute-done.c1, bf16[2,3,192,128]{3,2,1,0:T(8,128)(2,1)S(1)} %collective-permute-done.1.xr, ...), custom_call_target="tpu_custom_call" | custom-call | flops 2000000000 | tf_op jit(solution)/shard_map/hard_first/pallas_call | solution.py:59
  40.7 7.1 %collective-permute-done.12.refs_2_.refs_8_ = bf16[384,768]{1,0:T(8,128)(2,1)S(1)} collective-permute-done((bf16[384,768]{1,0:T(8,128)(2,1)S(1)}, bf16[384,768]{1,0:T(8,128)(2,1)S(1)}, u32[]{:S(2)}, u32[]{:S(2)}) %collective-permute-start.12) | collective-permute-done | bytes 589856 | tf_op jit(solution)/shard_map/ppermute | solution.py:659
  49.5 6.5 %inner.1 = (bf16[4,384,768]{2,1,0:T(8,128)(2,1)S(1)}, bf16[4,384,768]{2,1,0:T(8,128)(2,1)S(1)}) custom-call(s32[5]{0:T(128)S(1)} %stack.19.ids.h_ref, bf16[384,768]{1,0:T(8,128)(2,1)S(1)} %get-tuple-element.171.first_low.f0, bf16[768,768]{1,0:T(8,128)(2,1)S(1)} %copy-done.2, bf16[768,768]{1,0:T(8,128)(2,1)S(1)} %collective-permute-done.6.refs_1_, ...), custom_call_target="tpu_custom_call" | custom-call | flops 4000000000 | tf_op jit(solution)/shard_map/inner/pallas_call | solution.py:59
  56.1 5.7 %hard_inner.1.hidden = bf16[4,384,768]{2,1,0:T(8,128)(2,1)S(1)} custom-call(s32[5]{0:T(128)S(1)} %stack.19.ids.h_ref, bf16[384,768]{1,0:T(8,128)(2,1)S(1)} %get-tuple-element.157.first_low, bf16[768,768]{1,0:T(8,128)(2,1)S(1)} %copy-done.2, bf16[768,768]{1,0:T(8,128)(2,1)S(1)} %collective-permute-done.6.refs_1_, ...), custom_call_target="tpu_custom_call" | custom-call | flops 4000000000 | tf_op jit(solution)/shard_map/hard_inner/pallas_call | solution.py:59
  65.0 5.5 %second.1 = (bf16[384,768]{1,0:T(8,128)(2,1)S(1)}, f32[384,768]{1,0:T(8,128)S(1)}, bf16[384,768]{1,0:T(8,128)(2,1)S(1)}, f32[8,768]{1,0:T(8,128)S(1)}) custom-call(s32[5]{0:T(128)S(1)} %stack.19.ids.h_ref, bf16[4,384,768]{2,1,0:T(8,128)(2,1)S(1)} %get-tuple-element.153.hidden, f32[384,768]{1,0:T(8,128)S(1)} %get-tuple-element.154.normed.refs_17_, ...), custom_call_target="tpu_custom_call" | custom-call | flops 3000000000 | tf_op jit(solution)/shard_map/second/pallas_call | solution.py:59
  70.4 9.4 %back.1 = (bf16[3,192,128]{2,1,0:T(8,128)(2,1)S(1)}, bf16[3,192,128]{2,1,0:T(8,128)(2,1)S(1)}, bf16[2,3,192,128]{3,2,1,0:T(8,128)(2,1)S(1)}, bf16[2,208,768]{2,1...) custom-call(s32[5]{0:T(128)S(1)} %stack.19.ids.h_ref, ...), custom_call_target="tpu_custom_call" | custom-call | flops 6499999744 | tf_op jit(solution)/shard_map/back/pallas_call | solution.py:59
  81.9 5.7 %units.1 = (bf16[1536,768]{1,0:T(8,128)(2,1)S(1)}, bf16[1536,768]{1,0:T(8,128)(2,1)S(1)}) custom-call(bf16[384,768]{1,0:T(8,128)(2,1)S(1)} %get-tuple-element.171.first_low.f0, bf16[384,768]{1,0:T(8,128)(2,1)S(1)} %collective-permute-done.18.f1, bf16[384,768]{1,0:T(8,128)(2,1)S(1)} %collective-permute-done.19.fx, ...), custom_call_target="tpu_custom_call" | custom-call | flops 3000000000 | tf_op jit(solution)/shard_map/units/pallas_call | solution.py:59
  92.2 15.5 %attend_back.1 = (bf16[2,384,768]{2,1,0:T(8,128)(2,1)S(1)}, bf16[2,384,768]{2,1,0:T(8,128)(2,1)S(1)}, f32[576,768]{1,0:T(8,128)S(1)}, f32[16,768]{1,0:T(8,128)S(1)}) custom-call(s32[5]{0:T(128)S(1)} %stack.19.ids.h_ref, bf16[3,192,128]{2,1,0:T(8,128)(2,1)S(1)} %get-tuple-element.168.g0, bf16[3,192,128]{2,1,0:T(8,128)(2,1)S(1)} %collective-permute-done.16.g1, ...), custom_call_target="tpu_custom_call" | custom-call | flops 7500000256 | tf_op jit(solution)/shard_map/attend_back/pallas_call | solution.py:59
  107.7 4.3 %collective-permute-done.23.drecv = bf16[208,768]{1,0:T(8,128)(2,1)S(1)} collective-permute-done((bf16[208,768]{1,0:T(8,128)(2,1)S(1)}, bf16[208,768]{1,0:T(8,128)(2,1)S(1)}, u32[]{:S(2)}, u32[]{:S(2)}) %collective-permute-start.23) | collective-permute-done | bytes 319520 | tf_op jit(solution)/shard_map/ppermute | solution.py:659
  116.7 2.6 %near_grad.1 = (f32[768,768]{1,0:T(8,128)S(1)}, bf16[768,768]{1,0:T(8,128)(2,1)S(1)}, f32[2,8,768]{2,1,0:T(8,128)S(1)}) custom-call(bf16[384,768]{1,0:T(8,128)(2,1)S(1)} %get-tuple-element.194.gffn.g0, bf16[384,768]{1,0:T(8,128)(2,1)S(1)} %collective-permute-done.26.g1, bf16[768,768]{1,0:T(8,128)(2,1)S(1)} %copy-done, ...), custom_call_target="tpu_custom_call" | custom-call | flops 2500000000 | tf_op jit(solution)/shard_map/near_grad/pallas_call | solution.py:59
  121.0 2.1 outer_grad.1
  124.7 4.4 %inner_grad.1 = (bf16[2,208,768]{2,1,0:T(8,128)(2,1)S(1)}, bf16[2,208,768]{2,1,0:T(8,128)(2,1)S(1)}) custom-call(s32[5]{0:T(128)S(1)} %stack.19.ids.h_ref, bf16[384,768]{1,0:T(8,128)(2,1)S(1)} %get-tuple-element.171.first_low.f0, bf16[384,768]{1,0:T(8,128)(2,1)S(1)} %collective-permute-done.18.f1, bf16[384,768]{1,0:T(8,128)(2,1)S(1)} %collective-permute-done.19.fx, ...), custom_call_target="tpu_custom_call" | custom-call | flops 2000000000 | tf_op jit(solution)/shard_map/inner_grad/pallas_call | solution.py:59
  133.6 4.9 %hard.1 = (bf16[384,768]{1,0:T(8,128)(2,1)S(1)}, f32[8,128]{1,0:T(8,128)S(1)}) custom-call(s32[5]{0:T(128)S(1)} %stack.19.ids.h_ref, bf16[4,384,768]{2,1,0:T(8,128)(2,1)S(1)} %hard_inner.1.hidden, f32[384,768]{1,0:T(8,128)S(1)} %get-tuple-element.207.normed, bf16[768,768]{1,0:T(8,128)(2,1)S(1)} %copy-done, ...), custom_call_target="tpu_custom_call" | custom-call | flops 50000000 | tf_op jit(solution)/shard_map/hard/pallas_call | solution.py:59
  141.0 6.5 %collective-permute-done.32 = bf16[2,208,768]{2,1,0:T(8,128)(2,1)S(1)} collective-permute-done((bf16[2,208,768]{2,1,0:T(8,128)(2,1)S(1)}, bf16[2,208,768]{2,1,0:T(8,128)(2,1)S(1)}, u32[]{:S(2)}, u32[]{:S(2)}) %collective-permute-start.32) | collective-permute-done | bytes 639008 | tf_op jit(solution)/shard_map/ppermute | solution.py:659
  149.6 2.7 %collective-permute-start.34 = (bf16[208,768]{1,0:T(8,128)(2,1)S(1)}, bf16[208,768]{1,0:T(8,128)(2,1)S(1)}, u32[]{:S(2)}, u32[]{:S(2)}) collective-permute-start(bf16[208,768]{1,0:T(8,128)(2,1)S(1)} %fusion.2), channel_id=1, source_target_pairs={{0,16},{4,20},{8,24},{12,28},{16,0},{20,4},{24,8},{28,12},{1,17},{... | collective-permute-start | bytes 958472 | tf_op jit(solution)/shard_map/ppermute | solution.py:659
  152.7 2.7 %collective-permute-start.41 = (bf16[192,768]{1,0:T(8,128)(2,1)S(1)}, bf16[192,768]{1,0:T(8,128)(2,1)S(1)}, u32[]{:S(2)}, u32[]{:S(2)}) collective-permute-start(bf16[192,768]{1,0:T(8,128)(2,1)S(1)} %fusion.5), channel_id=1, source_target_pairs={{0,16},{4,20},{8,24},{12,28},{16,0},{20,4},{24,8},{28,12},{1,17},{... | collective-permute-start | bytes 884744 | tf_op jit(solution)/shard_map/ppermute | solution.py:659
  156.9 2.1 collective-permute-done.37
  159.0 2.1 collective-permute-done.35.got
  164.0 16.8 %collective-permute-done.34 = bf16[208,768]{1,0:T(8,128)(2,1)S(1)} collective-permute-done((bf16[208,768]{1,0:T(8,128)(2,1)S(1)}, bf16[208,768]{1,0:T(8,128)(2,1)S(1)}, u32[]{:S(2)}, u32[]{:S(2)}) %collective-permute-start.34) | collective-permute-done | bytes 319520 | tf_op jit(solution)/shard_map/ppermute | solution.py:659
  182.5 4.7 %collective-permute-done.41 = bf16[192,768]{1,0:T(8,128)(2,1)S(1)} collective-permute-done((bf16[192,768]{1,0:T(8,128)(2,1)S(1)}, bf16[192,768]{1,0:T(8,128)(2,1)S(1)}, u32[]{:S(2)}, u32[]{:S(2)}) %collective-permute-start.41) | collective-permute-done | bytes 294944 | tf_op jit(solution)/shard_map/ppermute | solution.py:659
  188.9 5.9 %collective-permute-done.40.other.co = bf16[208,768]{1,0:T(8,128)(2,1)S(1)} collective-permute-done((bf16[208,768]{1,0:T(8,128)(2,1)S(1)}, bf16[208,768]{1,0:T(8,128)(2,1)S(1)}, u32[]{:S(2)}, u32[]{:S(2)}) %collective-permute-start.40) | collective-permute-done | bytes 319520 | tf_op jit(solution)/shard_map/ppermute | solution.py:659
  197.3 10.3 %collective-permute-done.42.other = bf16[224,768]{1,0:T(8,128)(2,1)S(1)} collective-permute-done((bf16[224,768]{1,0:T(8,128)(2,1)S(1)}, bf16[224,768]{1,0:T(8,128)(2,1)S(1)}, u32[]{:S(2)}, u32[]{:S(2)}) %collective-permute-start.42) | collective-permute-done | bytes 344096 | tf_op jit(solution)/shard_map/ppermute | solution.py:659
  212.9 3.7 %spread.1 = (bf16[3,512,768]{2,1,0:T(8,128)(2,1)}, bf16[3,512,768]{2,1,0:T(8,128)(2,1)}, bf16[3,512,768]{2,1,0:T(8,128)(2,1)}) custom-call(s32[5]{0:T(128)S(1)} %stack.19.ids.h_ref, bf16[384,768]{1,0:T(8,128)(2,1)S(1)} %get-tuple-element.230.refs_0_, bf16[384,768]{1,0:T(8,128)(2,1)S(1)} %collective-permute-done.47.refs_1_, ...), custom_call_target="tpu_custom_call" | custom-call | flops 50000000 | tf_op jit(solution)/shard_map/spread/pallas_call | solution.py:59
  216.7 2.2 final.1
  218.9 6.6 %collective-permute-done.53.aq = bf16[2,192,768]{2,1,0:T(8,128)(2,1)S(1)} collective-permute-done((bf16[2,192,768]{2,1,0:T(8,128)(2,1)S(1)}, bf16[2,192,768]{2,1,0:T(8,128)(2,1)S(1)}, u32[]{:S(2)}, u32[]{:S(2)}) %collective-permute-start.53) | collective-permute-done | bytes 589856 | tf_op jit(solution)/shard_map/ppermute | solution.py:659
  225.5 3.8 %weights_out.1 = (f32[768,768]{1,0:T(8,128)}, f32[768,768]{1,0:T(8,128)}, f32[768]{0:T(1024)}, f32[768]{0:T(1024)}, f32[1]{0:T(128)}) custom-call(s32[5]{0:T(128)S(1)} %stack.19.ids.h_ref, f32[16,768]{1,0:T(8,128)S(1)} %get-tuple-element.141.consts.refs_8_.refs_23_, bf16[192,768]{1,0:T(8,128)(2,1)S(1)} %add_convert_fusion.10.mine.ak, ...), custom_call_target="tpu_custom_call" | custom-call | flops 50000000 | tf_op jit(solution)/shard_map/weights_out/pallas_call | solution.py:59
  (131 shorter events, 52.0 us)
Async XLA Ops:
  1.8 17.4 %collective-permute-start.7 = (bf16[768,384]{1,0:T(8,128)(2,1)S(1)}, bf16[768,384]{1,0:T(8,128)(2,1)S(1)}, u32[]{:S(2)}, u32[]{:S(2)}) collective-permute-start(bf16[768,384]{1,0:T(8,128)(2,1)S(1)} %constant_dynamic-slice_fusion), channel_id=1, source_target_pairs={{0,2},{1,3},{2,0},{3,1},{4,6},{5,7},{6,4},{7,5},{8,10},{9,11},{10,... | collective-permute-start | bytes 1769480 | tf_op jit(solution)/shard_map/ppermute | solution.py:659
  6.2 20.2 %collective-permute-start.4 = (bf16[224,768]{1,0:T(8,128)(2,1)S(1)}, bf16[224,768]{1,0:T(8,128)(2,1)S(1)}, u32[]{:S(2)}, u32[]{:S(2)}) collective-permute-start(bf16[224,768]{1,0:T(8,128)(2,1)S(1)} %get-tuple-element.145.s0.refs_6_.refs_12_), channel_id=1, source_target_pairs={{0,2},{1,3},{2,0},{3,1},{4,6},{5,7},{6,4},{7,5},{8,10},{9,11},{10,... | collective-permute-start | bytes 1032200 | tf_op jit(solution)/shard_map/ppermute | solution.py:659
  17.2 14.6 %collective-permute-start.1 = (bf16[2,3,192,128]{3,2,1,0:T(8,128)(2,1)S(1)}, bf16[2,3,192,128]{3,2,1,0:T(8,128)(2,1)S(1)}, u32[]{:S(2)}, u32[]{:S(2)}) collective-permute-start(bf16[2,3,192,128]{3,2,1,0:T(8,128)(2,1)S(1)} %get-tuple-element.144), channel_id=1, source_target_pairs={{0,2},{1,3},{2,0},{3,1},{4,6},{5,7},{6,4},{7,5},{8,10},{9,11},{10,... | collective-permute-start | bytes 884744 | tf_op jit(solution)/shard_map/ppermute | solution.py:659
  19.3 17.7 %collective-permute-start.8 = (bf16[768,384]{1,0:T(8,128)(2,1)S(1)}, bf16[768,384]{1,0:T(8,128)(2,1)S(1)}, u32[]{:S(2)}, u32[]{:S(2)}) collective-permute-start(bf16[768,384]{1,0:T(8,128)(2,1)S(1)} %collective-permute-done.7.refs_2_), channel_id=1, source_target_pairs={{0,4},{4,0},{8,12},{12,8},{16,20},{20,16},{24,28},{28,24},{1,5},{5... | collective-permute-start | bytes 1769480 | tf_op jit(solution)/shard_map/ppermute | solution.py:659
  21.1 28.4 %collective-permute-start.6 = (bf16[768,768]{1,0:T(8,128)(2,1)S(1)}, bf16[768,768]{1,0:T(8,128)(2,1)S(1)}, u32[]{:S(2)}, u32[]{:S(2)}) collective-permute-start(bf16[768,768]{1,0:T(8,128)(2,1)S(1)} %copy-done.2), channel_id=1, source_target_pairs={{0,1},{1,0},{2,3},{3,2},{4,5},{5,4},{6,7},{7,6},{8,9},{9,8},{10,11... | collective-permute-start | bytes 3538952 | tf_op jit(solution)/shard_map/ppermute | solution.py:659
  32.0 15.8 %collective-permute-start.12 = (bf16[384,768]{1,0:T(8,128)(2,1)S(1)}, bf16[384,768]{1,0:T(8,128)(2,1)S(1)}, u32[]{:S(2)}, u32[]{:S(2)}) collective-permute-start(bf16[384,768]{1,0:T(8,128)(2,1)S(1)} %get-tuple-element.262), channel_id=1, source_target_pairs={{0,2},{1,3},{2,0},{3,1},{4,6},{5,7},{6,4},{7,5},{8,10},{9,11},{10,... | collective-permute-start | bytes 1769480 | tf_op jit(solution)/shard_map/ppermute | solution.py:659
  33.8 15.7 %collective-permute-start.9 = (bf16[768,384]{1,0:T(8,128)(2,1)S(1)}, bf16[768,384]{1,0:T(8,128)(2,1)S(1)}, u32[]{:S(2)}, u32[]{:S(2)}) collective-permute-start(bf16[768,384]{1,0:T(8,128)(2,1)S(1)} %collective-permute-done.7.refs_2_), channel_id=1, source_target_pairs={{0,1},{1,0},{2,3},{3,2},{4,5},{5,4},{6,7},{7,6},{8,9},{9,8},{10,11... | collective-permute-start | bytes 1769480 | tf_op jit(solution)/shard_map/ppermute | solution.py:659
  37.3 27.7 %collective-permute-start.11 = (bf16[768,768]{1,0:T(8,128)(2,1)S(1)}, bf16[768,768]{1,0:T(8,128)(2,1)S(1)}, u32[]{:S(2)}, u32[]{:S(2)}) collective-permute-start(bf16[768,768]{1,0:T(8,128)(2,1)S(1)} %copy-done), channel_id=1, source_target_pairs={{0,1},{1,0},{2,3},{3,2},{4,5},{5,4},{6,7},{7,6},{8,9},{9,8},{10,11... | collective-permute-start | bytes 3538952 | tf_op jit(solution)/shard_map/ppermute | solution.py:659
  47.8 15.0 %collective-permute-start.13 = (bf16[384,768]{1,0:T(8,128)(2,1)S(1)}, bf16[384,768]{1,0:T(8,128)(2,1)S(1)}, u32[]{:S(2)}, u32[]{:S(2)}) collective-permute-start(bf16[384,768]{1,0:T(8,128)(2,1)S(1)} %get-tuple-element.261), channel_id=1, source_target_pairs={{0,2},{1,3},{2,0},{3,1},{4,6},{5,7},{6,4},{7,5},{8,10},{9,11},{10,... | collective-permute-start | bytes 1769480 | tf_op jit(solution)/shard_map/ppermute | solution.py:659
  49.5 15.5 %collective-permute-start.14 = (bf16[384,768]{1,0:T(8,128)(2,1)S(1)}, bf16[384,768]{1,0:T(8,128)(2,1)S(1)}, u32[]{:S(2)}, u32[]{:S(2)}) collective-permute-start(bf16[384,768]{1,0:T(8,128)(2,1)S(1)} %collective-permute-done.12.refs_2_.refs_8_), channel_id=1, source_target_pairs={{0,1},{1,0},{2,3},{3,2},{4,5},{5,4},{6,7},{7,6},{8,9},{9,8},{10,11... | collective-permute-start | bytes 1769480 | tf_op jit(solution)/shard_map/ppermute | solution.py:659
  62.7 19.2 %collective-permute-start.18 = (bf16[384,768]{1,0:T(8,128)(2,1)S(1)}, bf16[384,768]{1,0:T(8,128)(2,1)S(1)}, u32[]{:S(2)}, u32[]{:S(2)}) collective-permute-start(bf16[384,768]{1,0:T(8,128)(2,1)S(1)} %get-tuple-element.171.first_low.f0), channel_id=1, source_target_pairs={{0,1},{1,0},{2,3},{3,2},{4,5},{5,4},{6,7},{7,6},{8,9},{9,8},{10,11... | collective-permute-start | bytes 1769480 | tf_op jit(solution)/shard_map/ppermute | solution.py:659
  63.2 16.6 %collective-permute-start.19 = (bf16[384,768]{1,0:T(8,128)(2,1)S(1)}, bf16[384,768]{1,0:T(8,128)(2,1)S(1)}, u32[]{:S(2)}, u32[]{:S(2)}) collective-permute-start(bf16[384,768]{1,0:T(8,128)(2,1)S(1)} %get-tuple-element.171.first_low.f0), channel_id=1, source_target_pairs={{0,2},{1,3},{2,0},{3,1},{4,6},{5,7},{6,4},{7,5},{8,10},{9,11},{10,... | collective-permute-start | bytes 1769480 | tf_op jit(solution)/shard_map/ppermute | solution.py:659
  89.9 17.8 %collective-permute-start.24 = (bf16[384,768]{1,0:T(8,128)(2,1)S(1)}, bf16[384,768]{1,0:T(8,128)(2,1)S(1)}, u32[]{:S(2)}, u32[]{:S(2)}) collective-permute-start(bf16[384,768]{1,0:T(8,128)(2,1)S(1)} %get-tuple-element.194.gffn.g0), channel_id=1, source_target_pairs={{0,2},{1,3},{2,0},{3,1},{4,6},{5,7},{6,4},{7,5},{8,10},{9,11},{10,... | collective-permute-start | bytes 1769480 | tf_op jit(solution)/shard_map/ppermute | solution.py:659
  91.6 20.4 %collective-permute-start.23 = (bf16[208,768]{1,0:T(8,128)(2,1)S(1)}, bf16[208,768]{1,0:T(8,128)(2,1)S(1)}, u32[]{:S(2)}, u32[]{:S(2)}) collective-permute-start(bf16[208,768]{1,0:T(8,128)(2,1)S(1)} %get-tuple-element.259), channel_id=1, source_target_pairs={{0,2},{1,3},{2,0},{3,1},{4,6},{5,7},{6,4},{7,5},{8,10},{9,11},{10,... | collective-permute-start | bytes 958472 | tf_op jit(solution)/shard_map/ppermute | solution.py:659
  113.6 16.7 %collective-permute-start.28 = (bf16[2,208,768]{2,1,0:T(8,128)(2,1)S(1)}, bf16[2,208,768]{2,1,0:T(8,128)(2,1)S(1)}, u32[]{:S(2)}, u32[]{:S(2)}) collective-permute-start(bf16[2,208,768]{2,1,0:T(8,128)(2,1)S(1)} %get-tuple-element.198), channel_id=1, source_target_pairs={{0,4},{4,0},{8,12},{12,8},{16,20},{20,16},{24,28},{28,24},{1,5},{5... | collective-permute-start | bytes 1916936 | tf_op jit(solution)/shard_map/ppermute | solution.py:659
  119.4 19.1 %collective-permute-start.27 = (bf16[384,768]{1,0:T(8,128)(2,1)S(1)}, bf16[384,768]{1,0:T(8,128)(2,1)S(1)}, u32[]{:S(2)}, u32[]{:S(2)}) collective-permute-start(bf16[384,768]{1,0:T(8,128)(2,1)S(1)} %fusion.4), channel_id=1, source_target_pairs={{0,2},{1,3},{2,0},{3,1},{4,6},{5,7},{6,4},{7,5},{8,10},{9,11},{10,... | collective-permute-start | bytes 1769480 | tf_op jit(solution)/shard_map/ppermute | solution.py:659
  123.1 17.3 %collective-permute-start.33 = (bf16[2,192,768]{2,1,0:T(8,128)(2,1)S(1)}, bf16[2,192,768]{2,1,0:T(8,128)(2,1)S(1)}, u32[]{:S(2)}, u32[]{:S(2)}) collective-permute-start(bf16[2,192,768]{2,1,0:T(8,128)(2,1)S(1)} %get-tuple-element.211), channel_id=1, source_target_pairs={{0,8},{4,12},{8,0},{12,4},{16,24},{20,28},{24,16},{28,20},{1,9},{5... | collective-permute-start | bytes 1769480 | tf_op jit(solution)/shard_map/ppermute | solution.py:659
  130.3 17.3 %collective-permute-start.32 = (bf16[2,208,768]{2,1,0:T(8,128)(2,1)S(1)}, bf16[2,208,768]{2,1,0:T(8,128)(2,1)S(1)}, u32[]{:S(2)}, u32[]{:S(2)}) collective-permute-start(bf16[2,208,768]{2,1,0:T(8,128)(2,1)S(1)} %get-tuple-element.210), channel_id=1, source_target_pairs={{0,4},{4,0},{8,12},{12,8},{16,20},{20,16},{24,28},{28,24},{1,5},{5... | collective-permute-start | bytes 1916936 | tf_op jit(solution)/shard_map/ppermute | solution.py:659
  131.9 17.5 %collective-permute-start.31 = (bf16[208,768]{1,0:T(8,128)(2,1)S(1)}, bf16[208,768]{1,0:T(8,128)(2,1)S(1)}, u32[]{:S(2)}, u32[]{:S(2)}) collective-permute-start(bf16[208,768]{1,0:T(8,128)(2,1)S(1)} %fusion.8), channel_id=1, source_target_pairs={{0,8},{4,12},{8,0},{12,4},{16,24},{20,28},{24,16},{28,20},{1,9},{5... | collective-permute-start | bytes 958472 | tf_op jit(solution)/shard_map/ppermute | solution.py:659
  138.8 42.1 %collective-permute-start.30 = (bf16[384,768]{1,0:T(8,128)(2,1)S(1)}, bf16[384,768]{1,0:T(8,128)(2,1)S(1)}, u32[]{:S(2)}, u32[]{:S(2)}) collective-permute-start(bf16[384,768]{1,0:T(8,128)(2,1)S(1)} %fusion.1.refs_8_), channel_id=1, source_target_pairs={{0,2},{1,3},{2,0},{3,1},{4,6},{5,7},{6,4},{7,5},{8,10},{9,11},{10,... | collective-permute-start | bytes 1769480 | tf_op jit(solution)/shard_map/ppermute | solution.py:659
  147.8 13.4 %collective-permute-start.35 = (bf16[208,768]{1,0:T(8,128)(2,1)S(1)}, bf16[208,768]{1,0:T(8,128)(2,1)S(1)}, u32[]{:S(2)}, u32[]{:S(2)}) collective-permute-start(bf16[208,768]{1,0:T(8,128)(2,1)S(1)} %get-tuple-element.258), channel_id=1, source_target_pairs={{0,8},{4,12},{8,0},{12,4},{16,24},{20,28},{24,16},{28,20},{1,9},{5... | collective-permute-start | bytes 958472 | tf_op jit(solution)/shard_map/ppermute | solution.py:659
  149.6 31.2 %collective-permute-start.34 = (bf16[208,768]{1,0:T(8,128)(2,1)S(1)}, bf16[208,768]{1,0:T(8,128)(2,1)S(1)}, u32[]{:S(2)}, u32[]{:S(2)}) collective-permute-start(bf16[208,768]{1,0:T(8,128)(2,1)S(1)} %fusion.2), channel_id=1, source_target_pairs={{0,16},{4,20},{8,24},{12,28},{16,0},{20,4},{24,8},{28,12},{1,17},{... | collective-permute-start | bytes 958472 | tf_op jit(solution)/shard_map/ppermute | solution.py:659
  152.7 34.5 %collective-permute-start.41 = (bf16[192,768]{1,0:T(8,128)(2,1)S(1)}, bf16[192,768]{1,0:T(8,128)(2,1)S(1)}, u32[]{:S(2)}, u32[]{:S(2)}) collective-permute-start(bf16[192,768]{1,0:T(8,128)(2,1)S(1)} %fusion.5), channel_id=1, source_target_pairs={{0,16},{4,20},{8,24},{12,28},{16,0},{20,4},{24,8},{28,12},{1,17},{... | collective-permute-start | bytes 884744 | tf_op jit(solution)/shard_map/ppermute | solution.py:659
  161.1 35.3 %collective-permute-start.45 = (bf16[384,768]{1,0:T(8,128)(2,1)S(1)}, bf16[384,768]{1,0:T(8,128)(2,1)S(1)}, u32[]{:S(2)}, u32[]{:S(2)}) collective-permute-start(bf16[384,768]{1,0:T(8,128)(2,1)S(1)} %get-tuple-element.227.refs_4_), channel_id=1, source_target_pairs={{0,2},{1,3},{2,0},{3,1},{4,6},{5,7},{6,4},{7,5},{8,10},{9,11},{10,... | collective-permute-start | bytes 1769480 | tf_op jit(solution)/shard_map/ppermute | solution.py:659
  163.3 33.1 %collective-permute-start.39 = (bf16[224,768]{1,0:T(8,128)(2,1)S(1)}, bf16[224,768]{1,0:T(8,128)(2,1)S(1)}, u32[]{:S(2)}, u32[]{:S(2)}) collective-permute-start(bf16[224,768]{1,0:T(8,128)(2,1)S(1)} %third.1), channel_id=1, source_target_pairs={{0,16},{4,20},{8,24},{12,28},{16,0},{20,4},{24,8},{28,12},{1,17},{... | collective-permute-start | bytes 1032200 | tf_op jit(solution)/shard_map/ppermute | solution.py:659
  180.9 13.9 %collective-permute-start.40 = (bf16[208,768]{1,0:T(8,128)(2,1)S(1)}, bf16[208,768]{1,0:T(8,128)(2,1)S(1)}, u32[]{:S(2)}, u32[]{:S(2)}) collective-permute-start(bf16[208,768]{1,0:T(8,128)(2,1)S(1)} %add_convert_fusion.3.mine.ck), channel_id=1, source_target_pairs={{0,8},{4,12},{8,0},{12,4},{16,24},{20,28},{24,16},{28,20},{1,9},{5... | collective-permute-start | bytes 958472 | tf_op jit(solution)/shard_map/ppermute | solution.py:659
  181.0 16.2 %collective-permute-start.43 = (bf16[384,768]{1,0:T(8,128)(2,1)S(1)}, bf16[384,768]{1,0:T(8,128)(2,1)S(1)}, u32[]{:S(2)}, u32[]{:S(2)}) collective-permute-start(bf16[384,768]{1,0:T(8,128)(2,1)S(1)} %get-tuple-element.230.refs_0_), channel_id=1, source_target_pairs={{0,2},{1,3},{2,0},{3,1},{4,6},{5,7},{6,4},{7,5},{8,10},{9,11},{10,... | collective-permute-start | bytes 1769480 | tf_op jit(solution)/shard_map/ppermute | solution.py:659
  196.4 12.8 %collective-permute-start.51 = (bf16[384,768]{1,0:T(8,128)(2,1)S(1)}, bf16[384,768]{1,0:T(8,128)(2,1)S(1)}, u32[]{:S(2)}, u32[]{:S(2)}) collective-permute-start(bf16[384,768]{1,0:T(8,128)(2,1)S(1)} %fusion.1.refs_8_), channel_id=1, source_target_pairs={{0,1},{1,0},{2,3},{3,2},{4,5},{5,4},{6,7},{7,6},{8,9},{9,8},{10,11... | collective-permute-start | bytes 1769480 | tf_op jit(solution)/shard_map/ppermute | solution.py:659
  196.5 13.3 %collective-permute-start.49 = (bf16[384,768]{1,0:T(8,128)(2,1)S(1)}, bf16[384,768]{1,0:T(8,128)(2,1)S(1)}, u32[]{:S(2)}, u32[]{:S(2)}) collective-permute-start(bf16[384,768]{1,0:T(8,128)(2,1)S(1)} %get-tuple-element.227.refs_4_), channel_id=1, source_target_pairs={{0,1},{1,0},{2,3},{3,2},{4,5},{5,4},{6,7},{7,6},{8,9},{9,8},{10,11... | collective-permute-start | bytes 1769480 | tf_op jit(solution)/shard_map/ppermute | solution.py:659
  197.0 12.9 %collective-permute-start.47 = (bf16[384,768]{1,0:T(8,128)(2,1)S(1)}, bf16[384,768]{1,0:T(8,128)(2,1)S(1)}, u32[]{:S(2)}, u32[]{:S(2)}) collective-permute-start(bf16[384,768]{1,0:T(8,128)(2,1)S(1)} %get-tuple-element.230.refs_0_), channel_id=1, source_target_pairs={{0,1},{1,0},{2,3},{3,2},{4,5},{5,4},{6,7},{7,6},{8,9},{9,8},{10,11... | collective-permute-start | bytes 1769480 | tf_op jit(solution)/shard_map/ppermute | solution.py:659
  207.7 17.8 %collective-permute-start.54 = (bf16[432,768]{1,0:T(8,128)(2,1)S(1)}, bf16[432,768]{1,0:T(8,128)(2,1)S(1)}, u32[]{:S(2)}, u32[]{:S(2)}) collective-permute-start(bf16[432,768]{1,0:T(8,128)(2,1)S(1)} %last.1.pair), channel_id=1, source_target_pairs={{0,4},{4,0},{8,12},{12,8},{16,20},{20,16},{24,28},{28,24},{1,5},{5... | collective-permute-start | bytes 1990664 | tf_op jit(solution)/shard_map/ppermute | solution.py:659
  209.8 15.7 %collective-permute-start.53 = (bf16[2,192,768]{2,1,0:T(8,128)(2,1)S(1)}, bf16[2,192,768]{2,1,0:T(8,128)(2,1)S(1)}, u32[]{:S(2)}, u32[]{:S(2)}) collective-permute-start(bf16[2,192,768]{2,1,0:T(8,128)(2,1)S(1)} %pair.1), channel_id=1, source_target_pairs={{0,8},{4,12},{8,0},{12,4},{16,24},{20,28},{24,16},{28,20},{1,9},{5... | collective-permute-start | bytes 1769480 | tf_op jit(solution)/shard_map/ppermute | solution.py:659
  (30 other events, 230.4 us)
